TPU v7x, 32 devices: a whole 2x2x4 slice. The times are simulated.
32 devices in a mesh: fsdp: 8 (over z, core), dp: 4 (over y, x).
Axes of the slice: x: 2, y: 2, z: 4, core: 2. Of those that a mesh axis runs over, the one named last changes fastest.
Arguments:
- tokens: bfloat16 [8192, 1536], P(('fsdp', 'dp')), may hold values from -6 to 6
- w_query: bfloat16 [1536, 1536], P('fsdp'), may hold values from -0.15625 to 0.15625
- key_weight: bfloat16 [1536, 512], P('fsdp'), may hold values from -0.15625 to 0.15625
- value_weight: bfloat16 [1536, 512], P('fsdp'), may hold values from -0.15625 to 0.15625
- w_out: bfloat16 [1536, 1536], P('fsdp'), may hold values from -1.25 to 1.25
- gain_attn: bfloat16 [1536], P('fsdp'), may hold values from 0.099609375 to 1.8984375
- gain_ffn: bfloat16 [1536], P('fsdp'), may hold values from 0.099609375 to 1.8984375
- w_router: bfloat16 [1536, 16], P('fsdp'), may hold values from -0.078125 to 0.078125
- w_gate: bfloat16 [16, 1536, 512], P('fsdp'), may hold values from -0.15625 to 0.15625
- w_up: bfloat16 [16, 1536, 512], P('fsdp'), may hold values from -0.15625 to 0.15625
- w_down: bfloat16 [16, 512, 1536], P('fsdp'), may hold values from -0.75 to 0.75
- routes: int32 [8192, 8], P(('fsdp', 'dp')), may hold values from 0 to 15, all different within a row; in each aligned block of 256 rows (0 to 255, 256 to 511, ...) at most 144 rows name the same one
- cotangent: bfloat16 [8192, 1536], P(('fsdp', 'dp')), may hold values from -6 to 6
Outputs:
- output: bfloat16 [8192, 1536], P(('fsdp', 'dp'))
- grad_tokens: bfloat16 [8192, 1536], P(('fsdp', 'dp'))
- grad_w_query: float32 [1536, 1536], P('fsdp')
- grad_w_key: float32 [1536, 512], P('fsdp')
- grad_w_value: float32 [1536, 512], P('fsdp')
- grad_w_out: float32 [1536, 1536], P('fsdp')
- grad_gain_attn: float32 [1536], P('fsdp')
- grad_gain_ffn: float32 [1536], P('fsdp')
- grad_w_router: float32 [1536, 16], P('fsdp')
- grad_w_gate: float32 [16, 1536, 512], P('fsdp')
- grad_w_up: float32 [16, 1536, 512], P('fsdp')
- grad_w_down: float32 [16, 512, 1536], P('fsdp')
Inputs may be any that keep to these rules, and one draw needn't show every extreme that they name: `routes`: each row names 8 different experts. In each aligned block of 256 rows (the tokens of one sequence) no expert is named by more than 144 rows, and in some such blocks one expert is named by exactly 144 rows.
All inputs are finite; a program needn't handle non-finite values.
Results may differ from a plain program's by a relative error of at most 0.022.
Values may be sent and summed in bfloat16 or wider, within the bound.
A program may use at most 256 MiB of HBM per device.

v0:
```python
import jax
import jax.numpy as jnp
from jax import lax
from jax.sharding import PartitionSpec as P

MODEL_WIDTH = 1536
QUERY_HEADS = 24
KEY_VALUE_HEADS = 8
HEAD_SIZE = 64
TOP = 8


EPSILON = 1e-06
ROPE_BASE = 10000.0
MASKED = -1e30


def rope_tables(sequence_length):
    half_size = HEAD_SIZE // 2
    positions = jnp.arange(sequence_length, dtype=jnp.float32)
    frequency = ROPE_BASE ** (-2.0 * jnp.arange(half_size, dtype=jnp.float32) / HEAD_SIZE)
    angles = positions[:, None] * frequency[None, :]
    return (jnp.cos(angles)[:, None, :], jnp.sin(angles)[:, None, :])


def apply_rotary(values, cosine_table, sine_table):
    half_size = values.shape[-1] // 2
    first_half = values[..., :half_size]
    second_half = values[..., half_size:]
    return jnp.concatenate(
        [
            first_half * cosine_table - second_half * sine_table,
            first_half * sine_table + second_half * cosine_table,
        ],
        -1,
    )


def rotary_backward(grads, cosine_table, sine_table):
    half_size = grads.shape[-1] // 2
    first_half = grads[..., :half_size]
    second_half = grads[..., half_size:]
    return jnp.concatenate(
        [
            first_half * cosine_table + second_half * sine_table,
            second_half * cosine_table - first_half * sine_table,
        ],
        -1,
    )


def rms_scale(values):
    return lax.rsqrt(jnp.mean(values * values, -1, keepdims=True) + EPSILON)


def norm_back(grad_normed, normed, inv_rms, gain_vec):
    scaled = grad_normed * gain_vec
    grad_input = inv_rms * (scaled - normed * jnp.mean(scaled * normed, -1, keepdims=True))
    return (grad_input, jnp.sum(grad_normed * normed, 0))


def causal_keep(start_row, block_rows, sequence_length):
    query_pos = start_row + jnp.arange(block_rows, dtype=jnp.int32)
    key_pos = jnp.arange(sequence_length, dtype=jnp.int32)
    return key_pos[None, :] <= query_pos[:, None]


def block_scores(query_block, key_rot, start_row, sequence_length):
    factor = HEAD_SIZE ** (-0.5)
    scores = (
        jnp.einsum("qgrd,kgd->grqk", query_block, key_rot, preferred_element_type=jnp.float32)
        * factor
    )
    return jnp.where(causal_keep(start_row, query_block.shape[0], sequence_length), scores, MASKED)


def attention_forward(query_rotated, key_rot, value_per_head):
    sequence_length = query_rotated.shape[0]
    block_rows = min(512, sequence_length)

    def attend_block(block_index):
        start_row = block_index * block_rows
        scores = block_scores(query_rotated, key_rot, start_row, sequence_length)
        row_max = jnp.max(scores, -1, keepdims=True)
        exp_scores = jnp.exp(scores - row_max)
        row_total = jnp.sum(exp_scores, -1, keepdims=True)
        probs_low = (exp_scores / row_total).astype(jnp.bfloat16)
        mixed_block = jnp.einsum(
            "grqk,kgd->qgrd", probs_low, value_per_head, preferred_element_type=jnp.float32
        )
        return (mixed_block, (row_max + jnp.log(row_total))[..., 0])

    mixed, log_total = lax.map(
        attend_block, jnp.arange(sequence_length // block_rows, dtype=jnp.int32)
    )
    return (mixed.reshape(sequence_length, QUERY_HEADS * HEAD_SIZE), log_total)


def attention_backward(query_rotated, key_rot, value_per_head, log_total, grad_attention_mixed):
    sequence_length = query_rotated.shape[0]
    block_rows = min(512, sequence_length)
    factor = HEAD_SIZE ** (-0.5)

    def back_block(carry, block_index):
        grad_key, grad_value = carry
        start_row = block_index * block_rows
        scores = block_scores(query_rotated, key_rot, start_row, sequence_length)
        attn_probs = jnp.exp(scores - log_total[block_index][..., None])
        grad_probs = jnp.einsum(
            "qgrd,kgd->grqk",
            grad_attention_mixed,
            value_per_head,
            preferred_element_type=jnp.float32,
        )
        row_dot = jnp.sum(attn_probs * grad_probs, -1, keepdims=True)
        grad_scores = (attn_probs * (grad_probs - row_dot)).astype(jnp.bfloat16)
        grad_query = (
            jnp.einsum("grqk,kgd->qgrd", grad_scores, key_rot, preferred_element_type=jnp.float32)
            * factor
        )
        grad_key = (
            grad_key
            + jnp.einsum(
                "grqk,qgrd->kgd", grad_scores, query_rotated, preferred_element_type=jnp.float32
            )
            * factor
        )
        grad_value = grad_value + jnp.einsum(
            "grqk,qgrd->kgd",
            attn_probs.astype(jnp.bfloat16),
            grad_attention_mixed,
            preferred_element_type=jnp.float32,
        )
        return ((grad_key, grad_value), grad_query)

    zero_kv = jnp.zeros(key_rot.shape, jnp.float32)
    (grad_key, grad_value), grad_query = lax.scan(
        back_block, (zero_kv, zero_kv), jnp.arange(sequence_length // block_rows, dtype=jnp.int32)
    )
    return (grad_query.reshape(sequence_length, QUERY_HEADS, HEAD_SIZE), grad_key, grad_value)


def ffn_forward(inputs, gate_w, up_w, down_w):
    gate_val = jnp.einsum("necd,edf->necf", inputs, gate_w, preferred_element_type=jnp.float32)
    up_val = jnp.einsum("necd,edf->necf", inputs, up_w, preferred_element_type=jnp.float32)
    expert_hid = (jax.nn.silu(gate_val) * up_val).astype(jnp.bfloat16)
    return jnp.einsum(
        "necf,efd->necd", expert_hid, down_w, preferred_element_type=jnp.float32
    ).astype(jnp.bfloat16)


def ffn_back(inputs, grads, gate_w, up_w, down_w):
    gate_val = jnp.einsum("necd,edf->necf", inputs, gate_w, preferred_element_type=jnp.float32)
    up_val = jnp.einsum("necd,edf->necf", inputs, up_w, preferred_element_type=jnp.float32)
    sigmoid_gate = jax.nn.sigmoid(gate_val)
    activated = gate_val * sigmoid_gate
    expert_hid = (activated * up_val).astype(jnp.bfloat16)
    grad_hid = jnp.einsum("necd,efd->necf", grads, down_w, preferred_element_type=jnp.float32)
    grad_up = (grad_hid * activated).astype(jnp.bfloat16)
    grad_gate = (grad_hid * up_val * sigmoid_gate * (1.0 + gate_val * (1.0 - sigmoid_gate))).astype(
        jnp.bfloat16
    )
    grad_input = jnp.einsum("necf,edf->necd", grad_gate, gate_w, preferred_element_type=jnp.float32)
    grad_input = grad_input + jnp.einsum(
        "necf,edf->necd", grad_up, up_w, preferred_element_type=jnp.float32
    )
    return (grad_input.astype(jnp.bfloat16), grad_gate, grad_up, expert_hid)


def weight_terms(inputs, grads, grad_gate, grad_up, expert_hid):
    term_gate = jnp.einsum("necd,necf->edf", inputs, grad_gate, preferred_element_type=jnp.float32)
    term_up = jnp.einsum("necd,necf->edf", inputs, grad_up, preferred_element_type=jnp.float32)
    term_down = jnp.einsum("necd,necf->edf", grads, expert_hid, preferred_element_type=jnp.float32)
    return jnp.stack([term_gate, term_up, term_down], 1)


def body(
    tokens,
    w_query,
    key_weight,
    value_weight,
    w_out,
    gain_attn,
    gain_ffn,
    w_router,
    w_gate,
    w_up,
    w_down,
    routes,
    cotangent,
):
    sequence_length = tokens.shape[0]
    local_experts = w_gate.shape[0]
    experts_all = local_experts * lax.axis_size("fsdp")
    capacity = 9 * sequence_length * TOP // (8 * experts_all)
    query_full, key_full, value_full, out_full, gain_one, gain_two, router_full = (
        lax.all_gather(w_query, "fsdp", axis=0, tiled=True),
        lax.all_gather(key_weight, "fsdp", axis=0, tiled=True),
        lax.all_gather(value_weight, "fsdp", axis=0, tiled=True),
        lax.all_gather(w_out, "fsdp", axis=0, tiled=True),
        lax.all_gather(gain_attn, "fsdp", axis=0, tiled=True),
        lax.all_gather(gain_ffn, "fsdp", axis=0, tiled=True),
        lax.all_gather(w_router, "fsdp", axis=0, tiled=True),
    )
    tokens_f = tokens.astype(jnp.float32)
    inv_one = rms_scale(tokens_f)
    normed_one = tokens_f * inv_one
    attention_input = (normed_one * gain_one.astype(jnp.float32)).astype(jnp.bfloat16)
    query_projected = jnp.dot(
        attention_input, query_full, preferred_element_type=jnp.float32
    ).reshape(sequence_length, QUERY_HEADS, HEAD_SIZE)
    key_projected = jnp.dot(attention_input, key_full, preferred_element_type=jnp.float32).reshape(
        sequence_length, KEY_VALUE_HEADS, HEAD_SIZE
    )
    value_per_head = (
        jnp.dot(attention_input, value_full, preferred_element_type=jnp.float32)
        .astype(jnp.bfloat16)
        .reshape(sequence_length, KEY_VALUE_HEADS, HEAD_SIZE)
    )
    cosine_table, sine_table = rope_tables(sequence_length)
    query_rotated = (
        apply_rotary(query_projected, cosine_table, sine_table)
        .astype(jnp.bfloat16)
        .reshape(sequence_length, KEY_VALUE_HEADS, QUERY_HEADS // KEY_VALUE_HEADS, HEAD_SIZE)
    )
    key_rot = apply_rotary(key_projected, cosine_table, sine_table).astype(jnp.bfloat16)
    mixed_f, log_total = attention_forward(query_rotated, key_rot, value_per_head)
    attn_mixed = mixed_f.astype(jnp.bfloat16)
    hidden = tokens_f + jnp.dot(attn_mixed, out_full, preferred_element_type=jnp.float32)
    inv_two = rms_scale(hidden)
    normed_two = hidden * inv_two
    ffn_in = (normed_two * gain_two.astype(jnp.float32)).astype(jnp.bfloat16)
    logits = jnp.dot(ffn_in, router_full, preferred_element_type=jnp.float32)
    chosen = jnp.take_along_axis(logits, routes, 1)
    gate_probs = jax.nn.softmax(chosen, axis=-1)
    onehot = (routes[:, :, None] == jnp.arange(experts_all, dtype=jnp.int32)[None, None, :]).astype(
        jnp.float32
    )
    counts = jnp.sum(onehot, 1)
    row_ids = jnp.arange(sequence_length, dtype=jnp.int32)
    lower_tri = (row_ids[None, :] < row_ids[:, None]).astype(jnp.float32)
    before = jnp.dot(lower_tri, counts, precision=lax.Precision.HIGHEST)
    slot_ids = jnp.take_along_axis(before, routes, 1).astype(jnp.int32)
    target_rows = routes * capacity + slot_ids
    expert_in = (
        jnp.zeros((experts_all * capacity, MODEL_WIDTH), jnp.bfloat16)
        .at[target_rows]
        .set(jnp.broadcast_to(ffn_in[:, None, :], (sequence_length, TOP, MODEL_WIDTH)))
        .reshape(experts_all, capacity, MODEL_WIDTH)
    )
    received = lax.all_to_all(expert_in, "fsdp", split_axis=0, concat_axis=0, tiled=True)
    sources = received.shape[0] // local_experts
    grouped = received.reshape(sources, local_experts, received.shape[1], MODEL_WIDTH)
    result_rows = ffn_forward(grouped, w_gate, w_up, w_down).reshape(received.shape)
    returned = lax.all_to_all(result_rows, "fsdp", split_axis=0, concat_axis=0, tiled=True)
    picked = returned.reshape(experts_all * capacity, MODEL_WIDTH)[target_rows].astype(jnp.float32)
    output = (hidden + jnp.sum(gate_probs[:, :, None] * picked, 1)).astype(jnp.bfloat16)
    grad_out = cotangent.astype(jnp.float32)
    grad_probs = jnp.sum(grad_out[:, None, :] * picked, -1)
    grad_expert_out = (
        jnp.zeros((experts_all * capacity, MODEL_WIDTH), jnp.bfloat16)
        .at[target_rows]
        .set((gate_probs[:, :, None] * grad_out[:, None, :]).astype(jnp.bfloat16))
        .reshape(experts_all, capacity, MODEL_WIDTH)
    )
    owner_grads = lax.all_to_all(grad_expert_out, "fsdp", split_axis=0, concat_axis=0, tiled=True)
    sources = owner_grads.shape[0] // local_experts
    grouped_in = received.reshape(sources, local_experts, capacity, MODEL_WIDTH)
    grouped_grads = owner_grads.reshape(sources, local_experts, capacity, MODEL_WIDTH)
    grad_input, grad_gate, grad_up, expert_hid = ffn_back(
        grouped_in, grouped_grads, w_gate, w_up, w_down
    )
    grad_expert_in = lax.all_to_all(
        grad_input.reshape(experts_all, capacity, MODEL_WIDTH),
        "fsdp",
        split_axis=0,
        concat_axis=0,
        tiled=True,
    )
    expert_terms = weight_terms(grouped_in, grouped_grads, grad_gate, grad_up, expert_hid)
    grad_ffn_in = jnp.sum(
        grad_expert_in.reshape(experts_all * capacity, MODEL_WIDTH)[target_rows].astype(
            jnp.float32
        ),
        1,
    )
    gate_dot = jnp.sum(grad_probs * gate_probs, -1, keepdims=True)
    grad_chosen = gate_probs * (grad_probs - gate_dot)
    grad_logits = jnp.sum(grad_chosen[:, :, None] * onehot, 1).astype(jnp.bfloat16)
    query_full, key_full, value_full, out_full, gain_one, gain_two, router_full = (
        lax.all_gather(w_query, "fsdp", axis=0, tiled=True),
        lax.all_gather(key_weight, "fsdp", axis=0, tiled=True),
        lax.all_gather(value_weight, "fsdp", axis=0, tiled=True),
        lax.all_gather(w_out, "fsdp", axis=0, tiled=True),
        lax.all_gather(gain_attn, "fsdp", axis=0, tiled=True),
        lax.all_gather(gain_ffn, "fsdp", axis=0, tiled=True),
        lax.all_gather(w_router, "fsdp", axis=0, tiled=True),
    )
    grad_router = jnp.dot(ffn_in.T, grad_logits, preferred_element_type=jnp.float32)
    grad_ffn_in = grad_ffn_in + jnp.dot(
        grad_logits, router_full.T, preferred_element_type=jnp.float32
    )
    grad_hidden_norm, grad_gain_two = norm_back(
        grad_ffn_in, normed_two, inv_two, gain_two.astype(jnp.float32)
    )
    grad_hidden = grad_out + grad_hidden_norm
    grad_branch = grad_hidden.astype(jnp.bfloat16)
    grad_out_w = jnp.dot(attn_mixed.T, grad_branch, preferred_element_type=jnp.float32)
    grad_attention_mixed = jnp.dot(
        grad_branch, out_full.T, preferred_element_type=jnp.float32
    ).astype(jnp.bfloat16)
    grad_attention_mixed = grad_attention_mixed.reshape(
        sequence_length, KEY_VALUE_HEADS, QUERY_HEADS // KEY_VALUE_HEADS, HEAD_SIZE
    )
    grad_qrot, grad_key_rotated, grad_value_per_head = attention_backward(
        query_rotated, key_rot, value_per_head, log_total, grad_attention_mixed
    )
    grad_query_proj = (
        rotary_backward(grad_qrot, cosine_table, sine_table)
        .reshape(sequence_length, QUERY_HEADS * HEAD_SIZE)
        .astype(jnp.bfloat16)
    )
    grad_key_proj = (
        rotary_backward(grad_key_rotated, cosine_table, sine_table)
        .reshape(sequence_length, KEY_VALUE_HEADS * HEAD_SIZE)
        .astype(jnp.bfloat16)
    )
    grad_value_projected = grad_value_per_head.reshape(
        sequence_length, KEY_VALUE_HEADS * HEAD_SIZE
    ).astype(jnp.bfloat16)
    grad_query_w = jnp.dot(attention_input.T, grad_query_proj, preferred_element_type=jnp.float32)
    grad_key_w = jnp.dot(attention_input.T, grad_key_proj, preferred_element_type=jnp.float32)
    grad_value_w = jnp.dot(
        attention_input.T, grad_value_projected, preferred_element_type=jnp.float32
    )
    grad_attn_in = jnp.dot(grad_query_proj, query_full.T, preferred_element_type=jnp.float32)
    grad_attn_in = grad_attn_in + jnp.dot(
        grad_key_proj, key_full.T, preferred_element_type=jnp.float32
    )
    grad_attn_in = grad_attn_in + jnp.dot(
        grad_value_projected, value_full.T, preferred_element_type=jnp.float32
    )
    grad_tokens_norm, grad_gain_one = norm_back(
        grad_attn_in, normed_one, inv_one, gain_one.astype(jnp.float32)
    )
    grad_tokens = (grad_hidden + grad_tokens_norm).astype(jnp.bfloat16)
    shard_grads = (
        lax.psum_scatter(
            grad_query_w.astype(jnp.bfloat16), "fsdp", scatter_dimension=0, tiled=True
        ).astype(jnp.float32),
        lax.psum_scatter(
            grad_key_w.astype(jnp.bfloat16), "fsdp", scatter_dimension=0, tiled=True
        ).astype(jnp.float32),
        lax.psum_scatter(
            grad_value_w.astype(jnp.bfloat16), "fsdp", scatter_dimension=0, tiled=True
        ).astype(jnp.float32),
        lax.psum_scatter(
            grad_out_w.astype(jnp.bfloat16), "fsdp", scatter_dimension=0, tiled=True
        ).astype(jnp.float32),
        lax.psum_scatter(
            grad_gain_one.astype(jnp.bfloat16), "fsdp", scatter_dimension=0, tiled=True
        ).astype(jnp.float32),
        lax.psum_scatter(
            grad_gain_two.astype(jnp.bfloat16), "fsdp", scatter_dimension=0, tiled=True
        ).astype(jnp.float32),
        lax.psum_scatter(
            grad_router.astype(jnp.bfloat16), "fsdp", scatter_dimension=0, tiled=True
        ).astype(jnp.float32),
    )
    sq_query, sq_key, sq_value, sq_out, sq_gain_one, sq_gain_two, sq_router = shard_grads
    totals = (
        lax.psum(sq_query.astype(jnp.bfloat16), "dp").astype(jnp.float32),
        lax.psum(sq_key.astype(jnp.bfloat16), "dp").astype(jnp.float32),
        lax.psum(sq_value.astype(jnp.bfloat16), "dp").astype(jnp.float32),
        lax.psum(sq_out.astype(jnp.bfloat16), "dp").astype(jnp.float32),
        lax.psum(sq_gain_one.astype(jnp.bfloat16), "dp").astype(jnp.float32),
        lax.psum(sq_gain_two.astype(jnp.bfloat16), "dp").astype(jnp.float32),
        lax.psum(sq_router.astype(jnp.bfloat16), "dp").astype(jnp.float32),
        lax.psum(expert_terms.astype(jnp.bfloat16), "dp").astype(jnp.float32),
    )
    expert_sum = totals[7]
    grad_down_w = jnp.transpose(expert_sum[:, 2], (0, 2, 1))
    return (
        output,
        grad_tokens,
        totals[0],
        totals[1],
        totals[2],
        totals[3],
        totals[4],
        totals[5],
        totals[6],
        expert_sum[:, 0],
        expert_sum[:, 1],
        grad_down_w,
    )


def solution(mesh):
    in_specs = (
        P(("fsdp", "dp"), None),
        P("fsdp", None),
        P("fsdp", None),
        P("fsdp", None),
        P("fsdp", None),
        P("fsdp"),
        P("fsdp"),
        P("fsdp", None),
        P("fsdp", None, None),
        P("fsdp", None, None),
        P("fsdp", None, None),
        P(("fsdp", "dp"), None),
        P(("fsdp", "dp"), None),
    )
    out_specs = (
        P(("fsdp", "dp"), None),
        P(("fsdp", "dp"), None),
        P("fsdp", None),
        P("fsdp", None),
        P("fsdp", None),
        P("fsdp", None),
        P("fsdp"),
        P("fsdp"),
        P("fsdp", None),
        P("fsdp", None, None),
        P("fsdp", None, None),
        P("fsdp", None, None),
    )
    return jax.shard_map(body, mesh=mesh, in_specs=in_specs, out_specs=out_specs, check_vma=False)
```

profile of v0, /device:TPU:10, one launch (start us, length us, event | category | flops | bytes accessed | tf_op | source)
XLA Modules:
  0.0 1383.2 jit_solution(2335086406017914877)
XLA Ops:
  13.7 13.3 all-reduce.5
  27.0 14.9 %all-gather = bf16[8,192,16]{1,2,0:T(8,128)(2,1)S(1)} all-gather(bf16[1,192,16]{1,2,0:T(8,128)(2,1)} %bitcast.239), channel_id=1, replica_groups=mesh['fsdp'=8,'dp'=4] {'fsdp'}, dimensions={0}, use_global_device_ids=true | all-gather | bytes 55296 | tf_op jit(solution)/shard_map/all_gather | solution.py:203
  43.9 16.8 %gather_fusion.3 = f32[2048]{0:T(1024)S(1)} fusion(f32[256,16]{0,1:T(8,128)S(1)} %fusion.73, s32[2048]{0:T(1024)S(1)} %reshape.267), kind=kCustom, calls=%fused_computation.1.clone | custom fusion | bytes 32768 | tf_op jit(solution)/shard_map/jit(take_along_axis)/gather | solution.py:243
  71.3 42.5 %all-gather.10.cloned.1.call-done = bf16[1536,1536]{1,0:T(8,128)(2,1)} async-done(((bf16[192,1536]{1,0:T(8,128)(2,1)}), bf16[1536,1536]{1,0:T(8,128)(2,1)}) %all-gather.10.cloned.1.call-update) | async-done | bytes 4718608 | tf_op jit(solution)/shard_map/all_gather | solution.py:197
  124.8 41.1 %all-gather.12.cloned.1.call-done = bf16[1536,1536]{1,0:T(8,128)(2,1)} async-done(((bf16[192,1536]{1,0:T(8,128)(2,1)}), bf16[1536,1536]{1,0:T(8,128)(2,1)}) %all-gather.12.cloned.1.call-update) | async-done | bytes 4718608 | tf_op jit(solution)/shard_map/all_gather | solution.py:200
  172.7 16.8 %gather_fusion.2 = f32[2048]{0:T(1024)S(1)} fusion(f32[256,16]{0,1:T(8,128)S(1)} %fusion.95, s32[2048]{0:T(1024)S(1)} %reshape.267), kind=kCustom, calls=%fused_computation.clone | custom fusion | bytes 32768 | tf_op jit(solution)/shard_map/jit(take_along_axis)/gather | solution.py:234
  190.0 14.9 %scatter_custom_fusion = bf16[2304,1536]{1,0:T(8,128)(2,1)} fusion(s32[2048]{0:T(1024)S(1)} %reshape.220, bf16[]{:T(256)} %constant.57.clone.1, bf16[256,1536]{1,0:T(8,128)(2,1)} %copy-done.8), kind=kCustom, calls=%fused_computation.32 | custom fusion | bytes 7864322 | tf_op jit(solution)/shard_map/scatter | solution.py:248
  214.3 14.8 %scatter_custom_fusion.1 = bf16[2304,1536]{1,0:T(8,128)(2,1)} fusion(s32[2048]{0:T(1024)S(1)} %reshape.220, f32[256,1536]{1,0:T(8,128)} %convert_element_type.194, f32[256,8]{1,0:T(8,128)S(1)} %copy.169, bf16[]{:T(256)} %constant.57.clone.1), kind=kCustom, calls=%fused_computation.20 | custom fusion | flops 6291456 | bytes 8781826 | tf_op jit(solution)/shard_map/scatter | solution.py:263
  229.0 134.9 %all-to-all-done = bf16[16,144,1536]{2,1,0:T(8,128)(2,1)} async-done(((bf16[16,144,1536]{2,1,0:T(8,128)(2,1)}), bf16[16,144,1536]{2,1,0:T(8,128)(2,1)}, u32[]{:S(2)}, u32[]{:S(2)}) %all-to-all-start) | async-done | bytes 7077920 | tf_op jit(solution)/shard_map/all_to_all | solution.py:251
  372.5 10.1 fusion.14
  391.0 133.7 %all-to-all-done.2 = bf16[16,144,1536]{2,1,0:T(8,128)(2,1)} async-done(((bf16[16,144,1536]{2,1,0:T(8,128)(2,1)}), bf16[16,144,1536]{2,1,0:T(8,128)(2,1)}, u32[]{:S(2)}, u32[]{:S(2)}) %all-to-all-start.2) | async-done | bytes 7077920 | tf_op jit(solution)/shard_map/all_to_all | solution.py:266
  524.7 11.8 fusion.23
  579.3 127.1 %all-to-all-done.1 = bf16[16,144,1536]{2,1,0:T(8,128)(2,1)} async-done(((bf16[16,144,1536]{2,1,0:T(8,128)(2,1)}), bf16[16,144,1536]{2,1,0:T(8,128)(2,1)}, u32[]{:S(2)}, u32[]{:S(2)}) %all-to-all-start.1) | async-done | bytes 7077920 | tf_op jit(solution)/shard_map/all_to_all | solution.py:255
  715.2 17.3 %gather_fusion = bf16[2048,1536]{1,0:T(8,128)(2,1)} fusion(bf16[2304,1536]{1,0:T(8,128)(2,1)} %bitcast.29, s32[2048]{0:T(1024)S(1)} %broadcast_clamp_fusion), kind=kCustom, calls=%fused_computation.2 | custom fusion | bytes 12591104 | tf_op jit(solution)/shard_map/gather | solution.py:256
  742.1 125.1 %all-to-all-done.3 = bf16[16,144,1536]{2,1,0:T(8,128)(2,1)} async-done(((bf16[16,144,1536]{2,1,0:T(8,128)(2,1)}), bf16[16,144,1536]{2,1,0:T(8,128)(2,1)}, u32[]{:S(2)}, u32[]{:S(2)}) %all-to-all-start.3) | async-done | bytes 7077920 | tf_op jit(solution)/shard_map/all_to_all | solution.py:273
  867.2 17.2 %gather_fusion.1 = bf16[2048,1536]{1,0:T(8,128)(2,1)} fusion(bf16[2304,1536]{1,0:T(8,128)(2,1)} %bitcast.40, s32[2048]{0:T(1024)S(1)} %broadcast_clamp_fusion), kind=kCustom, calls=%fused_computation.3 | custom fusion | bytes 12591104 | tf_op jit(solution)/shard_map/gather | solution.py:282
  938.0 10.3 fusion.33
  948.3 10.3 fusion.32
  969.4 56.3 %reduce-scatter.14.cloned.1.call-done = bf16[192,1536]{1,0:T(8,128)(2,1)} async-done(((bf16[1536,1536]{1,0:T(8,128)(2,1)}), bf16[192,1536]{1,0:T(8,128)(2,1)}) %reduce-scatter.14.cloned.1.call-update) | async-done | bytes 589840 | tf_op jit(solution)/shard_map/reduce_scatter | solution.py:357
  1025.7 56.2 %reduce-scatter.8.cloned.1.call-done = bf16[192,1536]{1,0:T(8,128)(2,1)} async-done(((bf16[1536,1536]{1,0:T(8,128)(2,1)}), bf16[192,1536]{1,0:T(8,128)(2,1)}) %reduce-scatter.8.cloned.1.call-update) | async-done | bytes 589840 | tf_op jit(solution)/shard_map/reduce_scatter | solution.py:348
  1090.4 13.2 all-reduce.4
  1124.0 212.0 %all-reduce.10.cloned.1.call-done = (bf16[192,1536]{1,0:T(8,128)(2,1)}, bf16[192,512]{1,0:T(8,128)(2,1)}, bf16[192,512]{1,0:T(8,128)(2,1)}, bf16[192,1536]{1,0:T(8,128)(2,1)}, bf16[2,3,1536,512]{3,2,0,1:T(8,128)(2,1)}) async-done(((bf16[192,1536]{1,0:T(8,128)(2,1)}, bf16[192,512]{1,0:T(8,128)(2,1)}, bf16[192,512]{1,0:T(8,128)(2,1)}, bf16[192,1536]{1,0:T(8,128)(2,1)}, bf16[2,3,1536,512]{3,2,0,1:T(8,128)(2,1)}), ...) | async-done | bytes 11010064 | tf_op jit(solution)/shard_map/psum | solution.py:372
  1342.8 12.8 convert_element_type.226
  1355.6 13.8 slice_bitcast_fusion
  (239 shorter events, 229.5 us)
Async XLA Ops:
  7.2 517.6 %copy-start = (bf16[2,512,1536]{2,1,0:T(8,128)(2,1)S(1)}, bf16[2,512,1536]{2,1,0:T(8,128)(2,1)}, u32[]{:S(2)}) copy-start(bf16[2,512,1536]{2,1,0:T(8,128)(2,1)} %param.25) | copy-start | bytes 9437188
  7.2 56.7 %all-gather.6.cloned.1.call-start = ((), (), s32[]{:S(2)}) async-start(), calls=%async_computation.9 | async-start | bytes 1769472 | tf_op jit(solution)/shard_map/all_gather | solution.py:199
  7.9 60.1 %all-gather.8.cloned.1.call-start = ((), (), s32[]{:S(2)}) async-start(), calls=%async_computation.10 | async-start | bytes 1769472 | tf_op jit(solution)/shard_map/all_gather | solution.py:198
  8.7 105.1 %all-gather.10.cloned.1.call-start = ((), (), s32[]{:S(2)}) async-start(), calls=%async_computation.11 | async-start | bytes 5308416 | tf_op jit(solution)/shard_map/all_gather | solution.py:197
  9.4 156.4 %all-gather.12.cloned.1.call-start = ((), (), s32[]{:S(2)}) async-start(), calls=%async_computation.12 | async-start | bytes 5308416 | tf_op jit(solution)/shard_map/all_gather | solution.py:200
  27.0 86.9 %copy-start.29 = (f32[1536]{0:T(1024)}, f32[1536]{0:T(1024)S(1)}, u32[]{:S(2)}) copy-start(f32[1536]{0:T(1024)S(1)} %convert_element_type.178) | copy-start | bytes 18436
  27.0 143.2 %copy-start.38 = (f32[1536]{0:T(1024)}, f32[1536]{0:T(1024)S(1)}, u32[]{:S(2)}) copy-start(f32[1536]{0:T(1024)S(1)} %convert_element_type.185) | copy-start | bytes 18436
  42.0 129.5 %copy-start.35 = (bf16[1536,16]{0,1:T(8,128)(2,1)}, bf16[1536,16]{0,1:T(8,128)(2,1)S(1)}, u32[]{:S(2)}) copy-start(bf16[1536,16]{0,1:T(8,128)(2,1)S(1)} %reshape.261) | copy-start | bytes 147460
  63.6 50.2 %copy-start.43 = (f32[256]{0:T(256)}, f32[256]{0:T(256)S(1)}, u32[]{:S(2)}) copy-start(f32[256]{0:T(256)S(1)} %add_rsqrt_fusion.1) | copy-start | bytes 3076
  63.8 54.7 %copy-start.24 = (f32[256,32]{0,1:T(8,128)}, f32[256,32]{0,1:T(8,128)S(1)}, u32[]{:S(2)}) copy-start(f32[256,32]{0,1:T(8,128)S(1)} %get-tuple-element.168) | copy-start | bytes 98308
  63.8 54.7 %copy-start.26 = (f32[256,32]{0,1:T(8,128)}, f32[256,32]{0,1:T(8,128)S(1)}, u32[]{:S(2)}) copy-start(f32[256,32]{0,1:T(8,128)S(1)} %get-tuple-element.169) | copy-start | bytes 98308
  68.0 53.1 %copy-start.23 = (bf16[256,512]{0,1:T(8,128)(2,1)}, bf16[256,512]{0,1:T(8,128)(2,1)S(1)}, u32[]{:S(2)}) copy-start(bf16[256,512]{0,1:T(8,128)(2,1)S(1)} %copy.162) | copy-start | bytes 786436
  170.2 19.4 %copy-start.46 = (f32[256]{0:T(256)}, f32[256]{0:T(256)S(1)}, u32[]{:S(2)}) copy-start(f32[256]{0:T(256)S(1)} %add_rsqrt_fusion) | copy-start | bytes 3076
  204.8 159.1 %all-to-all-start = ((bf16[16,144,1536]{2,1,0:T(8,128)(2,1)}), bf16[16,144,1536]{2,1,0:T(8,128)(2,1)}, u32[]{:S(2)}, u32[]{:S(2)}) async-start(bf16[16,144,1536]{2,1,0:T(8,128)(2,1)} %bitcast.217), calls=%async_computation | async-start | bytes 14155776 | tf_op jit(solution)/shard_map/all_to_all | solution.py:251
  363.9 160.8 %all-to-all-start.2 = ((bf16[16,144,1536]{2,1,0:T(8,128)(2,1)}), bf16[16,144,1536]{2,1,0:T(8,128)(2,1)}, u32[]{:S(2)}, u32[]{:S(2)}) async-start(bf16[16,144,1536]{2,1,0:T(8,128)(2,1)} %bitcast.215), calls=%async_computation.2 | async-start | bytes 14155776 | tf_op jit(solution)/shard_map/all_to_all | solution.py:266
  545.5 160.9 %all-to-all-start.1 = ((bf16[16,144,1536]{2,1,0:T(8,128)(2,1)}), bf16[16,144,1536]{2,1,0:T(8,128)(2,1)}, u32[]{:S(2)}, u32[]{:S(2)}) async-start(bf16[16,144,1536]{2,1,0:T(8,128)(2,1)} %bitcast.216), calls=%async_computation.1 | async-start | bytes 14155776 | tf_op jit(solution)/shard_map/all_to_all | solution.py:255
  706.4 160.8 %all-to-all-start.3 = ((bf16[16,144,1536]{2,1,0:T(8,128)(2,1)}), bf16[16,144,1536]{2,1,0:T(8,128)(2,1)}, u32[]{:S(2)}, u32[]{:S(2)}) async-start(bf16[16,144,1536]{2,1,0:T(8,128)(2,1)} %bitcast.214), calls=%async_computation.3 | async-start | bytes 14155776 | tf_op jit(solution)/shard_map/all_to_all | solution.py:273
  714.9 254.5 %reduce-scatter.12.cloned.1.call-start = ((), (), s32[]{:S(2)}) async-start(), calls=%async_computation.15 | async-start | bytes 1769472 | tf_op jit(solution)/shard_map/reduce_scatter | solution.py:354
  715.2 17.3 %copy-start.7 = (f32[256,1536]{1,0:T(8,128)S(1)}, f32[256,1536]{1,0:T(8,128)}, u32[]{:S(2)}) copy-start(f32[256,1536]{1,0:T(8,128)} %convert_element_type.194) | copy-start | bytes 4718596
  901.9 67.5 %reduce-scatter.10.cloned.1.call-start = ((), (), s32[]{:S(2)}) async-start(), calls=%async_computation.14 | async-start | bytes 1769472 | tf_op jit(solution)/shard_map/reduce_scatter | solution.py:351
  916.6 109.0 %reduce-scatter.14.cloned.1.call-start = ((), (), s32[]{:S(2)}) async-start(), calls=%async_computation.16 | async-start | bytes 5308416 | tf_op jit(solution)/shard_map/reduce_scatter | solution.py:357
  920.3 161.6 %reduce-scatter.8.cloned.1.call-start = ((), (), s32[]{:S(2)}) async-start(), calls=%async_computation.13 | async-start | bytes 5308416 | tf_op jit(solution)/shard_map/reduce_scatter | solution.py:348
  927.9 185.1 %reduce-scatter.16.cloned.1.call-start = ((), (), s32[]{:S(2)}) async-start(), calls=%async_computation.17 | async-start | bytes 442368
  959.8 376.2 %all-reduce.10.cloned.1.call-start = ((), (), s32[]{:S(2)}) async-start(), calls=%async_computation.18 | async-start | bytes 22020096 | tf_op jit(solution)/shard_map/psum | solution.py:372
  (46 other events, 236.6 us)
Sparse Core Ops, SparseCore 0:
  9.7 26.5 all-gather.5
  37.9 24.3 all-gather.7
  64.0 49.8 all-gather.9
  115.3 50.4 all-gather.11
  902.0 32.2 reduce-scatter.11
  936.5 32.2 reduce-scatter.9
  971.6 53.9 reduce-scatter.13
  1028.5 53.3 reduce-scatter.7
  1084.7 28.2 reduce-scatter.15
  1117.8 218.1 all-reduce.9
where the time goes:
time: 1400 us; the launch traced here: 1380 us
  waiting for transfers between devices  938 us (67%)
  matrix products  133 us (10%)
  local copies, waits for them, and re-layouts  132 us (9%)
  other arithmetic  79.8 us (6%)
  blocking collectives  49.8 us (4%)
  starting transfers between devices  33.7 us (2%)
  between operations  16.6 us (1%)
    psum x1, waiting for transfers between devices, body(): lax.psum(sq_query.astype(jnp.bfloat16), 'dp').astype(jnp.float32)  212 us
    all_to_all x1, waiting for transfers between devices, body(): lax.all_to_all(expert_in, 'fsdp', split_axis=0, concat_axis=0, tiled=True)  135 us
    all_to_all x1, waiting for transfers between devices, body(): lax.all_to_all(grad_expert_out, 'fsdp', split_axis=0, concat_axis=0, tile...  134 us
    all_to_all x1, waiting for transfers between devices, body(): lax.all_to_all(result_rows, 'fsdp', split_axis=0, concat_axis=0, tiled=True)  127 us
    all_to_all x1, waiting for transfers between devices, body(): lax.all_to_all(grad_input.reshape(experts_all, capacity, MODEL_WIDTH), 'f...  125 us
    reduce_scatter x1, waiting for transfers between devices, body(): lax.psum_scatter(grad_out_w.astype(jnp.bfloat16), 'fsdp', scatter_dimensi...  56.3 us
    reduce_scatter x1, waiting for transfers between devices, body(): lax.psum_scatter(grad_query_w.astype(jnp.bfloat16), 'fsdp', scatter_dimen...  56.2 us
    all_gather x1, waiting for transfers between devices, body(): lax.all_gather(w_query, 'fsdp', axis=0, tiled=True)  42.5 us
  transfers between devices with their start and end apart: 14, of which 10 were waited for; matrix products, arithmetic and copies ran while one was open for 15% of the time, Pallas kernels for 0%

commit v1 on v0

v1 whole, which is shorter than its diff:
```python
import jax
import jax.numpy as jnp
from jax import lax
from jax.sharding import PartitionSpec as P

MODEL_WIDTH = 1536
QUERY_HEADS = 24
KEY_VALUE_HEADS = 8
HEAD_SIZE = 64
TOP = 8
GROUP = QUERY_HEADS // KEY_VALUE_HEADS
QW = QUERY_HEADS * HEAD_SIZE
KW = KEY_VALUE_HEADS * HEAD_SIZE

EPSILON = 1e-06
ROPE_BASE = 10000.0
MASKED = -1e30
F32 = jnp.float32
BF = jnp.bfloat16


def rope_tables(sequence_length):
    half_size = HEAD_SIZE // 2
    positions = jnp.arange(sequence_length, dtype=F32)
    frequency = ROPE_BASE ** (-2.0 * jnp.arange(half_size, dtype=F32) / HEAD_SIZE)
    angles = positions[:, None] * frequency[None, :]
    return (jnp.cos(angles)[:, None, :], jnp.sin(angles)[:, None, :])


def rotate(values, c, s):
    h = values.shape[-1] // 2
    a, b = values[..., :h], values[..., h:]
    return jnp.concatenate([a * c - b * s, a * s + b * c], -1)


def rms_scale(values):
    return lax.rsqrt(jnp.mean(values * values, -1, keepdims=True) + EPSILON)


def norm_back(grad_normed, normed, inv_rms, gain_vec):
    scaled = grad_normed * gain_vec
    grad_input = inv_rms * (scaled - normed * jnp.mean(scaled * normed, -1, keepdims=True))
    return (grad_input, jnp.sum(grad_normed * normed, 0))


def mm(spec, a, b):
    return jnp.einsum(spec, a, b, preferred_element_type=F32)


def body(tokens, w_query, key_weight, value_weight, w_out, gain_attn, gain_ffn, w_router,
         w_gate, w_up, w_down, routes, cotangent):
    T = tokens.shape[0]
    el = w_gate.shape[0]
    nf = lax.axis_size("fsdp")
    nd = lax.axis_size("dp")
    experts = el * nf
    cap = 9 * T * TOP // (8 * experts)
    dp = lax.axis_index("dp")
    fs = lax.axis_index("fsdp")

    packed = jnp.concatenate([w_query, key_weight, value_weight, w_out], 1)
    rows = packed.shape[0] // nd
    mine = lax.dynamic_slice_in_dim(packed, dp * rows, rows, 0)
    full = lax.all_gather(mine, ("fsdp", "dp"), axis=0, tiled=True)
    qkv_full = full[:, : QW + 2 * KW]
    out_full = full[:, QW + 2 * KW:]
    small = jnp.concatenate([w_router, gain_attn[:, None], gain_ffn[:, None]], 1)
    small_full = lax.all_gather(small, "fsdp", axis=0, tiled=True)
    router_full = small_full[:, :experts]
    gain_one = small_full[:, experts].astype(F32)
    gain_two = small_full[:, experts + 1].astype(F32)

    onehot = (routes[:, :, None] == jnp.arange(experts, dtype=jnp.int32)).any(1)
    before = jnp.cumsum(onehot.astype(jnp.int32), 0) - onehot.astype(jnp.int32)
    slots = jnp.where(onehot, before, -1).astype(F32)

    cot_all = lax.all_gather(cotangent, "fsdp", axis=0)

    xf = tokens.astype(F32)
    r1 = rms_scale(xf)
    n1 = xf * r1
    attn_in = (n1 * gain_one).astype(BF)
    proj = jnp.dot(attn_in, qkv_full, preferred_element_type=F32)
    c, s = rope_tables(T)
    q = rotate(proj[:, :QW].reshape(T, QUERY_HEADS, HEAD_SIZE), c, s).astype(BF)
    q = q.reshape(T, KEY_VALUE_HEADS, GROUP, HEAD_SIZE)
    k = rotate(proj[:, QW: QW + KW].reshape(T, KEY_VALUE_HEADS, HEAD_SIZE), c, s).astype(BF)
    v = proj[:, QW + KW:].astype(BF).reshape(T, KEY_VALUE_HEADS, HEAD_SIZE)
    factor = HEAD_SIZE ** (-0.5)
    scores = mm("qgrd,kgd->grqk", q, k) * factor
    keep = jnp.arange(T)[None, :] <= jnp.arange(T)[:, None]
    scores = jnp.where(keep, scores, MASKED)
    top = jnp.max(scores, -1, keepdims=True)
    ex = jnp.exp(scores - top)
    probs = ex / jnp.sum(ex, -1, keepdims=True)
    probs_low = probs.astype(BF)
    mixed = mm("grqk,kgd->qgrd", probs_low, v).reshape(T, QW).astype(BF)
    hidden = xf + jnp.dot(mixed, out_full, preferred_element_type=F32)
    r2 = rms_scale(hidden)
    n2 = hidden * r2
    ffn_in = (n2 * gain_two).astype(BF)
    logits = jnp.dot(ffn_in, router_full, preferred_element_type=F32)
    gates = jnp.where(onehot, logits, MASKED)
    gates = jnp.exp(gates - jnp.max(gates, -1, keepdims=True))
    gates = jnp.where(onehot, gates, 0.0)
    gates = gates / jnp.sum(gates, -1, keepdims=True)

    ffn_all = lax.all_gather(ffn_in, "fsdp", axis=0)
    side = lax.all_gather(jnp.stack([slots.T, gates.T]), "fsdp", axis=0)
    side = lax.dynamic_slice_in_dim(side, fs * el, el, 2)
    slot_l, gate_l = side[:, 0], side[:, 1]
    pick = slot_l[:, :, None, :] == jnp.arange(cap, dtype=F32)[None, None, :, None]
    sel = pick.astype(BF)
    gate_row = jnp.sum(jnp.where(pick, gate_l[:, :, None, :], 0.0), -1, keepdims=True)

    x = mm("nect,ntd->necd", sel, ffn_all).astype(BF)
    g = mm("nect,ntd->necd", sel, cot_all).astype(BF)
    gate_val = mm("necd,edf->necf", x, w_gate)
    up_val = mm("necd,edf->necf", x, w_up)
    sg = jax.nn.sigmoid(gate_val)
    act = gate_val * sg
    hid = act * up_val
    u = mm("necd,efd->necf", g, w_down)
    grad_probs_row = jnp.sum(hid.astype(BF).astype(F32) * u, -1)
    hid_g = (hid * gate_row).astype(BF)
    grad_hid = u * gate_row
    grad_up = (grad_hid * act).astype(BF)
    grad_gate = (grad_hid * up_val * sg * (1.0 + gate_val * (1.0 - sg))).astype(BF)
    out_rows = mm("necf,efd->necd", hid_g, w_down).astype(BF)
    gin_rows = (mm("necf,edf->necd", grad_gate, w_gate) + mm("necf,edf->necd", grad_up, w_up)).astype(BF)
    out_part = mm("nect,necd->ntd", sel, out_rows).astype(BF)
    gin_part = mm("nect,necd->ntd", sel, gin_rows).astype(BF)
    gp_part = jnp.sum(jnp.where(pick, grad_probs_row[..., None], 0.0), 2)
    gp_all = lax.all_to_all(gp_part, "fsdp", split_axis=0, concat_axis=0)
    grad_probs = gp_all.reshape(experts, T).T
    gin_own = lax.psum_scatter(gin_part, "fsdp", scatter_dimension=0, tiled=False)
    out_own = lax.psum_scatter(out_part, "fsdp", scatter_dimension=0, tiled=False)
    term_gate = mm("necd,necf->edf", x, grad_gate)
    term_up = mm("necd,necf->edf", x, grad_up)
    term_down = mm("necf,necd->efd", hid_g, g)
    terms = (term_gate.astype(BF), term_up.astype(BF), term_down.astype(BF))
    terms = lax.psum(terms, "dp")

    output = (hidden + out_own.astype(F32)).astype(BF)
    grad_out = cotangent.astype(F32)
    dot = jnp.sum(grad_probs * gates, -1, keepdims=True)
    grad_logits = (gates * (grad_probs - dot)).astype(BF)
    grad_router = jnp.dot(ffn_in.T, grad_logits, preferred_element_type=F32)
    gffn = gin_own.astype(F32) + jnp.dot(grad_logits, router_full.T, preferred_element_type=F32)
    gh, grad_gain_two = norm_back(gffn, n2, r2, gain_two)
    grad_hidden = grad_out + gh
    branch = grad_hidden.astype(BF)
    grad_out_w = jnp.dot(mixed.T, branch, preferred_element_type=F32)
    gm = jnp.dot(branch, out_full.T, preferred_element_type=F32).astype(BF)
    gm = gm.reshape(T, KEY_VALUE_HEADS, GROUP, HEAD_SIZE)
    gp = mm("qgrd,kgd->grqk", gm, v)
    row = jnp.sum(probs * gp, -1, keepdims=True)
    gs = (probs * (gp - row)).astype(BF)
    gq = mm("grqk,kgd->qgrd", gs, k) * factor
    gk = mm("grqk,qgrd->kgd", gs, q) * factor
    gv = mm("grqk,qgrd->kgd", probs_low, gm)
    gq = rotate(gq.reshape(T, QUERY_HEADS, HEAD_SIZE), c, -s).reshape(T, QW)
    gk = rotate(gk, c, -s).reshape(T, KW)
    gproj = jnp.concatenate([gq, gk, gv.reshape(T, KW)], 1).astype(BF)
    grad_qkv_w = jnp.dot(attn_in.T, gproj, preferred_element_type=F32)
    gattn = jnp.dot(gproj, qkv_full.T, preferred_element_type=F32)
    gt, grad_gain_one = norm_back(gattn, n1, r1, gain_one)
    grad_tokens = (grad_hidden + gt).astype(BF)

    big = jnp.concatenate([grad_qkv_w.astype(BF), grad_out_w.astype(BF)], 1)
    big = lax.psum_scatter(big, ("fsdp", "dp"), scatter_dimension=0, tiled=True)
    big = lax.all_gather(big, "dp", axis=0, tiled=True).astype(F32)
    tiny = jnp.concatenate([grad_router, grad_gain_one[:, None], grad_gain_two[:, None]], 1)
    tiny = lax.psum_scatter(tiny, "fsdp", scatter_dimension=0, tiled=True)
    tiny = lax.psum(tiny, "dp")
    return (
        output,
        grad_tokens,
        big[:, :QW],
        big[:, QW: QW + KW],
        big[:, QW + KW: QW + 2 * KW],
        big[:, QW + 2 * KW:],
        tiny[:, experts],
        tiny[:, experts + 1],
        tiny[:, :experts],
        terms[0].astype(F32),
        terms[1].astype(F32),
        terms[2].astype(F32),
    )


def solution(mesh):
    in_specs = (
        P(("fsdp", "dp"), None),
        P("fsdp", None),
        P("fsdp", None),
        P("fsdp", None),
        P("fsdp", None),
        P("fsdp"),
        P("fsdp"),
        P("fsdp", None),
        P("fsdp", None, None),
        P("fsdp", None, None),
        P("fsdp", None, None),
        P(("fsdp", "dp"), None),
        P(("fsdp", "dp"), None),
    )
    out_specs = (
        P(("fsdp", "dp"), None),
        P(("fsdp", "dp"), None),
        P("fsdp", None),
        P("fsdp", None),
        P("fsdp", None),
        P("fsdp", None),
        P("fsdp"),
        P("fsdp"),
        P("fsdp", None),
        P("fsdp", None, None),
        P("fsdp", None, None),
        P("fsdp", None, None),
    )
    return jax.shard_map(body, mesh=mesh, in_specs=in_specs, out_specs=out_specs, check_vma=False)
```

time: 1400 us -> 900 us (0.64)
  waiting for transfers between devices: 938 us -> 599 us
  local copies, waits for them, and re-layouts: 132 us -> 25.9 us
  starting transfers between devices: 33.7 us -> 0.37 us
  other arithmetic: 79.8 us -> 48 us
    all_to_all x4 -> x0, waiting for transfers between devices: 521 us -> none  [the longest x1 135 us: body(): lax.all_to_all(expert_in, 'fsdp', split_axis=0, concat_axis=0, tiled=True)]
    reduce_scatter x4 -> x3, waiting for transfers between devices: 113 us -> 232 us  [the longest x1 119 us: body(): big = lax.psum_scatter(big, ('fsdp', 'dp'), scatter_dimension=0, tiled=True)]
    all_gather x4, waiting for transfers between devices: 83.6 us -> 155 us  [the longest x1 80.6 us: body(): full = lax.all_gather(mine, ('fsdp', 'dp'), axis=0, tiled=True)]
    gather x10 -> x0, local copies, waits for them, and re-layouts: 69.3 us -> none  [the longest x3 17.6 us: body(): slot_ids = jnp.take_along_axis(before, routes, 1).astype(jnp.int32)]
    all_to_all x4 -> x0, starting transfers between devices: 32.4 us -> none  [the longest x1 8.58 us: body(): lax.all_to_all(result_rows, 'fsdp', split_axis=0, concat_axis=0, tiled=True)]
    unnamed x2 -> x0, blocking collectives: 26.5 us -> none
    all_gather x1 -> x2, blocking collectives: 14.9 us -> 39.2 us  [the longest x1 25 us: body(): side = lax.all_gather(jnp.stack([slots.T, gates.T]), 'fsdp', axis=0)]
    psum x1, waiting for transfers between devices: 212 us -> 194 us  [body(): terms = lax.psum(terms, 'dp')]
  transfers between devices with their start and end apart: 14 -> 9, of which waited for: 10 -> 8; matrix products, arithmetic and copies ran while one was open for 15% -> 13% of each run, Pallas kernels for 0% -> 0%
where the time goes in v1:
time: 900 us; the launch traced here: 891 us
  waiting for transfers between devices  599 us (67%)
  matrix products  140 us (16%)
  blocking collectives  63.1 us (7%)
  other arithmetic  48 us (5%)
  local copies, waits for them, and re-layouts  25.9 us (3%)
  between operations  14.8 us (2%)
    psum x1, waiting for transfers between devices, body(): terms = lax.psum(terms, 'dp')  194 us
    reduce_scatter x1, waiting for transfers between devices, body(): big = lax.psum_scatter(big, ('fsdp', 'dp'), scatter_dimension=0, tiled=True)  119 us
    dot_general x16, matrix products, mm(): return jnp.einsum(spec, a, b, preferred_element_type=F32)  103 us
    all_gather x1, waiting for transfers between devices, body(): full = lax.all_gather(mine, ('fsdp', 'dp'), axis=0, tiled=True)  80.6 us
    reduce_scatter x1, waiting for transfers between devices, body(): lax.psum_scatter(out_part, 'fsdp', scatter_dimension=0, tiled=False)  66.9 us
    all_gather x1, waiting for transfers between devices, body(): ffn_all = lax.all_gather(ffn_in, 'fsdp', axis=0)  56.6 us
    reduce_scatter x1, waiting for transfers between devices, body(): lax.psum_scatter(gin_part, 'fsdp', scatter_dimension=0, tiled=False)  45.5 us
    all_gather x1, blocking collectives, body(): side = lax.all_gather(jnp.stack([slots.T, gates.T]), 'fsdp', axis=0)  25 us
  transfers between devices with their start and end apart: 9, of which 8 were waited for; matrix products, arithmetic and copies ran while one was open for 13% of the time, Pallas kernels for 0%

profile of v1, /device:TPU:10, one launch (start us, length us, event | category | flops | bytes accessed | tf_op | source)
XLA Modules:
  0.0 890.7 jit_solution(15263671105453672468)
XLA Ops:
  10.1 14.2 %all-gather.3 = bf16[8,192,18]{1,2,0:T(8,128)(2,1)S(1)} all-gather(bf16[1,192,18]{1,2,0:T(8,128)(2,1)S(1)} %maximum_bitcast_fusion.6), channel_id=1, replica_groups=mesh['fsdp'=8,'dp'=4] {'fsdp'}, dimensions={0}, use_global_device_ids=true | all-gather | bytes 62208 | tf_op jit(solution)/shard_map/all_gather | solution.py:68
  27.4 80.6 %all-gather.9.cloned.1.call-done = bf16[1536,4096]{1,0:T(8,128)(2,1)} async-done(((bf16[48,4096]{1,0:T(8,128)(2,1)}), bf16[1536,4096]{1,0:T(8,128)(2,1)}) %all-gather.9.cloned.1.call-update) | async-done | bytes 12582928 | tf_op jit(solution)/shard_map/all_gather | solution.py:64
  108.0 5.8 fusion.9
  126.2 6.5 fusion.153
  149.0 25.0 %all-gather = f32[16,16,256]{2,1,0:T(8,128)S(1)} all-gather(f32[2,16,256]{2,1,0:T(8,128)S(1)} %pad_maximum_fusion.15), channel_id=2, replica_groups=mesh['fsdp'=8,'dp'=4] {'fsdp'}, dimensions={0}, use_global_device_ids=true | all-gather | bytes 294912 | tf_op jit(solution)/shard_map/all_gather | solution.py:109
  174.7 7.7 convolution_convert_fusion.2
  182.3 56.6 %all-gather.13.cloned.1.call-done = bf16[2048,1536]{1,0:T(8,128)(2,1)} async-done(((bf16[256,1536]{1,0:T(8,128)(2,1)}), bf16[2048,1536]{1,0:T(8,128)(2,1)}) %all-gather.13.cloned.1.call-update) | async-done | bytes 6291472 | tf_op jit(solution)/shard_map/all_gather | solution.py:108
  254.8 9.6 %fusion.29 = (f32[8,2,144]{2,0,1:T(8,128)S(1)}, f32[2,8,144,512]{3,2,1,0:T(8,128)}) fusion(f32[2,8,144,512]{3,2,1,0:T(8,128)} %fusion.18, f32[2,8,144,512]{3,2,1,0:T(8,128)} %fusion.20, bf16[2,512,1536]{2,1,0:T(8,128)(2,1)} %param.23, bf16[8,2,144,1536]{3,2,1,0:T(8,128)(2,1)S(1)} %bitcast.251), kind=kOutput, calls=%fused_computation.40 | convolution fusion | flops 3634493184 | bytes 24388608 | tf_op jit(solution)/shard_map/necd,efd->necf/dot_general | solution.py:47
  265.5 7.8 multiply_convert_fusion
  273.3 7.1 fusion.50
  280.3 13.2 %bitcast_convert_fusion = bf16[8,256,1536]{2,1,0:T(8,128)(2,1)} fusion(f32[2,8,144,1536]{3,2,0,1:T(8,128)} %fusion.50, bf16[2,1536,512]{2,1,0:T(8,128)(2,1)} %param.22, bf16[8,2,144,512]{3,2,0,1:T(8,128)(2,1)} %get-tuple-element.23, f32[8,2,256]{2,1,0:T(2,128)S(1)} %get-tuple-element.41), kind=kOutput, calls=%fused_computation.3 | convolution fusion | flops 5446631424 | bytes 25968640 | tf_op jit(solution)/shard_map/nect,necd->ntd/dot_general | solution.py:47
  295.2 10.7 %bitcast_convert_fusion.1 = bf16[8,256,1536]{2,1,0:T(8,128)(2,1)} fusion(f32[8,2,256]{2,1,0:T(2,128)S(1)} %get-tuple-element.41, bf16[2,512,1536]{2,1,0:T(8,128)(2,1)} %param.23, bf16[8,2,144,512]{3,2,0,1:T(8,128)(2,1)S(1)} %copy-done.20), kind=kOutput, calls=%fused_computation.4 | convolution fusion | flops 5443092480 | bytes 11812864 | tf_op jit(solution)/shard_map/nect,necd->ntd/dot_general | solution.py:47
  306.7 9.6 %all_to_all.5 = f32[8,2,256]{2,1,0:T(2,128)S(1)} all-to-all(f32[8,2,256]{2,1,0:T(2,128)S(1)} %copy-done.45), channel_id=1, replica_groups=mesh['fsdp'=8,'dp'=4] {'fsdp'}, dimensions={0} | all-to-all | bytes 32768 | tf_op jit(solution)/shard_map/all_to_all | solution.py:134
  316.4 45.5 %reduce-scatter.9.cloned.1.call-done = bf16[1,256,1536]{2,1,0:T(8,128)(2,1)} async-done(((bf16[8,256,1536]{2,1,0:T(8,128)(2,1)}), bf16[1,256,1536]{2,1,0:T(8,128)(2,1)}) %reduce-scatter.9.cloned.1.call-update) | async-done | bytes 786448 | tf_op jit(solution)/shard_map/reduce_scatter | solution.py:136
  365.9 66.9 %reduce-scatter.7.cloned.1.call-done = bf16[1,256,1536]{2,1,0:T(8,128)(2,1)} async-done(((bf16[8,256,1536]{2,1,0:T(8,128)(2,1)}), bf16[1,256,1536]{2,1,0:T(8,128)(2,1)}) %reduce-scatter.7.cloned.1.call-update) | async-done | bytes 786448 | tf_op jit(solution)/shard_map/reduce_scatter | solution.py:137
  465.4 9.0 %bitcast_convert_fusion.2 = bf16[2,512,1536]{2,1,0:T(8,128)(2,1)} fusion(bf16[8,2,144,512]{3,2,0,1:T(8,128)(2,1)S(1)} %copy-done.21, bf16[8,2,144,1536]{3,2,1,0:T(8,128)(2,1)} %convolution_convert_fusion.2), kind=kOutput, calls=%fused_computation.16 | convolution fusion | flops 3625451520 | bytes 12582912 | tf_op jit(solution)/shard_map/necf,necd->efd/dot_general | solution.py:47
  474.3 10.7 %bitcast_convert_fusion.4 = bf16[2,1536,512]{2,1,0:T(8,128)(2,1)} fusion(bf16[8,2,144,1536]{3,2,1,0:T(8,128)(2,1)} %copy-done.12, bf16[8,2,144,512]{3,2,0,1:T(8,128)(2,1)S(1)} %copy-done.19), kind=kOutput, calls=%fused_computation.18 | convolution fusion | flops 3625451520 | bytes 12582912 | tf_op jit(solution)/shard_map/necd,necf->edf/dot_general | solution.py:47
  485.0 5.7 bitcast_convert_fusion.3
  492.3 7.3 fusion.77
  500.8 119.2 %reduce-scatter.11.cloned.1.call-done = bf16[48,4096]{1,0:T(8,128)(2,1)} async-done(((bf16[1536,4096]{1,0:T(8,128)(2,1)}), bf16[48,4096]{1,0:T(8,128)(2,1)}) %reduce-scatter.11.cloned.1.call-update) | async-done | bytes 393232 | tf_op jit(solution)/shard_map/reduce_scatter | solution.py:171
  620.0 194.2 %all-reduce.3.cloned.1.call-done = (bf16[2,1536,512]{2,1,0:T(8,128)(2,1)}, bf16[2,1536,512]{2,1,0:T(8,128)(2,1)}, bf16[2,512,1536]{2,1,0:T(8,128)(2,1)}) async-done(((bf16[2,1536,512]{2,1,0:T(8,128)(2,1)}, bf16[2,1536,512]{2,1,0:T(8,128)(2,1)}, bf16[2,512,1536]{2,1,0:T(8,128)(2,1)}), (bf16[2,1536,512]{2,1,0:T(8,128)(2,1)}, bf16[2,1536,512]{2,1,0:T(8,128)(2,1)}, ...) | async-done | bytes 9437200 | tf_op jit(solution)/shard_map/psum | solution.py:142
  828.4 16.8 %reduce-scatter.13.cloned.1.call-done = f32[192,18]{1,0:T(8,128)} async-done(((f32[1536,18]{1,0:T(8,128)}), f32[192,18]{1,0:T(8,128)}) %reduce-scatter.13.cloned.1.call-update) | async-done | bytes 13840
  846.2 14.3 %psum.28 = f32[192,18]{0,1:T(8,128)S(1)} all-reduce(f32[192,18]{0,1:T(8,128)S(1)} %copy.138), channel_id=1, replica_groups=mesh['fsdp'=8,'dp'=4] {'dp'}, use_global_device_ids=true, to_apply=%region_22.23 | all-reduce | flops 3456 | bytes 27648 | tf_op jit(solution)/shard_map/psum | solution.py:175
  861.6 18.3 %all-gather.11.cloned.1.call-done = bf16[192,4096]{1,0:T(8,128)(2,1)} async-done(((bf16[48,4096]{1,0:T(8,128)(2,1)}), bf16[192,4096]{1,0:T(8,128)(2,1)}) %all-gather.11.cloned.1.call-update) | async-done | bytes 1572880 | tf_op jit(solution)/shard_map/all_gather | solution.py:172
  (233 shorter events, 113.9 us)
Async XLA Ops:
  7.2 242.1 %copy-start = (bf16[2,1536,512]{2,1,0:T(8,128)(2,1)S(1)}, bf16[2,1536,512]{2,1,0:T(8,128)(2,1)}, u32[]{:S(2)}) copy-start(bf16[2,1536,512]{2,1,0:T(8,128)(2,1)} %param.21) | copy-start | bytes 9437188
  7.2 100.8 %all-gather.9.cloned.1.call-start = ((), (), s32[]{:S(2)}) async-start(), calls=%async_computation.5 | async-start | bytes 12976128 | tf_op jit(solution)/shard_map/all_gather | solution.py:64
  9.3 165.4 %all-gather.15.cloned.1.call-start = ((), (), s32[]{:S(2)}) async-start(), calls=%async_computation.11 | async-start | bytes 7077888 | tf_op jit(solution)/shard_map/all_gather | solution.py:77
  10.0 228.9 %all-gather.13.cloned.1.call-start = ((), (), s32[]{:S(2)}) async-start(), calls=%async_computation.10 | async-start | bytes 7077888 | tf_op jit(solution)/shard_map/all_gather | solution.py:108
  24.5 83.5 %copy-start.30 = (bf16[1536,18]{0,1:T(8,128)(2,1)}, bf16[1536,18]{0,1:T(8,128)(2,1)S(1)}, u32[]{:S(2)}) copy-start(bf16[1536,18]{0,1:T(8,128)(2,1)S(1)} %reshape.199) | copy-start | bytes 165892
  25.2 82.8 %copy-start.41 = (f32[1536]{0:T(1024)}, f32[1536]{0:T(1024)S(1)}, u32[]{:S(2)}) copy-start(f32[1536]{0:T(1024)S(1)} %get-tuple-element.17) | copy-start | bytes 18436
  25.2 115.2 %copy-start.43 = (f32[1536]{0:T(1024)}, f32[1536]{0:T(1024)S(1)}, u32[]{:S(2)}) copy-start(f32[1536]{0:T(1024)S(1)} %get-tuple-element.16) | copy-start | bytes 18436
  26.6 87.2 %copy-start.51 = (f32[256]{0:T(256)}, f32[256]{0:T(256)S(1)}, u32[]{:S(2)}) copy-start(f32[256]{0:T(256)S(1)} %add_rsqrt_fusion.1) | copy-start | bytes 3076
  27.4 94.5 %copy-start.26 = (f32[256,32]{0,1:T(8,128)}, f32[256,32]{0,1:T(8,128)S(1)}, u32[]{:S(2)}) copy-start(f32[256,32]{0,1:T(8,128)S(1)} %get-tuple-element.46) | copy-start | bytes 98308
  27.4 94.5 %copy-start.35 = (f32[256,32]{0,1:T(8,128)}, f32[256,32]{0,1:T(8,128)S(1)}, u32[]{:S(2)}) copy-start(f32[256,32]{0,1:T(8,128)S(1)} %get-tuple-element.45) | copy-start | bytes 98308
  142.6 219.2 %reduce-scatter.9.cloned.1.call-start = ((), (), s32[]{:S(2)}) async-start(), calls=%async_computation.7 | async-start | bytes 7077888 | tf_op jit(solution)/shard_map/reduce_scatter | solution.py:136
  142.7 31.3 %copy-start.36 = (pred[256,16]{0,1:T(8,128)(4,1)}, pred[256,16]{0,1:T(8,128)(4,1)S(1)}, u32[]{:S(2)}) copy-start(pred[256,16]{0,1:T(8,128)(4,1)S(1)} %fusion.117) | copy-start | bytes 12292
  148.4 25.7 %copy-start.32 = (f32[256,16]{0,1:T(8,128)}, f32[256,16]{0,1:T(8,128)S(1)}, u32[]{:S(2)}) copy-start(f32[256,16]{0,1:T(8,128)S(1)} %get-tuple-element.52) | copy-start | bytes 49156
  293.6 139.2 %reduce-scatter.7.cloned.1.call-start = ((), (), s32[]{:S(2)}) async-start(), calls=%async_computation.6 | async-start | bytes 7077888 | tf_op jit(solution)/shard_map/reduce_scatter | solution.py:137
  306.0 55.9 %copy-start.4 = (f32[256,1536]{1,0:T(8,128)S(1)}, f32[256,1536]{1,0:T(8,128)}, u32[]{:S(2)}) copy-start(f32[256,1536]{1,0:T(8,128)} %copy-done.3) | copy-start | bytes 4718596
  306.0 55.9 %copy-start.31 = (bf16[1536,18]{0,1:T(8,128)(2,1)S(1)}, bf16[1536,18]{0,1:T(8,128)(2,1)}, u32[]{:S(2)}) copy-start(bf16[1536,18]{0,1:T(8,128)(2,1)} %copy-done.30) | copy-start | bytes 165892
  306.0 55.9 %copy-start.44 = (f32[1536]{0:T(1024)S(1)}, f32[1536]{0:T(1024)}, u32[]{:S(2)}) copy-start(f32[1536]{0:T(1024)} %copy-done.43) | copy-start | bytes 18436
  306.0 55.9 %copy-start.54 = (f32[256]{0:T(256)S(1)}, f32[256]{0:T(256)}, u32[]{:S(2)}) copy-start(f32[256]{0:T(256)} %copy-done.53) | copy-start | bytes 3076
  306.0 314.0 %reduce-scatter.11.cloned.1.call-start = ((), (), s32[]{:S(2)}) async-start(), calls=%async_computation.8 | async-start | bytes 12976128 | tf_op jit(solution)/shard_map/reduce_scatter | solution.py:171
  463.7 350.5 %all-reduce.3.cloned.1.call-start = ((), (), s32[]{:S(2)}) async-start(), calls=%async_computation.13 | async-start | bytes 18874368 | tf_op jit(solution)/shard_map/psum | solution.py:142
  465.4 19.7 %slice-start.2 = ((s8[7077888]{0:T(1024)(128)(4,1)}), s8[4194304]{0:T(1024)(128)(4,1)S(1)}, s32[]{:S(2)}) async-start(s8[7077888]{0:T(1024)(128)(4,1)} %bitcast.252), calls=%async_computation.16 | async-start | bytes 8388608
  490.8 354.5 %reduce-scatter.13.cloned.1.call-start = ((), (), s32[]{:S(2)}) async-start(), calls=%async_computation.12 | async-start | bytes 884736
  500.7 379.2 %all-gather.11.cloned.1.call-start = ((), (), s32[]{:S(2)}) async-start(), calls=%async_computation.9 | async-start | bytes 1966080 | tf_op jit(solution)/shard_map/all_gather | solution.py:172
  861.1 22.9 %copy-start.1 = (bf16[2,1536,512]{2,1,0:T(8,128)(2,1)S(1)}, bf16[2,1536,512]{2,1,0:T(8,128)(2,1)}, u32[]{:S(2)}) copy-start(bf16[2,1536,512]{2,1,0:T(8,128)(2,1)} %param.21) | copy-start | bytes 9437188
  (52 other events, 217.2 us)
Sparse Core Ops, SparseCore 0:
  11.5 96.4 all-gather.8
  109.7 63.0 all-gather.14
  174.9 63.8 all-gather.12
  293.7 68.1 reduce-scatter.8
  364.6 68.1 reduce-scatter.6
  463.8 156.1 reduce-scatter.10
  625.0 189.1 all-reduce.2
  817.1 28.0 reduce-scatter.12
  847.1 32.8 all-gather.10

commit v2 on v1

--- a/solution.py
+++ b/solution.py
@@ -1,7 +1,11 @@
+import functools
 import jax
 import jax.numpy as jnp
 from jax import lax
+from jax.experimental import pallas as pl
+from jax.experimental.pallas import tpu as pltpu
 from jax.sharding import PartitionSpec as P
+import numpy as np
 
 MODEL_WIDTH = 1536
 QUERY_HEADS = 24
@@ -17,6 +21,345 @@
 MASKED = -1e30
 F32 = jnp.float32
 BF = jnp.bfloat16
+
+
+def rope_rows(T):
+    half = HEAD_SIZE // 2
+    freq = ROPE_BASE ** (-2.0 * np.arange(half, dtype=np.float64) / HEAD_SIZE)
+    ang = (np.arange(T, dtype=np.float32)[:, None] * freq.astype(np.float32)[None, :]).astype(np.float32)
+    c, s = np.cos(ang), np.sin(ang)
+    return (jnp.asarray(np.concatenate([c, c, c, c], 1), F32), jnp.asarray(np.concatenate([-s, s, -s, s], 1), F32))
+
+
+MESH = pl.DeviceIdType.MESH
+VMEM = pltpu.VMEM
+
+
+def vm():
+    return pl.BlockSpec(memory_space=pltpu.VMEM)
+
+
+def hbm():
+    return pl.BlockSpec(memory_space=pl.ANY)
+
+
+def dot(a, b):
+    return lax.dot_general(a, b, (((1,), (0,)), ((), ())), preferred_element_type=F32)
+
+
+def dot_nt(a, b):
+    return lax.dot_general(a, b, (((1,), (1,)), ((), ())), preferred_element_type=F32)
+
+
+def dot_tn(a, b):
+    return lax.dot_general(a, b, (((0,), (0,)), ((), ())), preferred_element_type=F32)
+
+
+def half_roll(x, first):
+    n = x.shape[1]
+    h = HEAD_SIZE // 2
+    return jnp.where(first, pltpu.roll(x, n - h, axis=1), pltpu.roll(x, h, axis=1))
+
+
+def greet(nf, nd, f, d):
+    barrier = pltpu.get_barrier_semaphore()
+    for i in range(1, nf):
+        pl.semaphore_signal(barrier, inc=1, device_id=(lax.rem(f + i, nf), d), device_id_type=MESH)
+    for i in range(1, nd):
+        pl.semaphore_signal(barrier, inc=1, device_id=(f, jnp.bitwise_xor(d, i)), device_id_type=MESH)
+    pl.semaphore_wait(barrier, nf + nd - 2)
+
+
+def head_masks(kblk, lane):
+    kf = kblk.astype(F32)
+    kr = pltpu.roll(kf, HEAD_SIZE, axis=1)
+    low = lane < HEAD_SIZE
+    zero = jnp.zeros_like(kf)
+    a0 = jnp.where(low, kf, zero).astype(BF)
+    a1 = jnp.where(low, zero, kr).astype(BF)
+    b0 = jnp.where(low, kr, zero).astype(BF)
+    b1 = jnp.where(low, zero, kf).astype(BF)
+    return ((a0, a1), (b0, b1))
+
+
+def front_kernel(nf, nd, experts, tok, pk, small, cot, slots, cosr, sinr,
+                 ffn_o, hid_o, gates_o, mix_o, qk_o, v_o, prob_o, wf_o, cot_o, rt_o,
+                 wf, sm, attn, rot,
+                 s_sm, r_sm, s_z, r_z, s_dp, r_dp, s_sib, r_sib, s_cz, r_cz, s_cs, r_cs, s_loc):
+    T, D = tok.shape
+    C = nf // 2
+    R = pk.shape[0]
+    W = pk.shape[1]
+    Wq = W // nd
+    f = lax.axis_index("fsdp")
+    d = lax.axis_index("dp")
+    c = f // 2
+    k = lax.rem(f, 2)
+    sib = f + 1 - 2 * k
+    greet(nf, nd, f, d)
+
+    def rows(ff):
+        return pl.ds(pl.multiple_of(ff * R, 16), R)
+
+    def cols(dd):
+        return pl.ds(pl.multiple_of(dd * Wq, 128), Wq)
+
+    def remote(src, dst, ss, rs, to_f, to_d):
+        return pltpu.make_async_remote_copy(src_ref=src, dst_ref=dst, send_sem=ss, recv_sem=rs,
+                                            device_id=(to_f, to_d), device_id_type=MESH)
+
+    def src_chip(dr, s):
+        return c - s if dr == 0 else c + s
+
+    def has(dr, s):
+        return (c - s >= 0) if dr == 0 else (c + s < C)
+
+    def nxt_ok(dr):
+        return (c + 1 < C) if dr == 0 else (c - 1 >= 0)
+
+    def nxt_f(dr):
+        return f + 2 if dr == 0 else f - 2
+
+    def wz(dr, s, own):
+        ff = 2 * src_chip(dr, s - 1) + k
+        dst = wf.at[rows(ff), cols(d)]
+        src = pk.at[:, cols(d)] if own else dst
+        return remote(src, dst, s_z.at[dr, s - 1], r_z.at[dr, s - 1], nxt_f(dr), d)
+
+    def wz_in(dr, s):
+        ff = 2 * src_chip(dr, s) + k
+        blk = wf.at[rows(ff), cols(d)]
+        return remote(blk, blk, s_z.at[dr, s - 1], r_z.at[dr, s - 1], f, d)
+
+    own_small = pltpu.make_async_copy(small, sm.at[f], s_loc.at[0])
+    own_small.start()
+    sm_copies = []
+    for i in range(1, nf):
+        cp = remote(small, sm.at[f], s_sm.at[i - 1], r_sm.at[i - 1], lax.rem(f + i, nf), d)
+        cp.start()
+        sm_copies.append(cp)
+    for dr in range(2):
+        @pl.when(nxt_ok(dr))
+        def _():
+            wz(dr, 1, True).start()
+    sib_own = remote(pk, wf.at[rows(f)], s_sib.at[0, 0], r_sib.at[0, 0], sib, d)
+    sib_own.start()
+    own_w = pltpu.make_async_copy(pk, wf.at[rows(f)], s_loc.at[1])
+    own_w.start()
+    own_c = pltpu.make_async_copy(cot, cot_o.at[f], s_loc.at[2])
+    own_c.start()
+    sib_c = remote(cot, cot_o.at[f], s_cs.at[0, 0], r_cs.at[0, 0], sib, d)
+
+    def dp_copy(dr, s, i):
+        ff = 2 * src_chip(dr, s) + k
+        blk = wf.at[rows(ff), cols(d)]
+        return remote(blk, blk, s_dp.at[dr, s - 1, i - 1], r_dp.at[dr, s - 1, i - 1], f, jnp.bitwise_xor(d, i))
+
+    def dp_in(dr, s, i):
+        ff = 2 * src_chip(dr, s) + k
+        blk = wf.at[rows(ff), cols(jnp.bitwise_xor(d, i))]
+        return remote(blk, blk, s_dp.at[dr, s - 1, i - 1], r_dp.at[dr, s - 1, i - 1], f, d)
+
+    def sib_copy(dr, s):
+        blk = wf.at[rows(2 * src_chip(dr, s) + k)]
+        return remote(blk, blk, s_sib.at[dr, s], r_sib.at[dr, s], sib, d)
+
+    def sib_in(dr, s):
+        blk = wf.at[rows(2 * src_chip(dr, s) + 1 - k)]
+        return remote(blk, blk, s_sib.at[dr, s], r_sib.at[dr, s], sib, d)
+
+    def cz(dr, s, own):
+        ff = 2 * src_chip(dr, s - 1) + k
+        src = cot if own else cot_o.at[ff]
+        return remote(src, cot_o.at[ff], s_cz.at[dr, s - 1], r_cz.at[dr, s - 1], nxt_f(dr), d)
+
+    def cz_in(dr, s):
+        ff = 2 * src_chip(dr, s) + k
+        return remote(cot_o.at[ff], cot_o.at[ff], s_cz.at[dr, s - 1], r_cz.at[dr, s - 1], f, d)
+
+    def cs(dr, s):
+        ff = 2 * src_chip(dr, s) + k
+        return remote(cot_o.at[ff], cot_o.at[ff], s_cs.at[dr, s], r_cs.at[dr, s], sib, d)
+
+    def cs_in(dr, s):
+        ff = 2 * src_chip(dr, s) + 1 - k
+        return remote(cot_o.at[ff], cot_o.at[ff], s_cs.at[dr, s], r_cs.at[dr, s], sib, d)
+
+    for s in range(1, C):
+        for dr in range(2):
+            @pl.when(has(dr, s))
+            def _():
+                wz_in(dr, s).wait_recv()
+                if s < C - 1:
+                    @pl.when(nxt_ok(dr))
+                    def _():
+                        wz(dr, s + 1, False).start()
+                for i in range(1, nd):
+                    dp_copy(dr, s, i).start()
+    for dr in range(2):
+        @pl.when(nxt_ok(dr))
+        def _():
+            cz(dr, 1, True).start()
+    sib_c.start()
+
+    own_small.wait()
+    for cp in sm_copies:
+        cp.wait()
+    Ds = small.shape[1]
+    rt = jnp.concatenate([sm[i] for i in range(nf)], axis=1)
+    rt_o[...] = rt
+    gains = rt[experts:experts + 2].astype(F32)
+    gain_one, gain_two = gains[0:1], gains[1:2]
+    xf = tok[...].astype(F32)
+    r1 = lax.rsqrt(jnp.mean(xf * xf, -1, keepdims=True) + EPSILON)
+    attn[...] = (xf * r1 * gain_one).astype(BF)
+
+    for s in range(1, C):
+        for dr in range(2):
+            @pl.when(has(dr, s))
+            def _():
+                for i in range(1, nd):
+                    dp_in(dr, s, i).wait_recv()
+                sib_copy(dr, s).start()
+        for dr in range(2):
+            if s < C - 1:
+                pass
+
+    def cot_step(s):
+        for dr in range(2):
+            @pl.when(has(dr, s))
+            def _():
+                cz_in(dr, s).wait_recv()
+                if s < C - 1:
+                    @pl.when(nxt_ok(dr))
+                    def _():
+                        cz(dr, s + 1, False).start()
+                cs(dr, s).start()
+
+    cot_step(1)
+    sib_own.wait()
+    own_w.wait()
+    for s in range(1, C):
+        for dr in range(2):
+            @pl.when(has(dr, s))
+            def _():
+                sib_in(dr, s).wait_recv()
+    out_w = pltpu.make_async_copy(wf, wf_o, s_loc.at[3])
+    out_w.start()
+
+    first = lax.rem(lax.broadcasted_iota(jnp.int32, (T, 256), 1), HEAD_SIZE) < HEAD_SIZE // 2
+    cs_t = jnp.concatenate([cosr[...], cosr[...]], 1)
+    sn_t = jnp.concatenate([sinr[...], sinr[...]], 1)
+    nqk = (QW + KW) // 256
+
+    @pl.loop(0, nqk)
+    def _(i):
+        col = pl.ds(pl.multiple_of(i * 256, 256), 256)
+        x = dot(attn[...], wf[:, col])
+        qk_o[:, col] = (x * cs_t + half_roll(x, first) * sn_t).astype(BF)
+
+    @pl.loop(0, KW // 256)
+    def _(i):
+        col = pl.ds(pl.multiple_of(QW + KW + i * 256, 256), 256)
+        v_o[:, pl.ds(pl.multiple_of(i * 256, 256), 256)] = dot(attn[...], wf[:, col]).astype(BF)
+
+    for s in range(2, min(C, 3)):
+        cot_step(s)
+
+    factor = HEAD_SIZE ** (-0.5)
+    lane = lax.broadcasted_iota(jnp.int32, (T, 128), 1)
+    keep = lax.broadcasted_iota(jnp.int32, (T, T), 1) <= lax.broadcasted_iota(jnp.int32, (T, T), 0)
+
+    @pl.loop(0, KEY_VALUE_HEADS // 2)
+    def _(i):
+        kc = pl.ds(pl.multiple_of(QW + i * 128, 128), 128)
+        kh = head_masks(qk_o[:, kc], lane)
+        vh = head_masks(v_o[:, pl.ds(pl.multiple_of(i * 128, 128), 128)], lane)
+        for p in range(GROUP):
+            qc = pl.ds(pl.multiple_of((i * GROUP + p) * 128, 128), 128)
+            q = qk_o[:, qc]
+            acc = None
+            for half in range(2):
+                g = (2 * p + half) // GROUP
+                sc = dot_nt(q, kh[g][half]) * factor
+                sc = jnp.where(keep, sc, MASKED)
+                ex = jnp.exp(sc - jnp.max(sc, -1, keepdims=True))
+                pr = (ex / jnp.sum(ex, -1, keepdims=True)).astype(BF)
+                prob_o[i * 2 * GROUP + 2 * p + half] = pr
+                term = dot(pr, vh[g][half])
+                acc = term if acc is None else acc + term
+            mix_o[:, qc] = acc.astype(BF)
+
+    for s in range(3, C):
+        cot_step(s)
+
+    @pl.loop(0, D // 256)
+    def _(i):
+        col = pl.ds(pl.multiple_of(i * 256, 256), 256)
+        wc = pl.ds(pl.multiple_of(QW + 2 * KW + i * 256, 256), 256)
+        hid_o[:, col] = tok[:, col].astype(F32) + dot(mix_o[...], wf[:, wc])
+
+    hidden = hid_o[...]
+    r2 = lax.rsqrt(jnp.mean(hidden * hidden, -1, keepdims=True) + EPSILON)
+    ffn_o[...] = (hidden * r2 * gain_two).astype(BF)
+    logits = dot_nt(rt_o[...], ffn_o[...])[0:experts]
+    named = slots[...] >= 0.0
+    logits = jnp.where(named, logits, MASKED)
+    ex = jnp.where(named, jnp.exp(logits - jnp.max(logits, 0, keepdims=True)), 0.0)
+    gates_o[...] = ex / jnp.sum(ex, 0, keepdims=True)
+
+    own_c.wait()
+    sib_c.wait()
+    out_w.wait()
+    for dr in range(2):
+        for s in range(1, C):
+            @pl.when(has(dr, s))
+            def _():
+                cs_in(dr, s).wait_recv()
+                cs(dr, s).wait_send()
+                sib_copy(dr, s).wait_send()
+                for i in range(1, nd):
+                    dp_copy(dr, s, i).wait_send()
+
+            @pl.when(nxt_ok(dr) & (has(dr, s - 1) if s > 1 else True))
+            def _():
+                wz(dr, s, s == 1).wait_send()
+                cz(dr, s, s == 1).wait_send()
+
+
+def front(nf, nd, experts, tok, pk, small, cot, slots, cosr, sinr):
+    T, D = tok.shape
+    C = nf // 2
+    W = pk.shape[1]
+    out = [
+        (T, D, BF, 0), (T, D, F32, 0), (experts, T, F32, 0), (T, QW, BF, 0), (T, QW + KW, BF, 0),
+        (T, KW, BF, 0), (QUERY_HEADS, T, T, BF, 0), (D, W, BF, 1), (nf, T, D, BF, 1),
+        (small.shape[0], D, BF, 0),
+    ]
+    dma = pltpu.SemaphoreType.DMA
+    return pl.pallas_call(
+        functools.partial(front_kernel, nf, nd, experts),
+        out_shape=[jax.ShapeDtypeStruct(o[:-2], o[-2]) for o in out],
+        in_specs=[vm()] * 7,
+        out_specs=[hbm() if o[-1] else vm() for o in out],
+        scratch_shapes=[
+            VMEM((D, W), BF),
+            VMEM((nf,) + small.shape, BF),
+            VMEM((T, D), BF),
+            VMEM((8, 128), F32),
+            dma((nf,)), dma((nf,)),
+            dma((2, C)), dma((2, C)),
+            dma((2, C, nd)), dma((2, C, nd)),
+            dma((2, C)), dma((2, C)),
+            dma((2, C)), dma((2, C)),
+            dma((2, C)), dma((2, C)),
+            dma((4,)),
+        ],
+        compiler_params=pltpu.CompilerParams(collective_id=1, has_side_effects=True,
+                                             vmem_limit_bytes=60 * 2 ** 20),
+        cost_estimate=pl.CostEstimate(flops=4_000_000_000, bytes_accessed=60_000_000, transcendentals=2_000_000),
+        name="front",
+    )(tok, pk, small, cot, slots, cosr, sinr)
 
 
 def rope_tables(sequence_length):
@@ -59,51 +402,34 @@
     fs = lax.axis_index("fsdp")
 
     packed = jnp.concatenate([w_query, key_weight, value_weight, w_out], 1)
-    rows = packed.shape[0] // nd
-    mine = lax.dynamic_slice_in_dim(packed, dp * rows, rows, 0)
-    full = lax.all_gather(mine, ("fsdp", "dp"), axis=0, tiled=True)
-    qkv_full = full[:, : QW + 2 * KW]
-    out_full = full[:, QW + 2 * KW:]
-    small = jnp.concatenate([w_router, gain_attn[:, None], gain_ffn[:, None]], 1)
-    small_full = lax.all_gather(small, "fsdp", axis=0, tiled=True)
-    router_full = small_full[:, :experts]
-    gain_one = small_full[:, experts].astype(F32)
-    gain_two = small_full[:, experts + 1].astype(F32)
-
+    pad = -(experts + 2) % 16
+    small = jnp.concatenate([w_router, gain_attn[:, None], gain_ffn[:, None],
+                             jnp.zeros((w_router.shape[0], pad), BF)], 1).T
     onehot = (routes[:, :, None] == jnp.arange(experts, dtype=jnp.int32)).any(1)
     before = jnp.cumsum(onehot.astype(jnp.int32), 0) - onehot.astype(jnp.int32)
     slots = jnp.where(onehot, before, -1).astype(F32)
-
-    cot_all = lax.all_gather(cotangent, "fsdp", axis=0)
-
+    cosr, sinr = rope_rows(T)
+    ffn_in, hidden, gates_t, mixed, qk, v2, probs_low, full, cot_all, rt = front(
+        nf, nd, experts, tokens, packed, small, cotangent, slots.T, cosr, sinr)
+    gates = gates_t.T
+    qkv_full = full[:, : QW + 2 * KW]
+    out_full = full[:, QW + 2 * KW:]
+    router_full = rt[:experts].T
+    gain_one = rt[experts].astype(F32)
+    gain_two = rt[experts + 1].astype(F32)
     xf = tokens.astype(F32)
     r1 = rms_scale(xf)
     n1 = xf * r1
     attn_in = (n1 * gain_one).astype(BF)
-    proj = jnp.dot(attn_in, qkv_full, preferred_element_type=F32)
     c, s = rope_tables(T)
-    q = rotate(proj[:, :QW].reshape(T, QUERY_HEADS, HEAD_SIZE), c, s).astype(BF)
-    q = q.reshape(T, KEY_VALUE_HEADS, GROUP, HEAD_SIZE)
-    k = rotate(proj[:, QW: QW + KW].reshape(T, KEY_VALUE_HEADS, HEAD_SIZE), c, s).astype(BF)
-    v = proj[:, QW + KW:].astype(BF).reshape(T, KEY_VALUE_HEADS, HEAD_SIZE)
+    q = qk[:, :QW].reshape(T, KEY_VALUE_HEADS, GROUP, HEAD_SIZE)
+    k = qk[:, QW:].reshape(T, KEY_VALUE_HEADS, HEAD_SIZE)
+    v = v2.reshape(T, KEY_VALUE_HEADS, HEAD_SIZE)
     factor = HEAD_SIZE ** (-0.5)
-    scores = mm("qgrd,kgd->grqk", q, k) * factor
-    keep = jnp.arange(T)[None, :] <= jnp.arange(T)[:, None]
-    scores = jnp.where(keep, scores, MASKED)
-    top = jnp.max(scores, -1, keepdims=True)
-    ex = jnp.exp(scores - top)
-    probs = ex / jnp.sum(ex, -1, keepdims=True)
-    probs_low = probs.astype(BF)
-    mixed = mm("grqk,kgd->qgrd", probs_low, v).reshape(T, QW).astype(BF)
-    hidden = xf + jnp.dot(mixed, out_full, preferred_element_type=F32)
+    probs_low = probs_low.reshape(KEY_VALUE_HEADS, GROUP, T, T)
+    probs = probs_low.astype(F32)
     r2 = rms_scale(hidden)
     n2 = hidden * r2
-    ffn_in = (n2 * gain_two).astype(BF)
-    logits = jnp.dot(ffn_in, router_full, preferred_element_type=F32)
-    gates = jnp.where(onehot, logits, MASKED)
-    gates = jnp.exp(gates - jnp.max(gates, -1, keepdims=True))
-    gates = jnp.where(onehot, gates, 0.0)
-    gates = gates / jnp.sum(gates, -1, keepdims=True)
 
     ffn_all = lax.all_gather(ffn_in, "fsdp", axis=0)
     side = lax.all_gather(jnp.stack([slots.T, gates.T]), "fsdp", axis=0)

time: 900 us -> 862 us (0.958)
  Pallas kernels: 0 us -> 109 us
  waiting for transfers between devices: 599 us -> 494 us
  blocking collectives: 63.1 us -> 32.3 us
  matrix products: 140 us -> 125 us
    pallas_call x0 -> x1, Pallas kernels: none -> 109 us  [front(): pl.pallas_call(functools.partial(front_kernel, nf, nd, experts), out_shap...]
    all_gather x2 -> x0, waiting for transfers between devices: 80.6 us -> none  [the longest x1 80.6 us: body(): full = lax.all_gather(mine, ('fsdp', 'dp'), axis=0, tiled=True)]
    all_gather x1, waiting for transfers between devices: 56.6 us -> 40.2 us  [body(): ffn_all = lax.all_gather(ffn_in, 'fsdp', axis=0)]
    all_gather x1 -> x0, blocking collectives: 14.2 us -> none  [body(): small_full = lax.all_gather(small, 'fsdp', axis=0, tiled=True)]
    dot_general x3 -> x0, matrix products: 11.4 us -> none  [the longest x1 5.76 us: body(): proj = jnp.dot(attn_in, qkv_full, preferred_element_type=F32)]
    all_to_all x1 -> x0, blocking collectives: 9.58 us -> none  [body(): gp_all = lax.all_to_all(gp_part, 'fsdp', split_axis=0, concat_axis=0)]
    dot_general x16 -> x15, matrix products: 103 us -> 106 us  [mm(): return jnp.einsum(spec, a, b, preferred_element_type=F32)]
  transfers between devices with their start and end apart: 9 -> 8, of which waited for: 8 -> 7; matrix products, arithmetic and copies ran while one was open for 13% -> 10% of each run, Pallas kernels for 0% -> 0%
where the time goes in v2:
time: 862 us; the launch traced here: 853 us
  waiting for transfers between devices  494 us (57%)
  matrix products  125 us (15%)
  Pallas kernels  109 us (13%)
  other arithmetic  43.4 us (5%)
  blocking collectives  32.3 us (4%)
  local copies, waits for them, and re-layouts  29 us (3%)
  between operations  14.7 us (2%)
    psum x1, waiting for transfers between devices, body(): terms = lax.psum(terms, 'dp')  194 us
    reduce_scatter x1, waiting for transfers between devices, body(): big = lax.psum_scatter(big, ('fsdp', 'dp'), scatter_dimension=0, tiled=True)  119 us
    pallas_call x1, Pallas kernels, front(): pl.pallas_call(functools.partial(front_kernel, nf, nd, experts), out_shap...  109 us
    dot_general x15, matrix products, mm(): return jnp.einsum(spec, a, b, preferred_element_type=F32)  106 us
    reduce_scatter x1, waiting for transfers between devices, body(): lax.psum_scatter(out_part, 'fsdp', scatter_dimension=0, tiled=False)  67.7 us
    all_gather x1, waiting for transfers between devices, body(): ffn_all = lax.all_gather(ffn_in, 'fsdp', axis=0)  40.2 us
    reduce_scatter x1, waiting for transfers between devices, body(): lax.psum_scatter(gin_part, 'fsdp', scatter_dimension=0, tiled=False)  37.6 us
    all_gather x1, waiting for transfers between devices, body(): big = lax.all_gather(big, 'dp', axis=0, tiled=True).astype(F32)  18.3 us
  transfers between devices with their start and end apart: 8, of which 7 were waited for; matrix products, arithmetic and copies ran while one was open for 10% of the time, Pallas kernels for 0%

profile of v2, /device:TPU:10, one launch (start us, length us, event | category | flops | bytes accessed | tf_op | source)
XLA Modules:
  0.0 852.9 jit_solution(67936997115147620)
XLA Ops:
  14.5 108.9 %front.1 = (bf16[256,1536]{1,0:T(8,128)(2,1)}, f32[256,1536]{1,0:T(8,128)}, f32[16,256]{1,0:T(8,128)}, bf16[256,1536]{1,0:T(8,128)(2,1)}, bf16[256,2048]{1,0:T(8...) custom-call(bf16[256,1536]{1,0:T(8,128)(2,1)} %tok.1, ...), custom_call_target="tpu_custom_call" | custom-call | flops 4000000000 | bytes 60000000 | tf_op jit(solution)/shard_map/front/pallas_call | solution.py:340
  124.3 18.0 %all-gather = f32[16,16,256]{2,1,0:T(8,128)S(1)} all-gather(f32[2,16,256]{2,1,0:T(8,128)S(1)} %pad_maximum_fusion.8), channel_id=2, replica_groups=mesh['fsdp'=8,'dp'=4] {'fsdp'}, dimensions={0}, use_global_device_ids=true | all-gather | bytes 294912 | tf_op jit(solution)/shard_map/all_gather | solution.py:435
  142.3 7.7 fusion.22
  150.0 40.2 %all-gather.7.cloned.1.call-done = bf16[2048,1536]{1,0:T(8,128)(2,1)} async-done(((bf16[256,1536]{1,0:T(8,128)(2,1)}), bf16[2048,1536]{1,0:T(8,128)(2,1)}) %all-gather.7.cloned.1.call-update) | async-done | bytes 6291472 | tf_op jit(solution)/shard_map/all_gather | solution.py:434
  195.2 16.3 %fusion.16 = f32[2,8,144,512]{3,2,1,0:T(8,128)} fusion(bf16[8,2,144,1536]{3,2,1,0:T(8,128)(2,1)S(1)} %convolution_convert_fusion.2, bf16[2,1536,512]{2,1,0:T(8,128)(2,1)S(1)} %copy-done.2), kind=kOutput, calls=%fused_computation.27 | convolution fusion | flops 3623878656 | bytes 14942208 | tf_op jit(solution)/shard_map/necd,edf->necf/dot_general | solution.py:390
  217.0 9.6 %fusion.29 = (f32[8,2,144]{2,0,1:T(8,128)S(1)}, f32[2,8,144,512]{3,2,1,0:T(8,128)}) fusion(f32[2,8,144,512]{3,2,1,0:T(8,128)} %fusion.16, f32[2,8,144,512]{3,2,1,0:T(8,128)} %fusion.18, bf16[2,512,1536]{2,1,0:T(8,128)(2,1)} %param.25, bf16[8,2,144,1536]{3,2,1,0:T(8,128)(2,1)S(1)} %bitcast.214), kind=kOutput, calls=%fused_computation.36 | convolution fusion | flops 3634493184 | bytes 24388608 | tf_op jit(solution)/shard_map/necd,efd->necf/dot_general | solution.py:390
  227.7 7.8 multiply_convert_fusion
  235.5 7.0 fusion.48
  242.5 13.2 %bitcast_convert_fusion = bf16[8,256,1536]{2,1,0:T(8,128)(2,1)} fusion(f32[2,8,144,1536]{3,2,0,1:T(8,128)} %fusion.48, bf16[2,1536,512]{2,1,0:T(8,128)(2,1)} %param.24, bf16[8,2,144,512]{3,2,0,1:T(8,128)(2,1)} %get-tuple-element.43, f32[8,2,256]{2,1,0:T(2,128)S(1)} %get-tuple-element.57), kind=kOutput, calls=%fused_computation.2 | convolution fusion | flops 5446631424 | bytes 25968640 | tf_op jit(solution)/shard_map/nect,necd->ntd/dot_general | solution.py:390
  257.4 10.4 %bitcast_convert_fusion.1 = bf16[8,256,1536]{2,1,0:T(8,128)(2,1)} fusion(f32[8,2,256]{2,1,0:T(2,128)S(1)} %get-tuple-element.57, bf16[2,512,1536]{2,1,0:T(8,128)(2,1)} %param.25, bf16[8,2,144,512]{3,2,0,1:T(8,128)(2,1)S(1)} %copy-done.22), kind=kOutput, calls=%fused_computation.3 | convolution fusion | flops 5443092480 | bytes 11812864 | tf_op jit(solution)/shard_map/nect,necd->ntd/dot_general | solution.py:390
  269.9 5.6 all-to-all-start
  286.1 37.6 %reduce-scatter.9.cloned.1.call-done = bf16[1,256,1536]{2,1,0:T(8,128)(2,1)} async-done(((bf16[8,256,1536]{2,1,0:T(8,128)(2,1)}), bf16[1,256,1536]{2,1,0:T(8,128)(2,1)}) %reduce-scatter.9.cloned.1.call-update) | async-done | bytes 786448 | tf_op jit(solution)/shard_map/reduce_scatter | solution.py:462
  327.0 67.7 %reduce-scatter.7.cloned.1.call-done = bf16[1,256,1536]{2,1,0:T(8,128)(2,1)} async-done(((bf16[8,256,1536]{2,1,0:T(8,128)(2,1)}), bf16[1,256,1536]{2,1,0:T(8,128)(2,1)}) %reduce-scatter.7.cloned.1.call-update) | async-done | bytes 786448 | tf_op jit(solution)/shard_map/reduce_scatter | solution.py:463
  420.3 5.5 pad_maximum_fusion
  427.5 9.0 %bitcast_convert_fusion.2 = bf16[2,512,1536]{2,1,0:T(8,128)(2,1)} fusion(bf16[8,2,144,512]{3,2,0,1:T(8,128)(2,1)S(1)} %copy-done.23, bf16[8,2,144,1536]{3,2,1,0:T(8,128)(2,1)} %fusion.22), kind=kOutput, calls=%fused_computation.19 | convolution fusion | flops 3625451520 | bytes 12582912 | tf_op jit(solution)/shard_map/necf,necd->efd/dot_general | solution.py:390
  436.5 10.7 %bitcast_convert_fusion.4 = bf16[2,1536,512]{2,1,0:T(8,128)(2,1)} fusion(bf16[8,2,144,1536]{3,2,1,0:T(8,128)(2,1)} %copy-done.12, bf16[8,2,144,512]{3,2,0,1:T(8,128)(2,1)S(1)} %copy-done.21), kind=kOutput, calls=%fused_computation.21 | convolution fusion | flops 3625451520 | bytes 12582912 | tf_op jit(solution)/shard_map/necd,necf->edf/dot_general | solution.py:390
  447.2 5.7 bitcast_convert_fusion.3
  454.4 7.3 fusion.69
  462.9 119.2 %reduce-scatter.11.cloned.1.call-done = bf16[48,4096]{1,0:T(8,128)(2,1)} async-done(((bf16[1536,4096]{1,0:T(8,128)(2,1)}), bf16[48,4096]{1,0:T(8,128)(2,1)}) %reduce-scatter.11.cloned.1.call-update) | async-done | bytes 393232 | tf_op jit(solution)/shard_map/reduce_scatter | solution.py:497
  582.2 194.1 %all-reduce.3.cloned.1.call-done = (bf16[2,1536,512]{2,1,0:T(8,128)(2,1)}, bf16[2,1536,512]{2,1,0:T(8,128)(2,1)}, bf16[2,512,1536]{2,1,0:T(8,128)(2,1)}) async-done(((bf16[2,1536,512]{2,1,0:T(8,128)(2,1)}, bf16[2,1536,512]{2,1,0:T(8,128)(2,1)}, bf16[2,512,1536]{2,1,0:T(8,128)(2,1)}), (bf16[2,1536,512]{2,1,0:T(8,128)(2,1)}, bf16[2,1536,512]{2,1,0:T(8,128)(2,1)}, ...) | async-done | bytes 9437200 | tf_op jit(solution)/shard_map/psum | solution.py:468
  776.2 5.6 convert_element_type.157
  790.4 16.7 %reduce-scatter.13.cloned.1.call-done = f32[192,18]{1,0:T(8,128)} async-done(((f32[1536,18]{1,0:T(8,128)}), f32[192,18]{1,0:T(8,128)}) %reduce-scatter.13.cloned.1.call-update) | async-done | bytes 13840
  808.1 14.3 %psum.28 = f32[192,18]{0,1:T(8,128)S(1)} all-reduce(f32[192,18]{0,1:T(8,128)S(1)} %copy.121), channel_id=1, replica_groups=mesh['fsdp'=8,'dp'=4] {'dp'}, use_global_device_ids=true, to_apply=%region_18.19 | all-reduce | flops 3456 | bytes 27648 | tf_op jit(solution)/shard_map/psum | solution.py:501
  823.5 18.3 %all-gather.5.cloned.1.call-done = bf16[192,4096]{1,0:T(8,128)(2,1)} async-done(((bf16[48,4096]{1,0:T(8,128)(2,1)}), bf16[192,4096]{1,0:T(8,128)(2,1)}) %all-gather.5.cloned.1.call-update) | async-done | bytes 1572880 | tf_op jit(solution)/shard_map/all_gather | solution.py:498
  (157 shorter events, 81.9 us)
Async XLA Ops:
  7.2 204.3 %copy-start = (bf16[2,1536,512]{2,1,0:T(8,128)(2,1)S(1)}, bf16[2,1536,512]{2,1,0:T(8,128)(2,1)}, u32[]{:S(2)}) copy-start(bf16[2,1536,512]{2,1,0:T(8,128)(2,1)} %param.23) | copy-start | bytes 9437188
  7.2 6.6 copy-start.32
  7.2 183.0 %all-gather.7.cloned.1.call-start = ((), (), s32[]{:S(2)}) async-start(), calls=%async_computation.9 | async-start | bytes 7077888 | tf_op jit(solution)/shard_map/all_gather | solution.py:434
  14.5 109.0 %copy-start.31 = (f32[16,256]{1,0:T(8,128)S(1)}, f32[16,256]{1,0:T(8,128)}, u32[]{:S(2)}) copy-start(f32[16,256]{1,0:T(8,128)} %fusion.96.slots) | copy-start | bytes 49156
  123.5 200.2 %reduce-scatter.9.cloned.1.call-start = ((), (), s32[]{:S(2)}) async-start(), calls=%async_computation.6 | async-start | bytes 7077888 | tf_op jit(solution)/shard_map/reduce_scatter | solution.py:462
  190.2 4.9 copy-start.2
  195.2 16.3 %copy-start.12 = (bf16[8,2,144,1536]{3,2,1,0:T(8,128)(2,1)}, bf16[8,2,144,1536]{3,2,1,0:T(8,128)(2,1)S(1)}, u32[]{:S(2)}) copy-start(bf16[8,2,144,1536]{3,2,1,0:T(8,128)(2,1)S(1)} %convolution_convert_fusion.2) | copy-start | bytes 21233668
  195.2 21.8 %slice-start = ((s8[7077888]{0:T(1024)(128)(4,1)}), s8[4194304]{0:T(1024)(128)(4,1)S(1)}, s32[]{:S(2)}) async-start(s8[7077888]{0:T(1024)(128)(4,1)} %bitcast.213), calls=%async_computation.12 | async-start | bytes 8388608
  211.5 5.5 slice-start.1
  235.5 7.0 copy-start.20
  255.7 139.0 %reduce-scatter.7.cloned.1.call-start = ((), (), s32[]{:S(2)}) async-start(), calls=%async_computation.5 | async-start | bytes 7077888 | tf_op jit(solution)/shard_map/reduce_scatter | solution.py:463
  269.9 16.1 %all-to-all-start = ((f32[8,2,256]{2,1,0:T(2,128)}), f32[8,2,256]{2,1,0:T(2,128)S(1)}, u32[]{:S(2)}, u32[]{:S(2)}) async-start(f32[8,2,256]{2,1,0:T(2,128)} %get-tuple-element.38), calls=%async_computation.2 | async-start | bytes 32768 | tf_op jit(solution)/shard_map/all_to_all | solution.py:460
  275.4 306.7 %reduce-scatter.11.cloned.1.call-start = ((), (), s32[]{:S(2)}) async-start(), calls=%async_computation.7 | async-start | bytes 12976128 | tf_op jit(solution)/shard_map/reduce_scatter | solution.py:497
  279.6 6.4 copy-start.30
  283.2 126.2 %copy-start.3 = (bf16[8,3,256,256]{2,3,1,0:T(8,128)(2,1)}, bf16[8,3,256,256]{2,3,1,0:T(8,128)(2,1)S(1)}, u32[]{:S(2)}) copy-start(bf16[8,3,256,256]{2,3,1,0:T(8,128)(2,1)S(1)} %copy.95) | copy-start | bytes 9437188
  425.9 350.4 %all-reduce.3.cloned.1.call-start = ((), (), s32[]{:S(2)}) async-start(), calls=%async_computation.11 | async-start | bytes 18874368 | tf_op jit(solution)/shard_map/psum | solution.py:468
  427.5 9.0 %copy-start.21 = (bf16[8,2,144,512]{3,2,0,1:T(8,128)(2,1)S(1)}, bf16[8,2,144,512]{3,2,0,1:T(8,128)(2,1)}, u32[]{:S(2)}) copy-start(bf16[8,2,144,512]{3,2,0,1:T(8,128)(2,1)} %copy-done.20) | copy-start | bytes 7077892
  427.5 19.7 %slice-start.2 = ((s8[7077888]{0:T(1024)(128)(4,1)}), s8[4194304]{0:T(1024)(128)(4,1)S(1)}, s32[]{:S(2)}) async-start(s8[7077888]{0:T(1024)(128)(4,1)} %bitcast.215), calls=%async_computation.14 | async-start | bytes 8388608
  436.5 10.7 %copy-start.8 = (bf16[8,2,144,512]{3,2,0,1:T(8,128)(2,1)S(1)}, bf16[8,2,144,512]{3,2,0,1:T(8,128)(2,1)}, u32[]{:S(2)}) copy-start(bf16[8,2,144,512]{3,2,0,1:T(8,128)(2,1)} %get-tuple-element.43) | copy-start | bytes 7077892
  436.5 10.7 %slice-start.3 = ((s8[7077888]{0:T(1024)(128)(4,1)}), s8[2883584]{0:T(1024)(128)(4,1)S(1)}, s32[]{:S(2)}) async-start(s8[7077888]{0:T(1024)(128)(4,1)} %bitcast.215), calls=%async_computation.15 | async-start | bytes 5767168
  452.9 354.2 %reduce-scatter.13.cloned.1.call-start = ((), (), s32[]{:S(2)}) async-start(), calls=%async_computation.10 | async-start | bytes 884736
  462.9 378.9 %all-gather.5.cloned.1.call-start = ((), (), s32[]{:S(2)}) async-start(), calls=%async_computation.8 | async-start | bytes 1966080 | tf_op jit(solution)/shard_map/all_gather | solution.py:498
  776.2 5.6 copy-start.18
  822.9 22.9 %copy-start.1 = (bf16[2,1536,512]{2,1,0:T(8,128)(2,1)S(1)}, bf16[2,1536,512]{2,1,0:T(8,128)(2,1)}, u32[]{:S(2)}) copy-start(bf16[2,1536,512]{2,1,0:T(8,128)(2,1)} %param.23) | copy-start | bytes 9437188
  (21 other events, 45.0 us)
Sparse Core Ops, SparseCore 0:
  123.6 66.5 all-gather.6
  255.9 67.7 reduce-scatter.8
  326.5 68.1 reduce-scatter.6
  426.0 156.1 reduce-scatter.10
  586.9 189.2 all-reduce.2
  779.0 28.0 reduce-scatter.12
  808.9 32.8 all-gather.4

commit v3 on v2

--- a/solution.py
+++ b/solution.py
@@ -362,143 +362,900 @@
     )(tok, pk, small, cot, slots, cosr, sinr)
 
 
-def rope_tables(sequence_length):
-    half_size = HEAD_SIZE // 2
-    positions = jnp.arange(sequence_length, dtype=F32)
-    frequency = ROPE_BASE ** (-2.0 * jnp.arange(half_size, dtype=F32) / HEAD_SIZE)
-    angles = positions[:, None] * frequency[None, :]
-    return (jnp.cos(angles)[:, None, :], jnp.sin(angles)[:, None, :])
-
-
-def rotate(values, c, s):
-    h = values.shape[-1] // 2
-    a, b = values[..., :h], values[..., h:]
-    return jnp.concatenate([a * c - b * s, a * s + b * c], -1)
-
-
-def rms_scale(values):
-    return lax.rsqrt(jnp.mean(values * values, -1, keepdims=True) + EPSILON)
-
-
-def norm_back(grad_normed, normed, inv_rms, gain_vec):
-    scaled = grad_normed * gain_vec
-    grad_input = inv_rms * (scaled - normed * jnp.mean(scaled * normed, -1, keepdims=True))
-    return (grad_input, jnp.sum(grad_normed * normed, 0))
-
-
-def mm(spec, a, b):
-    return jnp.einsum(spec, a, b, preferred_element_type=F32)
+def visit(c, C, j):
+    both = jnp.minimum(c, C - 1 - c)
+    near = j <= 2 * both
+    dist = jnp.where(near, (j + 1) // 2, j - both)
+    down = jnp.where(near, lax.rem(j, 2) == 0, c < C - 1 - c)
+    chip = jnp.where(down, c + dist, c - dist)
+    return chip, jnp.where(down, 1, 0), dist
+
+
+def experts_kernel(nf, el, cap, capp, ffn, cot_a, side, wg_h, wu_h, wd_h,
+                   out_o, gin_o, gp_o, t1_o, t2_o,
+                   wg, wu, wd, fa, sd, cotb, xs, gs, hs, hgs, orb, irb, st_o, st_i, st1, st2,
+                   s_sd, r_sd, s_z, r_z, s_sib, r_sib, s_w, s_loc, s_t):
+    T, D = ffn.shape
+    FFW = wg.shape[2]
+    C = nf // 2
+    B = 2 * capp
+    f = lax.axis_index("fsdp")
+    d = lax.axis_index("dp")
+    c = f // 2
+    k = lax.rem(f, 2)
+    sib = f + 1 - 2 * k
+    greet(nf, 1, f, d)
+
+    def remote(src, dst, ss, rs, to_f):
+        return pltpu.make_async_remote_copy(src_ref=src, dst_ref=dst, send_sem=ss, recv_sem=rs,
+                                            device_id=(to_f, d), device_id_type=MESH)
+
+    def chip_at(dr, s):
+        return jnp.where(dr == 0, c - s, c + s)
+
+    def has(dr, s):
+        at = chip_at(dr, s)
+        return (at >= 0) & (at < C)
+
+    def nxt_ok(dr):
+        return (c + 1 < C) if dr == 0 else (c - 1 >= 0)
+
+    def nxt_f(dr):
+        return f + 2 if dr == 0 else f - 2
+
+    def z_out(dr, s):
+        ff = 2 * chip_at(dr, s - 1) + k
+        return remote(fa.at[ff], fa.at[ff], s_z.at[dr, s - 1], r_z.at[dr, s - 1], nxt_f(dr))
+
+    def z_own(dr):
+        return remote(ffn, fa.at[f], s_z.at[dr, 0], r_z.at[dr, 0], nxt_f(dr))
+
+    def z_in(dr, s):
+        ff = 2 * chip_at(dr, s) + k
+        return remote(fa.at[ff], fa.at[ff], s_z.at[dr, s - 1], r_z.at[dr, s - 1], f)
+
+    def sib_out(dr, s):
+        ff = 2 * chip_at(dr, s) + k
+        return remote(fa.at[ff], fa.at[ff], s_sib.at[dr, s], r_sib.at[dr, s], sib)
+
+    def sib_in(dr, s):
+        ff = 2 * chip_at(dr, s) + 1 - k
+        return remote(fa.at[ff], fa.at[ff], s_sib.at[dr, s], r_sib.at[dr, s], f)
+
+    for dr in range(2):
+        @pl.when(nxt_ok(dr))
+        def _():
+            z_own(dr).start()
+    sib_own = remote(ffn, fa.at[f], s_sib.at[1, 0], r_sib.at[1, 0], sib)
+    sib_own.start()
+    own = pltpu.make_async_copy(ffn, fa.at[f], s_loc.at[0])
+    own.start()
+    own_sd = pltpu.make_async_copy(side.at[f], sd.at[f], s_loc.at[1])
+    own_sd.start()
+    sd_copies = []
+    for i in range(1, nf):
+        to = lax.rem(f + i, nf)
+        cp = remote(side.at[to], sd.at[f], s_sd.at[i - 1], r_sd.at[i - 1], to)
+        cp.start()
+        sd_copies.append(cp)
+    w_copies = []
+    for i, (src, dst) in enumerate(((wg_h, wg), (wu_h, wu), (wd_h, wd))):
+        cp = pltpu.make_async_copy(src, dst, s_w.at[i])
+        cp.start()
+        w_copies.append(cp)
+    own.wait()
+    own_sd.wait()
+    for cp in sd_copies:
+        cp.wait()
+    for cp in w_copies:
+        cp.wait()
+
+    row_ids = lax.broadcasted_iota(jnp.int32, (capp, T), 0).astype(F32)
+
+    @pl.loop(0, C)
+    def _(j):
+        b, dr_b, dist_b = visit(c, C, j)
+        cot_cp = pltpu.make_async_copy(cot_a.at[pl.ds(2 * b, 2)], cotb, s_loc.at[2])
+        cot_cp.start()
+
+        @pl.when(j >= 1)
+        def _():
+            for dr in range(2):
+                @pl.when(has(dr, j))
+                def _():
+                    z_in(dr, j).wait_recv()
+
+                    @pl.when(nxt_ok(dr) & (j < C - 1))
+                    def _():
+                        z_out(dr, j + 1).start()
+                    sib_out(dr, j).start()
+        sib_in(dr_b, dist_b).wait_recv()
+        cot_cp.wait()
+
+        base = pl.multiple_of(b * B, 16)
+        gate_rows = [[None, None] for _ in range(el)]
+        picks = []
+        for kk in range(2):
+            s = 2 * b + kk
+            parts = []
+            for e in range(el):
+                hit = row_ids == sd[s, e:e + 1, :]
+                gate_rows[e][kk] = jnp.sum(jnp.where(hit, sd[s, el + e:el + e + 1, :], 0.0), -1, keepdims=True)
+                parts.append(jnp.where(hit, 1.0, 0.0).astype(BF))
+            p2 = jnp.concatenate(parts, 0)
+            picks.append(p2)
+            for n in range(0, D, 512):
+                xv = dot(p2, fa[s, :, n:n + 512]).astype(BF)
+                gv_ = dot(p2, cotb[kk, :, n:n + 512]).astype(BF)
+                for e in range(el):
+                    at = pl.ds(pl.multiple_of(base + kk * capp, 16), capp)
+                    xs[e, at, n:n + 512] = xv[e * capp:(e + 1) * capp]
+                    gs[e, at, n:n + 512] = gv_[e * capp:(e + 1) * capp]
+        here = pl.ds(base, B)
+        gp_rows = []
+        for e in range(el):
+            gate_row = jnp.concatenate(gate_rows[e], 0)
+            gpr = jnp.zeros((B, 1), F32)
+            for n in range(0, FFW, 256):
+                gv = dot(xs[e, here, :], wg[e, :, n:n + 256])
+                uv = dot(xs[e, here, :], wu[e, :, n:n + 256])
+                u = dot_nt(gs[e, here, :], wd[e, n:n + 256, :])
+                sg = 1.0 / (1.0 + jnp.exp(-gv))
+                act = gv * sg
+                hid = act * uv
+                gpr = gpr + jnp.sum(hid * u, -1, keepdims=True)
+                hgs[e, here, n:n + 256] = (hid * gate_row).astype(BF)
+                gh = u * gate_row
+                hs[e, here, n:n + 256] = (gh * uv * (sg * (1.0 + gv * (1.0 - sg)))).astype(BF)
+                hs[e, here, FFW + n:FFW + n + 256] = (gh * act).astype(BF)
+            gp_rows.append(gpr)
+            for n in range(0, D, 512):
+                orow = dot(hgs[e, here, :], wd[e, :, n:n + 512]).astype(BF)
+                irow = (dot_nt(hs[e, here, 0:FFW], wg[e, n:n + 512, :])
+                        + dot_nt(hs[e, here, FFW:2 * FFW], wu[e, n:n + 512, :])).astype(BF)
+                for kk in range(2):
+                    orb[kk, e * capp:(e + 1) * capp, n:n + 512] = orow[kk * capp:(kk + 1) * capp]
+                    irb[kk, e * capp:(e + 1) * capp, n:n + 512] = irow[kk * capp:(kk + 1) * capp]
+
+        def back(bb):
+            return (pltpu.make_async_copy(st_o, out_o.at[pl.ds(2 * bb, 2)], s_loc.at[3]),
+                    pltpu.make_async_copy(st_i, gin_o.at[pl.ds(2 * bb, 2)], s_loc.at[4]))
+
+        @pl.when(j >= 1)
+        def _():
+            for cp in back(0):
+                cp.wait()
+        for kk in range(2):
+            s = 2 * b + kk
+            for e in range(el):
+                hit = picks[kk][e * capp:(e + 1) * capp].astype(F32)
+                gp_o[s, e:e + 1, :] = jnp.sum(hit * gp_rows[e][kk * capp:(kk + 1) * capp], 0, keepdims=True)
+            for n in range(0, D, 512):
+                st_o[kk, :, n:n + 512] = dot_tn(picks[kk], orb[kk, :, n:n + 512]).astype(BF)
+                st_i[kk, :, n:n + 512] = dot_tn(picks[kk], irb[kk, :, n:n + 512]).astype(BF)
+        for cp in back(b):
+            cp.start()
+
+    n1 = D // 256
+    n2 = FFW // 256
+
+    def t1_copy(e, i):
+        return pltpu.make_async_copy(st1.at[lax.rem(i, 2)], t1_o.at[e, pl.ds(pl.multiple_of(i * 256, 256), 256)],
+                                     s_t.at[0, lax.rem(i, 2)])
+
+    def t2_copy(e, i):
+        return pltpu.make_async_copy(st2.at[lax.rem(i, 2)], t2_o.at[e, pl.ds(pl.multiple_of(i * 256, 256), 256)],
+                                     s_t.at[1, lax.rem(i, 2)])
+
+    for e in range(el):
+        @pl.loop(0, n1)
+        def _(i):
+            @pl.when(i >= 2)
+            def _():
+                t1_copy(e, i).wait()
+            col = pl.ds(pl.multiple_of(i * 256, 256), 256)
+            st1[lax.rem(i, 2)] = dot_tn(xs[e, :, col], hs[e]).astype(BF)
+            t1_copy(e, i).start()
+
+        @pl.loop(0, n2)
+        def _(i):
+            @pl.when(i >= 2)
+            def _():
+                t2_copy(e, i).wait()
+            col = pl.ds(pl.multiple_of(i * 256, 256), 256)
+            st2[lax.rem(i, 2)] = dot_tn(hgs[e, :, col], gs[e]).astype(BF)
+            t2_copy(e, i).start()
+        for i in range(2):
+            t1_copy(e, i).wait()
+            t2_copy(e, i).wait()
+
+    pltpu.make_async_copy(st_o, out_o.at[pl.ds(0, 2)], s_loc.at[3]).wait()
+    pltpu.make_async_copy(st_i, gin_o.at[pl.ds(0, 2)], s_loc.at[4]).wait()
+    sib_own.wait_send()
+    for dr in range(2):
+        for s in range(1, C):
+            @pl.when(has(dr, s))
+            def _():
+                sib_out(dr, s).wait_send()
+        for s in range(1, C):
+            @pl.when(nxt_ok(dr) & has(dr, s - 1))
+            def _():
+                z_out(dr, s).wait_send()
+
+
+def experts_call(nf, cap, ffn_in, cot_all, side, w_gate, w_up, w_down):
+    T, D = ffn_in.shape
+    el, _, FFW = w_gate.shape
+    capp = cap + (-cap % 16)
+    C = nf // 2
+    rows = C * 2 * capp
+    dma = pltpu.SemaphoreType.DMA
+    out = [((nf, T, D), BF, 1), ((nf, T, D), BF, 1), ((nf, el, T), F32, 0),
+           ((el, D, 2 * FFW), BF, 1), ((el, FFW, D), BF, 1)]
+    return pl.pallas_call(
+        functools.partial(experts_kernel, nf, el, cap, capp),
+        out_shape=[jax.ShapeDtypeStruct(o[0], o[1]) for o in out],
+        in_specs=[vm(), hbm(), vm(), hbm(), hbm(), hbm()],
+        out_specs=[hbm() if o[2] else vm() for o in out],
+        scratch_shapes=[
+            VMEM((el, D, FFW), BF), VMEM((el, D, FFW), BF), VMEM((el, FFW, D), BF),
+            VMEM((nf, T, D), BF), VMEM(side.shape, F32), VMEM((2, T, D), BF),
+            VMEM((el, rows, D), BF), VMEM((el, rows, D), BF),
+            VMEM((el, rows, 2 * FFW), BF), VMEM((el, rows, FFW), BF),
+            VMEM((2, el * capp, D), BF), VMEM((2, el * capp, D), BF),
+            VMEM((2, T, D), BF), VMEM((2, T, D), BF),
+            VMEM((2, 256, 2 * FFW), BF), VMEM((2, 256, D), BF),
+            dma((nf,)), dma((nf,)),
+            dma((2, C)), dma((2, C)), dma((2, C)), dma((2, C)),
+            dma((3,)), dma((5,)), dma((2, 2)),
+        ],
+        compiler_params=pltpu.CompilerParams(collective_id=2, has_side_effects=True,
+                                             vmem_limit_bytes=62 * 2 ** 20),
+        cost_estimate=pl.CostEstimate(flops=40_000_000_000, bytes_accessed=60_000_000, transcendentals=2_000_000),
+        name="experts",
+    )(ffn_in, cot_all, side, w_gate, w_up, w_down)
+
+
+def add_blocks(dst, srcs, extra=None):
+    @pl.loop(0, dst.shape[0] // 16)
+    def _(i):
+        at = pl.ds(pl.multiple_of(i * 16, 16), 16)
+        total = srcs[0][at, :].astype(F32)
+        for s in srcs[1:]:
+            total = total + s[at, :].astype(F32)
+        dst[at, :] = total.astype(dst.dtype)
+
+
+class Line:
+    def __init__(self, nf, f, d, acc, give, sib, rcv, stage, sems, stage_sem, credit=None):
+        self.nf, self.f, self.d = nf, f, d
+        self.C = nf // 2
+        self.c, self.k = f // 2, lax.rem(f, 2)
+        self.acc, self.give, self.sib, self.rcv, self.stage = acc, give, sib, rcv, stage
+        self.s_sib, self.r_sib, self.s_z, self.r_z = sems
+        self.stage_sem, self.credit = stage_sem, credit
+
+    def remote(self, src, dst, ss, rs, to):
+        return pltpu.make_async_remote_copy(src_ref=src, dst_ref=dst, send_sem=ss, recv_sem=rs,
+                                            device_id=(to, self.d), device_id_type=MESH)
+
+    def dest(self, dr, s):
+        i = s - 1 - (self.C - 1 - self.c) if dr == 0 else s - 1 - self.c
+        room = self.c if dr == 0 else self.C - 1 - self.c
+        chip = i if dr == 0 else self.C - 1 - i
+        return jnp.clip(chip, 0, self.C - 1), (i >= 0) & (i < room), i == 0
+
+    def sib_copy(self, chip):
+        return self.remote(self.give(chip), self.sib(chip), self.s_sib.at[chip], self.r_sib.at[chip],
+                           self.f + 1 - 2 * self.k)
+
+    def z_copy(self, dr, s, chip):
+        return self.remote(self.acc(chip), self.rcv(dr, s - 1), self.s_z.at[dr, s - 1], self.r_z.at[dr, s - 1],
+                           self.f - 2 if dr == 0 else self.f + 2)
+
+    def z_in(self, dr, s):
+        return self.remote(self.rcv(dr, s - 1), self.rcv(dr, s - 1), self.s_z.at[dr, s - 1], self.r_z.at[dr, s - 1],
+                           self.f)
+
+    def start_sib(self):
+        if self.credit is not None:
+            pl.semaphore_wait(self.credit.at[2], 1)
+        for s in range(1, self.C):
+            for dr in range(2):
+                chip, ok, _ = self.dest(dr, s)
+
+                @pl.when(ok)
+                def _():
+                    self.sib_copy(chip).start()
+        self.sib_copy(self.c).start()
+
+    def gather(self, chip, srcs):
+        acc = self.acc(chip)
+        if self.stage is None:
+            add_blocks(acc, [acc] + srcs)
+            return
+        for s in srcs:
+            cp = pltpu.make_async_copy(s, self.stage, self.stage_sem)
+            cp.start()
+            cp.wait()
+            add_blocks(acc, [acc, self.stage])
+
+    def step(self, s):
+        for dr in range(2):
+            chip, ok, opening = self.dest(dr, s)
+            begins = (self.c == self.C - 1) if dr == 0 else (self.c == 0)
+
+            @pl.when(ok)
+            def _():
+                self.sib_copy(chip).wait_recv()
+
+                @pl.when(begins)
+                def _():
+                    self.gather(chip, [self.sib(chip)])
+                if s > 1:
+                    @pl.when(jnp.logical_not(begins))
+                    def _():
+                        self.z_in(dr, s - 1).wait_recv()
+                        self.gather(chip, [self.sib(chip), self.rcv(dr, s - 2)])
+                if self.credit is not None:
+                    @pl.when(opening)
+                    def _():
+                        pl.semaphore_wait(self.credit.at[dr], 1)
+                self.z_copy(dr, s, chip).start()
+
+    def last(self):
+        self.sib_copy(self.c).wait_recv()
+        mid = (self.c > 0) & (self.c < self.C - 1)
+        s = self.C - 1
+        for dr in range(2):
+            @pl.when((self.c < self.C - 1) if dr == 0 else (self.c > 0))
+            def _():
+                self.z_in(dr, s).wait_recv()
+
+        @pl.when(mid)
+        def _():
+            self.gather(self.c, [self.sib(self.c), self.rcv(0, s - 1), self.rcv(1, s - 1)])
+
+        @pl.when(self.c == 0)
+        def _():
+            self.gather(self.c, [self.sib(self.c), self.rcv(0, s - 1)])
+
+        @pl.when(self.c == self.C - 1)
+        def _():
+            self.gather(self.c, [self.sib(self.c), self.rcv(1, s - 1)])
+
+    def sent(self):
+        self.sib_copy(self.c).wait_send()
+        for s in range(1, self.C):
+            for dr in range(2):
+                chip, ok, _ = self.dest(dr, s)
+
+                @pl.when(ok)
+                def _():
+                    self.sib_copy(chip).wait_send()
+                    self.z_copy(dr, s, chip).wait_send()
+
+    def free(self, credit):
+        def tell(i, to):
+            pl.semaphore_signal(credit.at[i], inc=1, device_id=(to, self.d), device_id_type=MESH)
+
+        tell(2, self.f + 1 - 2 * self.k)
+
+        @pl.when(self.c < self.C - 1)
+        def _():
+            tell(0, self.f + 2)
+
+        @pl.when(self.c > 0)
+        def _():
+            tell(1, self.f - 2)
+
+
+class Cube:
+    def __init__(self, nd, f, d, flip, lanes, size, own, land, total, out, sems):
+        m = nd.bit_length() - 1
+        self.bits = list(range(m))[::-1] if flip else list(range(m))
+        self.f, self.d, self.lanes = f, d, lanes
+        self.own, self.land, self.total, self.out = own, land, total, out
+        self.ss, self.rs = sems
+        self.m = m
+        self.low, self.length = [0], [size]
+        for b in self.bits:
+            half = self.length[-1] // 2
+            side = lax.rem(d // (1 << b), 2)
+            self.low.append(self.low[-1] + side * half)
+            self.length.append(half)
+
+    def cut(self, ref, at, n):
+        if self.lanes:
+            return ref.at[:, pl.ds(pl.multiple_of(at, 128), n)]
+        return ref.at[pl.ds(pl.multiple_of(at, 16), n)]
+
+    def remote(self, src, dst, i, to_bit):
+        return pltpu.make_async_remote_copy(src_ref=src, dst_ref=dst, send_sem=self.ss.at[i], recv_sem=self.rs.at[i],
+                                            device_id=(self.f, jnp.bitwise_xor(self.d, 1 << to_bit)),
+                                            device_id_type=MESH)
+
+    def level(self, i):
+        if i == 0:
+            return self.own, 0
+        if i == self.m:
+            return self.out, 0
+        return self.total(i - 1), self.low[i]
+
+    def down(self, i):
+        ref, base = self.level(i)
+        half = self.length[i + 1]
+        other = 2 * self.low[i] + half - self.low[i + 1]
+        return self.remote(self.cut(ref, other - base, half), self.land(i), i, self.bits[i])
+
+    def merge(self, i, add):
+        self.down(i).wait_recv()
+        ref, base = self.level(i)
+        dst, dbase = self.level(i + 1)
+        half = self.length[i + 1]
+        low = self.low[i + 1]
+        add(self.cut(dst, low - dbase, half), self.cut(ref, low - base, half), self.land(i))
+
+    def up(self, i):
+        blk = self.cut(self.out, self.low[i + 1], self.length[i + 1])
+        return self.remote(blk, blk, self.m + i, self.bits[i])
+
+    def up_in(self, i):
+        half = self.length[i + 1]
+        other = 2 * self.low[i] + half - self.low[i + 1]
+        blk = self.cut(self.out, other, half)
+        return self.remote(blk, blk, self.m + i, self.bits[i])
+
+    def sent(self):
+        for i in range(self.m):
+            self.down(i).wait_send()
+            self.up(i).wait_send()
+
+
+def pipe_add(dst, a, b):
+    n, w = dst.shape
+    tile = 32
+    spec = pl.BlockSpec((tile, w), lambda i: (i, 0))
+
+    def inner(a_ref, b_ref, o_ref):
+        o_ref[...] = (a_ref[...].astype(F32) + b_ref[...].astype(F32)).astype(o_ref.dtype)
+
+    pltpu.emit_pipeline(inner, grid=(n // tile,), in_specs=[spec, spec], out_specs=[spec])(a, b, dst)
+
+
+def back_kernel(nf, nd, el, land_hbm, *refs):
+    m = nd.bit_length() - 1
+    it = iter(refs)
+
+    def take(n):
+        return [next(it) for _ in range(n)]
+
+    (gin_p, out_p, gp_p, t1, t2, tok_h, cot_h, hid_h, ffn_h, gates, mix_h, qk_h, v_h, prob_h, wf_h, rt,
+     cosr, sinr) = take(18)
+    out_o, gt_o, sh_o, sm_o, t1_o, t2_o = take(6)
+    l1 = take(m)
+    l2 = take(m)
+    a1 = take(m - 1)
+    a2 = take(m - 1)
+    sib, rcv, sibq, rcvq = take(4)
+    (acc, wb, wg, tok, cot, hid, ffn, mix, qk, v, prob, branch, gh, ga, gproj, gpb, smg, smr, smd, shb, sms) = take(21)
+    attn, gm = ffn, mix
+    shl = take(m)
+    stage, stageq = take(2)
+    (s_load, s_acc, s_gp, r_gp, s_sib, r_sib, s_z, r_z, s_cube, r_cube, s_sc, r_sc, s_sm, r_sm, s_sd, r_sd,
+     s_stage, s_prob, cred) = take(19)
+
+    T, D = tok.shape
+    R = wg.shape[0] // nf
+    W = wg.shape[1]
+    E = gates.shape[0]
+    C = nf // 2
+    f = lax.axis_index("fsdp")
+    d = lax.axis_index("dp")
+    c = f // 2
+    k = lax.rem(f, 2)
+    QV = QW + 2 * KW
+    greet(nf, nd, f, d)
+
+    def remote(src, dst, ss, rs, to_f, to_d):
+        return pltpu.make_async_remote_copy(src_ref=src, dst_ref=dst, send_sem=ss, recv_sem=rs,
+                                            device_id=(to_f, to_d), device_id_type=MESH)
+
+    def rows(ff):
+        return pl.ds(pl.multiple_of(ff * R, 16), R)
+
+    st = stage if land_hbm else None
+    stq = stageq if land_hbm else None
+
+    def sems(i):
+        return (s_sib.at[i], r_sib.at[i], s_z.at[i], r_z.at[i])
+
+    gin_line = Line(nf, f, d, lambda ch: acc.at[ch], lambda ch: gin_p.at[2 * ch + 1 - k], lambda ch: sib.at[ch],
+                    lambda dr, s: rcv.at[dr, s], st, sems(0), s_stage)
+    wo_cols = pl.ds(QV, D)
+    o_line = Line(nf, f, d, lambda ch: wg.at[rows(2 * ch + k), wo_cols], lambda ch: wg.at[rows(2 * ch + 1 - k), wo_cols],
+                  lambda ch: sib.at[ch, 0:R], lambda dr, s: rcv.at[dr, s, 0:R],
+                  stage.at[0:R] if land_hbm else None, sems(1), s_stage, cred.at[0])
+    q_cols = pl.ds(0, QV)
+    q_line = Line(nf, f, d, lambda ch: wg.at[rows(2 * ch + k), q_cols], lambda ch: wg.at[rows(2 * ch + 1 - k), q_cols],
+                  lambda ch: sibq.at[ch], lambda dr, s: rcvq.at[dr, s], stq, sems(2), s_stage)
+    out_line = Line(nf, f, d, lambda ch: acc.at[ch], lambda ch: out_p.at[2 * ch + 1 - k], lambda ch: sib.at[ch],
+                    lambda dr, s: rcv.at[dr, s], st, sems(3), s_stage, cred.at[1])
+
+    def acc_loads(src):
+        return [pltpu.make_async_copy(src.at[2 * ch + k], acc.at[ch], s_acc.at[ch]) for ch in range(C)]
+
+    gp_copies = []
+    for i in range(1, nf):
+        to = lax.rem(f + i, nf)
+        cp = remote(gp_p.at[to], gpb.at[f], s_gp.at[i - 1], r_gp.at[i - 1], to, d)
+        cp.start()
+        gp_copies.append(cp)
+    loads = acc_loads(gin_p)
+    for cp in loads:
+        cp.start()
+    gin_line.start_sib()
+    cubes = []
+    for e in range(el):
+        for j, (src, out, ls, ts, size) in enumerate(((t1, t1_o, l1, a1, D), (t2, t2_o, l2, a2, t2.shape[1]))):
+            cube = Cube(nd, f, d, e >= el // 2, False, size, src.at[e],
+                        functools.partial(lambda ls, e, i: ls[i].at[e], ls, e),
+                        functools.partial(lambda ts, e, i: ts[i].at[e], ts, e), out.at[e],
+                        (s_cube.at[2 * e + j], r_cube.at[2 * e + j]))
+            cubes.append(cube)
+    for cube in cubes:
+        cube.down(0).start()
+    own_gp = pltpu.make_async_copy(gp_p.at[f], gpb.at[f], s_load.at[0])
+    own_gp.start()
+    wo = pltpu.make_async_copy(wf_h.at[:, QV:QV + D], wb.at[:, 0:D], s_load.at[1])
+    wo.start()
+    others = [(tok_h, tok), (cot_h, cot), (hid_h, hid), (ffn_h, ffn), (mix_h, mix), (qk_h, qk), (v_h, v)]
+    more = [pltpu.make_async_copy(a, b, s_load.at[2 + i]) for i, (a, b) in enumerate(others)]
+    for cp in more:
+        cp.start()
+
+    def prob_load(i):
+        at = pl.ds(i * 2 * GROUP, 2 * GROUP)
+        return pltpu.make_async_copy(prob_h.at[at], prob.at[lax.rem(i, 2)], s_prob.at[lax.rem(i, 2)])
+
+    prob_load(0).start()
+    for cp in loads:
+        cp.wait()
+
+    for s in range(1, C):
+        gin_line.step(s)
+    for cp in more:
+        cp.wait()
+    own_gp.wait()
+    for cp in gp_copies:
+        cp.wait()
+    gin_line.last()
+    gin_line.free(cred.at[0])
+
+    gains = rt[E:E + 2].astype(F32)
+    gain_one, gain_two = gains[0:1], gains[1:2]
+    gpt = jnp.concatenate([gpb[i] for i in range(nf)], 0)
+    gates_v = gates[...]
+    gl = (gates_v * (gpt - jnp.sum(gpt * gates_v, 0, keepdims=True))).astype(BF)
+    for n in range(0, D, 512):
+        sms[0:E, n:n + 512] = dot(gl, ffn[:, n:n + 512])
+    for n in range(0, D, 512):
+        ga[:, n:n + 512] = dot_tn(gl, rt[0:E, n:n + 512])
+    sms[E:, :] = jnp.zeros((sms.shape[0] - E, D), F32)
+    TR = 32
+
+    @pl.loop(0, T // TR)
+    def _(i):
+        at = pl.ds(pl.multiple_of(i * TR, TR), TR)
+        h = hid[at, :]
+        r2 = lax.rsqrt(jnp.mean(h * h, -1, keepdims=True) + EPSILON)
+        n2 = h * r2
+        gf = acc[c, at, :].astype(F32) + ga[at, :]
+        sms[E + 1:E + 2, :] += jnp.sum(gf * n2, 0, keepdims=True)
+        g2 = gf * gain_two
+        x = cot[at, :].astype(F32) + r2 * (g2 - n2 * jnp.mean(g2 * n2, -1, keepdims=True))
+        gh[at, :] = x
+        branch[at, :] = x.astype(BF)
+
+    @pl.loop(0, QW // 256)
+    def _(i):
+        at = pl.ds(pl.multiple_of(i * 256, 256), 256)
+        wg[at, QV:QV + D] = dot_tn(mix[:, at], branch[...]).astype(BF)
+    o_line.start_sib()
+    o_line.step(1)
+    gin_line.sent()
+    wo.wait()
+
+    @pl.loop(0, QW // 256)
+    def _(i):
+        at = pl.ds(pl.multiple_of(i * 256, 256), 256)
+        gm[:, at] = dot_nt(branch[...], wb[at, 0:D]).astype(BF)
+    wq = pltpu.make_async_copy(wf_h.at[:, 0:QV], wb, s_load.at[1])
+    wq.start()
+    for cube in cubes:
+        cube.merge(0, pipe_add)
+    for cube in cubes:
+        cube.down(1).start() if m > 1 else cube.up(0).start()
+
+    factor = HEAD_SIZE ** (-0.5)
+    lane = lax.broadcasted_iota(jnp.int32, (T, 128), 1)
+    low = lane < HEAD_SIZE
+    first = lax.rem(lane, HEAD_SIZE) < HEAD_SIZE // 2
+
+    def unrotate(x):
+        return x * cosr[...] - half_roll(x, first) * sinr[...]
+
+    @pl.loop(0, KEY_VALUE_HEADS // 2)
+    def _(i):
+        @pl.when(i + 1 < KEY_VALUE_HEADS // 2)
+        def _():
+            prob_load(i + 1).start()
+        prob_load(i).wait()
+        slot = lax.rem(i, 2)
+        kcol = pl.ds(pl.multiple_of(i * 128, 128), 128)
+        kh = head_masks(qk[:, pl.ds(pl.multiple_of(QW + i * 128, 128), 128)], lane)
+        vh = head_masks(v[:, kcol], lane)
+        gk = [[None, None], [None, None]]
+        gv = [[None, None], [None, None]]
+        for p in range(GROUP):
+            qc = pl.ds(pl.multiple_of((i * GROUP + p) * 128, 128), 128)
+            q = qk[:, qc]
+            g = gm[:, qc]
+            gq = None
+            for half in range(2):
+                kv = (2 * p + half) // GROUP
+                pr = prob[slot, 2 * p + half]
+                prf = pr.astype(F32)
+                gp = dot_nt(g, vh[kv][half])
+                gs = (prf * (gp - jnp.sum(prf * gp, -1, keepdims=True))).astype(BF)
+                term = dot(gs, kh[kv][half])
+                gq = term if gq is None else gq + term
+                tk = dot_tn(gs, q)
+                tv = dot_tn(pr, g)
+                gk[kv][half] = tk if gk[kv][half] is None else gk[kv][half] + tk
+                gv[kv][half] = tv if gv[kv][half] is None else gv[kv][half] + tv
+            gproj[:, qc] = unrotate(gq * factor).astype(BF)
+
+        def join(x):
+            a = jnp.where(low, x[0][0] + pltpu.roll(x[0][1], HEAD_SIZE, axis=1), 0.0)
+            b = jnp.where(low, 0.0, pltpu.roll(x[1][0], HEAD_SIZE, axis=1) + x[1][1])
+            return a + b
+
+        gproj[:, pl.ds(pl.multiple_of(QW + i * 128, 128), 128)] = unrotate(join(gk) * factor).astype(BF)
+        gproj[:, pl.ds(pl.multiple_of(QW + KW + i * 128, 128), 128)] = join(gv).astype(BF)
+
+    if C > 2:
+        o_line.step(2)
+    @pl.loop(0, T // TR)
+    def _(i):
+        at = pl.ds(pl.multiple_of(i * TR, TR), TR)
+        x = tok[at, :].astype(F32)
+        r1 = lax.rsqrt(jnp.mean(x * x, -1, keepdims=True) + EPSILON)
+        attn[at, :] = (x * r1 * gain_one).astype(BF)
+
+    @pl.loop(0, D // 256)
+    def _(i):
+        at = pl.ds(pl.multiple_of(i * 256, 256), 256)
+        for n in range(0, QV, 512):
+            wg[at, n:n + 512] = dot_tn(attn[:, at], gproj[:, n:n + 512]).astype(BF)
+    q_line.start_sib()
+    for s in range(3, C):
+        o_line.step(s)
+    q_line.step(1)
+    if m > 1:
+        for cube in cubes:
+            cube.merge(1, pipe_add)
+        for cube in cubes:
+            cube.down(2).start() if m > 2 else cube.up(1).start()
+    wq.wait()
+
+    @pl.loop(0, D // 256)
+    def _(i):
+        at = pl.ds(pl.multiple_of(i * 256, 256), 256)
+        ga[:, at] = dot_nt(gproj[...], wb[at, :])
+
+    @pl.loop(0, T // TR)
+    def _(i):
+        at = pl.ds(pl.multiple_of(i * TR, TR), TR)
+        x = tok[at, :].astype(F32)
+        r1 = lax.rsqrt(jnp.mean(x * x, -1, keepdims=True) + EPSILON)
+        n1 = x * r1
+        gat = ga[at, :]
+        sms[E:E + 1, :] += jnp.sum(gat * n1, 0, keepdims=True)
+        g1 = gat * gain_one
+        gt_o[at, :] = (gh[at, :] + r1 * (g1 - n1 * jnp.mean(g1 * n1, -1, keepdims=True))).astype(BF)
+
+    small = sms[...]
+    for i in range(nf):
+        smg[i] = small[:, i * R:(i + 1) * R]
+    sm_copies = []
+    for i in range(1, nf):
+        to = lax.rem(f + i, nf)
+        cp = remote(smg.at[to], smr.at[f], s_sm.at[i - 1], r_sm.at[i - 1], to, d)
+        cp.start()
+        sm_copies.append(cp)
+    smr_own = pltpu.make_async_copy(smg.at[f], smr.at[f], s_load.at[0])
+    smr_own.start()
+
+    o_line.last()
+    o_line.free(cred.at[1])
+    if C > 2:
+        q_line.step(2)
+    o_line.sent()
+    out_loads = acc_loads(out_p)
+    for cp in out_loads:
+        cp.start()
+    smr_own.wait()
+    for cp in sm_copies:
+        cp.wait()
+    total = smr[0]
+    for i in range(1, nf):
+        total = total + smr[i]
+    smd[0] = total
+    sd_copies = []
+    for i in range(1, nd):
+        cp = remote(smd.at[0], smd.at[i], s_sd.at[i - 1], r_sd.at[i - 1], f, jnp.bitwise_xor(d, i))
+        cp.start()
+        sd_copies.append(cp)
+    for s in range(3, C):
+        q_line.step(s)
+    out_line.start_sib()
+    for cp in out_loads:
+        cp.wait()
+    if m > 2:
+        for i in range(2, m):
+            for cube in cubes:
+                cube.merge(i, pipe_add)
+            for cube in cubes:
+                cube.down(i + 1).start() if i + 1 < m else cube.up(m - 1).start()
+    for i in range(m - 1, 0, -1):
+        for cube in cubes:
+            cube.up_in(i).wait_recv()
+        for cube in cubes:
+            cube.up(i - 1).start()
+    out_line.step(1)
+    q_line.last()
+
+    own = wg.at[rows(f)]
+    add_blocks(shb, [own])
+    half = W // 2
+    shards = []
+    for h in range(2):
+        shards.append(Cube(nd, f, d, h == 1, True, half, shb.at[:, h * half:(h + 1) * half],
+                           functools.partial(lambda h, i: shl[i].at[h], h),
+                           functools.partial(lambda h, i: shb.at[:, h * half:(h + 1) * half], h),
+                           sh_o.at[:, h * half:(h + 1) * half], (s_sc.at[h], r_sc.at[h])))
+
+    def level(self, i):
+        return (self.own, 0) if i < self.m else (self.out, 0)
+
+    for cube in shards:
+        cube.level = functools.partial(level, cube)
+        cube.down(0).start()
+
+    def vadd(dst, a, b):
+        add_blocks(dst, [a, b])
+
+    if C > 2:
+        out_line.step(2)
+    for i in range(m):
+        for cube in shards:
+            cube.merge(i, vadd)
+        for cube in shards:
+            cube.down(i + 1).start() if i + 1 < m else cube.up(i).start()
+    for s in range(3, C):
+        out_line.step(s)
+    for i in range(m - 1, 0, -1):
+        for cube in shards:
+            cube.up_in(i).wait_recv()
+        for cube in shards:
+            cube.up(i - 1).start()
+    for cp in sd_copies:
+        cp.wait()
+    total = smd[0]
+    for i in range(1, nd):
+        total = total + smd[i]
+    sm_o[...] = total
+    out_line.last()
+
+    @pl.loop(0, T // TR)
+    def _(i):
+        at = pl.ds(pl.multiple_of(i * TR, TR), TR)
+        out_o[at, :] = (hid[at, :] + acc[c, at, :].astype(F32)).astype(BF)
+
+
+    q_line.sent()
+    out_line.sent()
+    for cube in cubes + shards:
+        cube.up_in(0).wait_recv()
+        cube.sent()
+
+
+def back(nf, nd, el, args):
+    gin, t1, t2 = args[0], args[3], args[4]
+    _, T, D = gin.shape
+    E = args[9].shape[0]
+    W = args[14].shape[1]
+    R = D // nf
+    C = nf // 2
+    m = nd.bit_length() - 1
+    QV = QW + 2 * KW
+    FFW = t2.shape[1]
+    SR = E + 2 + (-(E + 2) % 8)
+    land_hbm = C > 4
+    s = jax.ShapeDtypeStruct
+    out_shape = [s((T, D), BF), s((T, D), BF), s((R, W), BF), s((SR, R), F32), s(t1.shape, BF), s(t2.shape, BF)]
+    out_specs = [vm(), vm(), vm(), vm(), hbm(), hbm()]
+    extra = [(el, D >> (i + 1), t1.shape[2]) for i in range(m)] + [(el, FFW >> (i + 1), D) for i in range(m)]
+    extra += [(el, D >> (i + 1), t1.shape[2]) for i in range(m - 1)] + [(el, FFW >> (i + 1), D) for i in range(m - 1)]
+    lands = [(C, T, D), (2, C - 1, T, D), (C, R, QV), (2, C - 1, R, QV)]
+    scratch = []
+    if land_hbm:
+        extra += lands
+    else:
+        scratch += [VMEM(x, BF) for x in lands]
+    out_shape += [s(x, BF) for x in extra]
+    out_specs += [hbm()] * len(extra)
+    dma = pltpu.SemaphoreType.DMA
+    scratch += [
+        VMEM((C, T, D), BF), VMEM((D, QV), BF), VMEM((D, W), BF),
+        VMEM((T, D), BF), VMEM((T, D), BF), VMEM((T, D), F32), VMEM((T, D), BF), VMEM((T, QW), BF),
+        VMEM((T, QW + KW), BF), VMEM((T, KW), BF), VMEM((2, 2 * GROUP, T, T), BF),
+        VMEM((T, D), BF), VMEM((T, D), F32), VMEM((T, D), F32), VMEM((T, QV), BF),
+        VMEM((nf, el, T), F32), VMEM((nf, SR, R), F32), VMEM((nf, SR, R), F32), VMEM((nd, SR, R), F32), VMEM((R, W), BF),
+        VMEM((SR, D), F32),
+    ]
+    scratch += [VMEM((2, R, W >> (i + 2)), BF) for i in range(m)]
+    scratch += [VMEM((T, D) if land_hbm else (16, 128), BF), VMEM((R, QV) if land_hbm else (16, 128), BF)]
+    scratch += [
+        dma((10,)), dma((C,)), dma((nf,)), dma((nf,)),
+        dma((4, C)), dma((4, C)), dma((4, 2, C)), dma((4, 2, C)),
+        dma((2 * el, 2 * m)), dma((2 * el, 2 * m)), dma((2, 2 * m)), dma((2, 2 * m)),
+        dma((nf,)), dma((nf,)), dma((nd,)), dma((nd,)), dma(()), dma((2,)),
+        pltpu.SemaphoreType.REGULAR((2, 3)),
+    ]
+    inner = [hbm(), hbm(), vm(), hbm(), hbm(), hbm(), hbm(), hbm(), hbm(), vm(), hbm(), hbm(), hbm(), hbm(), hbm(), vm(),
+             vm(), vm()]
+    return pl.pallas_call(
+        functools.partial(back_kernel, nf, nd, el, land_hbm),
+        out_shape=out_shape,
+        in_specs=inner,
+        out_specs=out_specs,
+        scratch_shapes=scratch,
+        compiler_params=pltpu.CompilerParams(collective_id=3, has_side_effects=True,
+                                             vmem_limit_bytes=63 * 2 ** 20),
+        cost_estimate=pl.CostEstimate(flops=8_000_000_000, bytes_accessed=90_000_000, transcendentals=100_000),
+        name="back",
+    )(*args)[:6]
 
 
 def body(tokens, w_query, key_weight, value_weight, w_out, gain_attn, gain_ffn, w_router,
          w_gate, w_up, w_down, routes, cotangent):
     T = tokens.shape[0]
     el = w_gate.shape[0]
+    ff = w_gate.shape[2]
     nf = lax.axis_size("fsdp")
     nd = lax.axis_size("dp")
     experts = el * nf
     cap = 9 * T * TOP // (8 * experts)
-    dp = lax.axis_index("dp")
-    fs = lax.axis_index("fsdp")
 
     packed = jnp.concatenate([w_query, key_weight, value_weight, w_out], 1)
     pad = -(experts + 2) % 16
     small = jnp.concatenate([w_router, gain_attn[:, None], gain_ffn[:, None],
                              jnp.zeros((w_router.shape[0], pad), BF)], 1).T
-    onehot = (routes[:, :, None] == jnp.arange(experts, dtype=jnp.int32)).any(1)
-    before = jnp.cumsum(onehot.astype(jnp.int32), 0) - onehot.astype(jnp.int32)
-    slots = jnp.where(onehot, before, -1).astype(F32)
+    onehot = (routes[:, :, None] == jnp.arange(experts, dtype=jnp.int32)).any(1).astype(BF)
+    earlier = (jnp.arange(T)[:, None] < jnp.arange(T)[None, :]).astype(BF)
+    before = lax.dot_general(onehot, earlier, (((0,), (0,)), ((), ())), preferred_element_type=F32)
+    slots = jnp.where(onehot.T > 0, before, -1.0)
     cosr, sinr = rope_rows(T)
-    ffn_in, hidden, gates_t, mixed, qk, v2, probs_low, full, cot_all, rt = front(
-        nf, nd, experts, tokens, packed, small, cotangent, slots.T, cosr, sinr)
-    gates = gates_t.T
-    qkv_full = full[:, : QW + 2 * KW]
-    out_full = full[:, QW + 2 * KW:]
-    router_full = rt[:experts].T
-    gain_one = rt[experts].astype(F32)
-    gain_two = rt[experts + 1].astype(F32)
-    xf = tokens.astype(F32)
-    r1 = rms_scale(xf)
-    n1 = xf * r1
-    attn_in = (n1 * gain_one).astype(BF)
-    c, s = rope_tables(T)
-    q = qk[:, :QW].reshape(T, KEY_VALUE_HEADS, GROUP, HEAD_SIZE)
-    k = qk[:, QW:].reshape(T, KEY_VALUE_HEADS, HEAD_SIZE)
-    v = v2.reshape(T, KEY_VALUE_HEADS, HEAD_SIZE)
-    factor = HEAD_SIZE ** (-0.5)
-    probs_low = probs_low.reshape(KEY_VALUE_HEADS, GROUP, T, T)
-    probs = probs_low.astype(F32)
-    r2 = rms_scale(hidden)
-    n2 = hidden * r2
-
-    ffn_all = lax.all_gather(ffn_in, "fsdp", axis=0)
-    side = lax.all_gather(jnp.stack([slots.T, gates.T]), "fsdp", axis=0)
-    side = lax.dynamic_slice_in_dim(side, fs * el, el, 2)
-    slot_l, gate_l = side[:, 0], side[:, 1]
-    pick = slot_l[:, :, None, :] == jnp.arange(cap, dtype=F32)[None, None, :, None]
-    sel = pick.astype(BF)
-    gate_row = jnp.sum(jnp.where(pick, gate_l[:, :, None, :], 0.0), -1, keepdims=True)
-
-    x = mm("nect,ntd->necd", sel, ffn_all).astype(BF)
-    g = mm("nect,ntd->necd", sel, cot_all).astype(BF)
-    gate_val = mm("necd,edf->necf", x, w_gate)
-    up_val = mm("necd,edf->necf", x, w_up)
-    sg = jax.nn.sigmoid(gate_val)
-    act = gate_val * sg
-    hid = act * up_val
-    u = mm("necd,efd->necf", g, w_down)
-    grad_probs_row = jnp.sum(hid.astype(BF).astype(F32) * u, -1)
-    hid_g = (hid * gate_row).astype(BF)
-    grad_hid = u * gate_row
-    grad_up = (grad_hid * act).astype(BF)
-    grad_gate = (grad_hid * up_val * sg * (1.0 + gate_val * (1.0 - sg))).astype(BF)
-    out_rows = mm("necf,efd->necd", hid_g, w_down).astype(BF)
-    gin_rows = (mm("necf,edf->necd", grad_gate, w_gate) + mm("necf,edf->necd", grad_up, w_up)).astype(BF)
-    out_part = mm("nect,necd->ntd", sel, out_rows).astype(BF)
-    gin_part = mm("nect,necd->ntd", sel, gin_rows).astype(BF)
-    gp_part = jnp.sum(jnp.where(pick, grad_probs_row[..., None], 0.0), 2)
-    gp_all = lax.all_to_all(gp_part, "fsdp", split_axis=0, concat_axis=0)
-    grad_probs = gp_all.reshape(experts, T).T
-    gin_own = lax.psum_scatter(gin_part, "fsdp", scatter_dimension=0, tiled=False)
-    out_own = lax.psum_scatter(out_part, "fsdp", scatter_dimension=0, tiled=False)
-    term_gate = mm("necd,necf->edf", x, grad_gate)
-    term_up = mm("necd,necf->edf", x, grad_up)
-    term_down = mm("necf,necd->efd", hid_g, g)
-    terms = (term_gate.astype(BF), term_up.astype(BF), term_down.astype(BF))
-    terms = lax.psum(terms, "dp")
-
-    output = (hidden + out_own.astype(F32)).astype(BF)
-    grad_out = cotangent.astype(F32)
-    dot = jnp.sum(grad_probs * gates, -1, keepdims=True)
-    grad_logits = (gates * (grad_probs - dot)).astype(BF)
-    grad_router = jnp.dot(ffn_in.T, grad_logits, preferred_element_type=F32)
-    gffn = gin_own.astype(F32) + jnp.dot(grad_logits, router_full.T, preferred_element_type=F32)
-    gh, grad_gain_two = norm_back(gffn, n2, r2, gain_two)
-    grad_hidden = grad_out + gh
-    branch = grad_hidden.astype(BF)
-    grad_out_w = jnp.dot(mixed.T, branch, preferred_element_type=F32)
-    gm = jnp.dot(branch, out_full.T, preferred_element_type=F32).astype(BF)
-    gm = gm.reshape(T, KEY_VALUE_HEADS, GROUP, HEAD_SIZE)
-    gp = mm("qgrd,kgd->grqk", gm, v)
-    row = jnp.sum(probs * gp, -1, keepdims=True)
-    gs = (probs * (gp - row)).astype(BF)
-    gq = mm("grqk,kgd->qgrd", gs, k) * factor
-    gk = mm("grqk,qgrd->kgd", gs, q) * factor
-    gv = mm("grqk,qgrd->kgd", probs_low, gm)
-    gq = rotate(gq.reshape(T, QUERY_HEADS, HEAD_SIZE), c, -s).reshape(T, QW)
-    gk = rotate(gk, c, -s).reshape(T, KW)
-    gproj = jnp.concatenate([gq, gk, gv.reshape(T, KW)], 1).astype(BF)
-    grad_qkv_w = jnp.dot(attn_in.T, gproj, preferred_element_type=F32)
-    gattn = jnp.dot(gproj, qkv_full.T, preferred_element_type=F32)
-    gt, grad_gain_one = norm_back(gattn, n1, r1, gain_one)
-    grad_tokens = (grad_hidden + gt).astype(BF)
-
-    big = jnp.concatenate([grad_qkv_w.astype(BF), grad_out_w.astype(BF)], 1)
-    big = lax.psum_scatter(big, ("fsdp", "dp"), scatter_dimension=0, tiled=True)
-    big = lax.all_gather(big, "dp", axis=0, tiled=True).astype(F32)
-    tiny = jnp.concatenate([grad_router, grad_gain_one[:, None], grad_gain_two[:, None]], 1)
-    tiny = lax.psum_scatter(tiny, "fsdp", scatter_dimension=0, tiled=True)
-    tiny = lax.psum(tiny, "dp")
+    ffn_in, hidden, gates, mixed, qk, v, probs, full, cot_all, rt = front(
+        nf, nd, experts, tokens, packed, small, cotangent, slots, cosr, sinr)
+    side = jnp.concatenate([slots.reshape(nf, el, T), gates.reshape(nf, el, T)], 1)
+    out_part, gin_part, gp_part, t1, t2 = experts_call(nf, cap, ffn_in, cot_all, side, w_gate, w_up, w_down)
+    output, grad_tokens, shard, smalls, t1, t2 = back(nf, nd, el, (
+        gin_part, out_part, gp_part, t1, t2, tokens, cotangent, hidden, ffn_in, gates, mixed, qk, v, probs, full, rt,
+        cosr, sinr))
+    big = shard.astype(F32)
     return (
         output,
         grad_tokens,
@@ -506,12 +1263,12 @@
         big[:, QW: QW + KW],
         big[:, QW + KW: QW + 2 * KW],
         big[:, QW + 2 * KW:],
-        tiny[:, experts],
-        tiny[:, experts + 1],
-        tiny[:, :experts],
-        terms[0].astype(F32),
-        terms[1].astype(F32),
-        terms[2].astype(F32),
+        smalls[experts],
+        smalls[experts + 1],
+        smalls[:experts].T,
+        t1[:, :, :ff].astype(F32),
+        t1[:, :, ff:].astype(F32),
+        t2.astype(F32),
     )
 
 

time: 862 us -> 526 us (0.61)
  waiting for transfers between devices: 494 us -> 0 us
  Pallas kernels: 109 us -> 491 us
  matrix products: 125 us -> 0.15 us
  blocking collectives: 32.3 us -> 0 us
  other arithmetic: 43.4 us -> 15.5 us
  local copies, waits for them, and re-layouts: 29 us -> 10.5 us
  between operations: 14.7 us -> 0.71 us
    pallas_call x0 -> x2, Pallas kernels: none -> 383 us  [the longest x1 289 us: back(): pl.pallas_call(functools.partial(back_kernel, nf, nd, el, land_hbm), out_...]
    reduce_scatter x3 -> x0, waiting for transfers between devices: 224 us -> none  [the longest x1 119 us: body(): big = lax.psum_scatter(big, ('fsdp', 'dp'), scatter_dimension=0, tiled=True)]
    psum x1 -> x0, waiting for transfers between devices: 194 us -> none  [body(): terms = lax.psum(terms, 'dp')]
    dot_general x21 -> x1, matrix products: 125 us -> 0.15 us  [body(): lax.dot_general(onehot, earlier, (((0,), (0,)), ((), ())), preferred_elem...]
    all_gather x2 -> x0, waiting for transfers between devices: 58.5 us -> none  [the longest x1 40.2 us: body(): ffn_all = lax.all_gather(ffn_in, 'fsdp', axis=0)]
    all_gather x1 -> x0, blocking collectives: 18 us -> none  [body(): side = lax.all_gather(jnp.stack([slots.T, gates.T]), 'fsdp', axis=0)]
    unnamed x8 -> x0, waiting for transfers between devices: 16.8 us -> none
    convert_element_type x8 -> x2, other arithmetic: 25.7 us -> 10.1 us  [the longest x1 6.49 us: body(): t1[:, :, ff:].astype(F32)]
  transfers between devices with their start and end apart: 8 -> 0, of which waited for: 7 -> 0; matrix products, arithmetic and copies ran while one was open for 10% -> 0% of each run, Pallas kernels for 0% -> 0%
where the time goes in v3:
time: 526 us; the launch traced here: 518 us
  Pallas kernels  491 us (93%)
  other arithmetic  15.5 us (3%)
  local copies, waits for them, and re-layouts  10.5 us (2%)
    pallas_call x1, Pallas kernels, back(): pl.pallas_call(functools.partial(back_kernel, nf, nd, el, land_hbm), out_...  289 us
    pallas_call x1, Pallas kernels, front(): pl.pallas_call(functools.partial(front_kernel, nf, nd, experts), out_shap...  109 us
    pallas_call x1, Pallas kernels, experts_call(): pl.pallas_call(functools.partial(experts_kernel, nf, el, cap, capp), out_...  94 us

profile of v3, /device:TPU:10, one launch (start us, length us, event | category | flops | bytes accessed | tf_op | source)
XLA Modules:
  0.0 518.2 jit_solution(16567368368232426065)
XLA Ops:
  0.7 0.1 pad.5.clone
  0.7 0.7 broadcast_in_dim.17
  1.4 0.7 broadcast_in_dim.18
  2.0 0.7 fusion
  2.8 0.1 convolution_select_fusion.slots
  2.9 1.4 maximum_bitcast_fusion.small
  4.3 2.7 pad_maximum_fusion.pk
  7.0 0.0 copy-done.4
  7.0 108.8 %front.1 = (bf16[256,1536]{1,0:T(8,128)(2,1)}, f32[256,1536]{1,0:T(8,128)}, f32[16,256]{1,0:T(8,128)}, bf16[256,1536]{1,0:T(8,128)(2,1)}, bf16[256,2048]{1,0:T(8...) custom-call(bf16[256,1536]{1,0:T(8,128)(2,1)} %refs_5_.1, ...), custom_call_target="tpu_custom_call" | custom-call | flops 4000000000 | bytes 60000000 | tf_op jit(solution)/shard_map/front/pallas_call | solution.py:340
  115.8 0.7 reshape.32
  116.5 0.6 pad_maximum_fusion.1.side
  117.2 94.0 %experts.1 = (bf16[8,256,1536]{2,1,0:T(8,128)(2,1)}, bf16[8,256,1536]{2,1,0:T(8,128)(2,1)}, f32[8,2,256]{2,1,0:T(2,128)}, bf16[2,1536,1024]{2,1,0:T(8,128)(2,1)}, bf16[2,512,1536]{2,1,0:T(8,128)(2,1)}) custom-call(bf16[256,1536]{1,0:T(8,128)(2,1)} %get-tuple-element.33.ffn.refs_8_, bf16[8,256,1536]{2,1,0:T(8,128)(2,1)} %get-tuple-element.34.cot_a, ...), custom_call_target="tpu_custom_call" | custom-call | flops 40000000000 | bytes 60000000 | tf_op jit(solution)/shard_map/experts/pallas_call | solution.py:595
  211.2 288.6 %back.1 = (bf16[256,1536]{1,0:T(8,128)(2,1)}, bf16[256,1536]{1,0:T(8,128)(2,1)}, bf16[192,4096]{1,0:T(8,128)(2,1)}, f32[24,192]{1,0:T(8,128)}, bf16[2,1536,1024]...) custom-call(bf16[8,256,1536]{2,1,0:T(8,128)(2,1)} %get-tuple-element, ...), custom_call_target="tpu_custom_call" | custom-call | flops 8000000000 | bytes 90000000 | tf_op jit(solution)/shard_map/back/pallas_call | solution.py:1219
  499.8 0.0 copy-start
  499.8 1.4 fusion.3
  501.2 1.3 slice_bitcast_fusion
  502.5 2.1 fusion.2
  504.7 0.0 copy-done
  504.7 1.7 fusion.1
  506.4 0.0 copy-done.1
  506.4 3.6 convert_element_type.22
  510.0 6.5 %slice_convert_fusion = (f32[2,1536,512]{2,1,0:T(8,128)}, f32[2,1536,512]{2,1,0:T(8,128)}) fusion(bf16[2,1536,1024]{2,1,0:T(8,128)(2,1)S(1)} %bitcast.10), kind=kLoop, calls=%fused_computation | loop fusion | flops 3145728 | bytes 18874368 | tf_op jit(solution)/shard_map/convert_element_type | solution.py:1270
  516.5 0.9 copy.30
  517.4 0.9 copy.31
  (13 shorter events, 0.0 us)
Async XLA Ops:
  2.9 4.1 copy-start.4
  499.8 4.9 copy-start
  502.5 3.8 copy-start.1
  504.7 5.3 %slice-start = ((s8[6291456]{0:T(1024)(128)(4,1)}), s8[4194304]{0:T(1024)(128)(4,1)S(1)}, s32[]{:S(2)}) async-start(s8[6291456]{0:T(1024)(128)(4,1)} %bitcast.9), calls=%async_computation | async-start | bytes 8388608
  506.4 3.6 slice-start.1
  510.0 6.5 %copy-start.3 = (bf16[256,1536]{1,0:T(8,128)(2,1)S(1)}, bf16[256,1536]{1,0:T(8,128)(2,1)}, u32[]{:S(2)}) copy-start(bf16[256,1536]{1,0:T(8,128)(2,1)} %get-tuple-element.74) | copy-start | bytes 2359300
  510.0 7.4 %copy-start.2 = (bf16[256,1536]{1,0:T(8,128)(2,1)S(1)}, bf16[256,1536]{1,0:T(8,128)(2,1)}, u32[]{:S(2)}) copy-start(bf16[256,1536]{1,0:T(8,128)(2,1)} %get-tuple-element.75) | copy-start | bytes 2359300

commit v4 on v3

--- a/solution.py
+++ b/solution.py
@@ -82,15 +82,16 @@
     return ((a0, a1), (b0, b1))
 
 
-def front_kernel(nf, nd, experts, tok, pk, small, cot, slots, cosr, sinr,
+def front_kernel(nf, nd, experts, tok, wq, wk, wv, wo, small, cot, slots, cosr, sinr,
                  ffn_o, hid_o, gates_o, mix_o, qk_o, v_o, prob_o, wf_o, cot_o, rt_o,
                  wf, sm, attn, rot,
-                 s_sm, r_sm, s_z, r_z, s_dp, r_dp, s_sib, r_sib, s_cz, r_cz, s_cs, r_cs, s_loc):
+                 s_sm, r_sm, s_z, r_z, s_dp, r_dp, s_sib, r_sib, s_cz, r_cz, s_cs, r_cs, s_loc, s_w):
     T, D = tok.shape
     C = nf // 2
-    R = pk.shape[0]
-    W = pk.shape[1]
-    Wq = W // nd
+    R = wq.shape[0]
+    W = wf.shape[1]
+    WA = 3 * W // 4
+    parts = ((0, WA), (WA, W - WA))
     f = lax.axis_index("fsdp")
     d = lax.axis_index("dp")
     c = f // 2
@@ -101,8 +102,9 @@
     def rows(ff):
         return pl.ds(pl.multiple_of(ff * R, 16), R)
 
-    def cols(dd):
-        return pl.ds(pl.multiple_of(dd * Wq, 128), Wq)
+    def cols(dd, g):
+        at, n = parts[g]
+        return pl.ds(pl.multiple_of(at + dd * (n // nd), 128), n // nd)
 
     def remote(src, dst, ss, rs, to_f, to_d):
         return pltpu.make_async_remote_copy(src_ref=src, dst_ref=dst, send_sem=ss, recv_sem=rs,
@@ -120,16 +122,28 @@
     def nxt_f(dr):
         return f + 2 if dr == 0 else f - 2
 
-    def wz(dr, s, own):
-        ff = 2 * src_chip(dr, s - 1) + k
-        dst = wf.at[rows(ff), cols(d)]
-        src = pk.at[:, cols(d)] if own else dst
-        return remote(src, dst, s_z.at[dr, s - 1], r_z.at[dr, s - 1], nxt_f(dr), d)
-
-    def wz_in(dr, s):
-        ff = 2 * src_chip(dr, s) + k
-        blk = wf.at[rows(ff), cols(d)]
-        return remote(blk, blk, s_z.at[dr, s - 1], r_z.at[dr, s - 1], f, d)
+    def wz(dr, s, g):
+        blk = wf.at[rows(2 * src_chip(dr, s - 1) + k), cols(d, g)]
+        return remote(blk, blk, s_z.at[g, dr, s - 1], r_z.at[g, dr, s - 1], nxt_f(dr), d)
+
+    def wz_in(dr, s, g):
+        blk = wf.at[rows(2 * src_chip(dr, s) + k), cols(d, g)]
+        return remote(blk, blk, s_z.at[g, dr, s - 1], r_z.at[g, dr, s - 1], f, d)
+
+    at = 0
+    w_own = []
+    for i, w in enumerate((wq, wk, wv, wo)):
+        w_own.append(pltpu.make_async_copy(w, wf.at[rows(f), at:at + w.shape[1]], s_w.at[i]))
+        at += w.shape[1]
+    for cp in w_own:
+        cp.start()
+    for cp in w_own:
+        cp.wait()
+    for g in range(2):
+        for dr in range(2):
+            @pl.when(nxt_ok(dr))
+            def _():
+                wz(dr, 1, g).start()
 
     own_small = pltpu.make_async_copy(small, sm.at[f], s_loc.at[0])
     own_small.start()
@@ -138,35 +152,29 @@
         cp = remote(small, sm.at[f], s_sm.at[i - 1], r_sm.at[i - 1], lax.rem(f + i, nf), d)
         cp.start()
         sm_copies.append(cp)
-    for dr in range(2):
-        @pl.when(nxt_ok(dr))
-        def _():
-            wz(dr, 1, True).start()
-    sib_own = remote(pk, wf.at[rows(f)], s_sib.at[0, 0], r_sib.at[0, 0], sib, d)
+    sib_own = remote(wf.at[rows(f)], wf.at[rows(f)], s_sib.at[0, 0, 0], r_sib.at[0, 0, 0], sib, d)
     sib_own.start()
-    own_w = pltpu.make_async_copy(pk, wf.at[rows(f)], s_loc.at[1])
-    own_w.start()
     own_c = pltpu.make_async_copy(cot, cot_o.at[f], s_loc.at[2])
     own_c.start()
     sib_c = remote(cot, cot_o.at[f], s_cs.at[0, 0], r_cs.at[0, 0], sib, d)
 
-    def dp_copy(dr, s, i):
-        ff = 2 * src_chip(dr, s) + k
-        blk = wf.at[rows(ff), cols(d)]
-        return remote(blk, blk, s_dp.at[dr, s - 1, i - 1], r_dp.at[dr, s - 1, i - 1], f, jnp.bitwise_xor(d, i))
-
-    def dp_in(dr, s, i):
-        ff = 2 * src_chip(dr, s) + k
-        blk = wf.at[rows(ff), cols(jnp.bitwise_xor(d, i))]
-        return remote(blk, blk, s_dp.at[dr, s - 1, i - 1], r_dp.at[dr, s - 1, i - 1], f, d)
-
-    def sib_copy(dr, s):
-        blk = wf.at[rows(2 * src_chip(dr, s) + k)]
-        return remote(blk, blk, s_sib.at[dr, s], r_sib.at[dr, s], sib, d)
-
-    def sib_in(dr, s):
-        blk = wf.at[rows(2 * src_chip(dr, s) + 1 - k)]
-        return remote(blk, blk, s_sib.at[dr, s], r_sib.at[dr, s], sib, d)
+    def dp_copy(dr, s, g, i):
+        blk = wf.at[rows(2 * src_chip(dr, s) + k), cols(d, g)]
+        return remote(blk, blk, s_dp.at[g, dr, s - 1, i - 1], r_dp.at[g, dr, s - 1, i - 1], f, jnp.bitwise_xor(d, i))
+
+    def dp_in(dr, s, g, i):
+        blk = wf.at[rows(2 * src_chip(dr, s) + k), cols(jnp.bitwise_xor(d, i), g)]
+        return remote(blk, blk, s_dp.at[g, dr, s - 1, i - 1], r_dp.at[g, dr, s - 1, i - 1], f, d)
+
+    def sib_copy(dr, s, g):
+        at, n = parts[g]
+        blk = wf.at[rows(2 * src_chip(dr, s) + k), at:at + n]
+        return remote(blk, blk, s_sib.at[g, dr, s], r_sib.at[g, dr, s], sib, d)
+
+    def sib_in(dr, s, g):
+        at, n = parts[g]
+        blk = wf.at[rows(2 * src_chip(dr, s) + 1 - k), at:at + n]
+        return remote(blk, blk, s_sib.at[g, dr, s], r_sib.at[g, dr, s], sib, d)
 
     def cz(dr, s, own):
         ff = 2 * src_chip(dr, s - 1) + k
@@ -186,21 +194,44 @@
         return remote(cot_o.at[ff], cot_o.at[ff], s_cs.at[dr, s], r_cs.at[dr, s], sib, d)
 
     for s in range(1, C):
-        for dr in range(2):
-            @pl.when(has(dr, s))
-            def _():
-                wz_in(dr, s).wait_recv()
-                if s < C - 1:
-                    @pl.when(nxt_ok(dr))
-                    def _():
-                        wz(dr, s + 1, False).start()
-                for i in range(1, nd):
-                    dp_copy(dr, s, i).start()
+        for g in range(2):
+            for dr in range(2):
+                @pl.when(has(dr, s))
+                def _():
+                    wz_in(dr, s, g).wait_recv()
+                    if s < C - 1:
+                        @pl.when(nxt_ok(dr))
+                        def _():
+                            wz(dr, s + 1, g).start()
+                    if g == 0:
+                        for i in range(1, nd):
+                            dp_copy(dr, s, g, i).start()
     for dr in range(2):
         @pl.when(nxt_ok(dr))
         def _():
             cz(dr, 1, True).start()
     sib_c.start()
+    for s in range(1, C):
+        for dr in range(2):
+            @pl.when(has(dr, s))
+            def _():
+                for i in range(1, nd):
+                    dp_copy(dr, s, 1, i).start()
+
+    def group_in(s, g):
+        for dr in range(2):
+            @pl.when(has(dr, s))
+            def _():
+                for i in range(1, nd):
+                    dp_in(dr, s, g, i).wait_recv()
+                sib_copy(dr, s, g).start()
+
+    def cores_in(g):
+        for s in range(1, C):
+            for dr in range(2):
+                @pl.when(has(dr, s))
+                def _():
+                    sib_in(dr, s, g).wait_recv()
 
     own_small.wait()
     for cp in sm_copies:
@@ -214,17 +245,6 @@
     r1 = lax.rsqrt(jnp.mean(xf * xf, -1, keepdims=True) + EPSILON)
     attn[...] = (xf * r1 * gain_one).astype(BF)
 
-    for s in range(1, C):
-        for dr in range(2):
-            @pl.when(has(dr, s))
-            def _():
-                for i in range(1, nd):
-                    dp_in(dr, s, i).wait_recv()
-                sib_copy(dr, s).start()
-        for dr in range(2):
-            if s < C - 1:
-                pass
-
     def cot_step(s):
         for dr in range(2):
             @pl.when(has(dr, s))
@@ -236,16 +256,12 @@
                         cz(dr, s + 1, False).start()
                 cs(dr, s).start()
 
+    for s in range(1, C - 1):
+        group_in(s, 0)
     cot_step(1)
+    group_in(C - 1, 0)
     sib_own.wait()
-    own_w.wait()
-    for s in range(1, C):
-        for dr in range(2):
-            @pl.when(has(dr, s))
-            def _():
-                sib_in(dr, s).wait_recv()
-    out_w = pltpu.make_async_copy(wf, wf_o, s_loc.at[3])
-    out_w.start()
+    cores_in(0)
 
     first = lax.rem(lax.broadcasted_iota(jnp.int32, (T, 256), 1), HEAD_SIZE) < HEAD_SIZE // 2
     cs_t = jnp.concatenate([cosr[...], cosr[...]], 1)
@@ -290,8 +306,11 @@
                 acc = term if acc is None else acc + term
             mix_o[:, qc] = acc.astype(BF)
 
-    for s in range(3, C):
-        cot_step(s)
+    for s in range(1, C):
+        group_in(s, 1)
+    cores_in(1)
+    out_w = pltpu.make_async_copy(wf, wf_o, s_loc.at[3])
+    out_w.start()
 
     @pl.loop(0, D // 256)
     def _(i):
@@ -308,6 +327,8 @@
     ex = jnp.where(named, jnp.exp(logits - jnp.max(logits, 0, keepdims=True)), 0.0)
     gates_o[...] = ex / jnp.sum(ex, 0, keepdims=True)
 
+    for s in range(3, C):
+        cot_step(s)
     own_c.wait()
     sib_c.wait()
     out_w.wait()
@@ -317,20 +338,22 @@
             def _():
                 cs_in(dr, s).wait_recv()
                 cs(dr, s).wait_send()
-                sib_copy(dr, s).wait_send()
-                for i in range(1, nd):
-                    dp_copy(dr, s, i).wait_send()
+                for g in range(2):
+                    sib_copy(dr, s, g).wait_send()
+                    for i in range(1, nd):
+                        dp_copy(dr, s, g, i).wait_send()
 
             @pl.when(nxt_ok(dr) & (has(dr, s - 1) if s > 1 else True))
             def _():
-                wz(dr, s, s == 1).wait_send()
+                for g in range(2):
+                    wz(dr, s, g).wait_send()
                 cz(dr, s, s == 1).wait_send()
 
 
-def front(nf, nd, experts, tok, pk, small, cot, slots, cosr, sinr):
+def front(nf, nd, experts, tok, ws, small, cot, slots, cosr, sinr):
     T, D = tok.shape
     C = nf // 2
-    W = pk.shape[1]
+    W = sum(w.shape[1] for w in ws)
     out = [
         (T, D, BF, 0), (T, D, F32, 0), (experts, T, F32, 0), (T, QW, BF, 0), (T, QW + KW, BF, 0),
         (T, KW, BF, 0), (QUERY_HEADS, T, T, BF, 0), (D, W, BF, 1), (nf, T, D, BF, 1),
@@ -340,7 +363,7 @@
     return pl.pallas_call(
         functools.partial(front_kernel, nf, nd, experts),
         out_shape=[jax.ShapeDtypeStruct(o[:-2], o[-2]) for o in out],
-        in_specs=[vm()] * 7,
+        in_specs=[vm()] + [hbm()] * 4 + [vm()] * 5,
         out_specs=[hbm() if o[-1] else vm() for o in out],
         scratch_shapes=[
             VMEM((D, W), BF),
@@ -348,19 +371,229 @@
             VMEM((T, D), BF),
             VMEM((8, 128), F32),
             dma((nf,)), dma((nf,)),
-            dma((2, C)), dma((2, C)),
-            dma((2, C, nd)), dma((2, C, nd)),
+            dma((2, 2, C)), dma((2, 2, C)),
+            dma((2, 2, C, nd)), dma((2, 2, C, nd)),
+            dma((2, 2, C)), dma((2, 2, C)),
             dma((2, C)), dma((2, C)),
             dma((2, C)), dma((2, C)),
-            dma((2, C)), dma((2, C)),
-            dma((4,)),
+            dma((4,)), dma((4,)),
         ],
         compiler_params=pltpu.CompilerParams(collective_id=1, has_side_effects=True,
                                              vmem_limit_bytes=60 * 2 ** 20),
         cost_estimate=pl.CostEstimate(flops=4_000_000_000, bytes_accessed=60_000_000, transcendentals=2_000_000),
         name="front",
-    )(tok, pk, small, cot, slots, cosr, sinr)
-
+    )(tok, *ws, small, cot, slots, cosr, sinr)
+
+
+def add_blocks(dst, srcs, extra=None):
+    @pl.loop(0, dst.shape[0] // 16)
+    def _(i):
+        at = pl.ds(pl.multiple_of(i * 16, 16), 16)
+        total = srcs[0][at, :].astype(F32)
+        for s in srcs[1:]:
+            total = total + s[at, :].astype(F32)
+        dst[at, :] = total.astype(dst.dtype)
+
+
+class Line:
+    def __init__(self, nf, f, d, acc, give, sib, rcv, stage, sems, stage_sem, credit=None):
+        self.nf, self.f, self.d = nf, f, d
+        self.C = nf // 2
+        self.c, self.k = f // 2, lax.rem(f, 2)
+        self.acc, self.give, self.sib, self.rcv, self.stage = acc, give, sib, rcv, stage
+        self.s_sib, self.r_sib, self.s_z, self.r_z = sems
+        self.stage_sem, self.credit = stage_sem, credit
+
+    def remote(self, src, dst, ss, rs, to):
+        return pltpu.make_async_remote_copy(src_ref=src, dst_ref=dst, send_sem=ss, recv_sem=rs,
+                                            device_id=(to, self.d), device_id_type=MESH)
+
+    def dest(self, dr, s):
+        i = s - 1 - (self.C - 1 - self.c) if dr == 0 else s - 1 - self.c
+        room = self.c if dr == 0 else self.C - 1 - self.c
+        chip = i if dr == 0 else self.C - 1 - i
+        return jnp.clip(chip, 0, self.C - 1), (i >= 0) & (i < room), i == 0
+
+    def sib_copy(self, chip):
+        return self.remote(self.give(chip), self.sib(chip), self.s_sib.at[chip], self.r_sib.at[chip],
+                           self.f + 1 - 2 * self.k)
+
+    def z_copy(self, dr, s, chip):
+        return self.remote(self.acc(chip), self.rcv(dr, s - 1), self.s_z.at[dr, s - 1], self.r_z.at[dr, s - 1],
+                           self.f - 2 if dr == 0 else self.f + 2)
+
+    def z_in(self, dr, s):
+        return self.remote(self.rcv(dr, s - 1), self.rcv(dr, s - 1), self.s_z.at[dr, s - 1], self.r_z.at[dr, s - 1],
+                           self.f)
+
+    def start_sib(self):
+        if self.credit is not None:
+            pl.semaphore_wait(self.credit.at[2], 1)
+        for s in range(1, self.C):
+            for dr in range(2):
+                chip, ok, _ = self.dest(dr, s)
+
+                @pl.when(ok)
+                def _():
+                    self.sib_copy(chip).start()
+        self.sib_copy(self.c).start()
+
+    def gather(self, chip, srcs):
+        acc = self.acc(chip)
+        if self.stage is None:
+            add_blocks(acc, [acc] + srcs)
+            return
+        for s in srcs:
+            cp = pltpu.make_async_copy(s, self.stage, self.stage_sem)
+            cp.start()
+            cp.wait()
+            add_blocks(acc, [acc, self.stage])
+
+    def step(self, s):
+        for dr in range(2):
+            chip, ok, opening = self.dest(dr, s)
+            begins = (self.c == self.C - 1) if dr == 0 else (self.c == 0)
+
+            @pl.when(ok)
+            def _():
+                self.sib_copy(chip).wait_recv()
+
+                @pl.when(begins)
+                def _():
+                    self.gather(chip, [self.sib(chip)])
+                if s > 1:
+                    @pl.when(jnp.logical_not(begins))
+                    def _():
+                        self.z_in(dr, s - 1).wait_recv()
+                        self.gather(chip, [self.sib(chip), self.rcv(dr, s - 2)])
+                if self.credit is not None:
+                    @pl.when(opening)
+                    def _():
+                        pl.semaphore_wait(self.credit.at[dr], 1)
+                self.z_copy(dr, s, chip).start()
+
+    def last(self):
+        self.sib_copy(self.c).wait_recv()
+        mid = (self.c > 0) & (self.c < self.C - 1)
+        s = self.C - 1
+        for dr in range(2):
+            @pl.when((self.c < self.C - 1) if dr == 0 else (self.c > 0))
+            def _():
+                self.z_in(dr, s).wait_recv()
+
+        @pl.when(mid)
+        def _():
+            self.gather(self.c, [self.sib(self.c), self.rcv(0, s - 1), self.rcv(1, s - 1)])
+
+        @pl.when(self.c == 0)
+        def _():
+            self.gather(self.c, [self.sib(self.c), self.rcv(0, s - 1)])
+
+        @pl.when(self.c == self.C - 1)
+        def _():
+            self.gather(self.c, [self.sib(self.c), self.rcv(1, s - 1)])
+
+    def sent(self):
+        self.sib_copy(self.c).wait_send()
+        for s in range(1, self.C):
+            for dr in range(2):
+                chip, ok, _ = self.dest(dr, s)
+
+                @pl.when(ok)
+                def _():
+                    self.sib_copy(chip).wait_send()
+                    self.z_copy(dr, s, chip).wait_send()
+
+    def free(self, credit):
+        def tell(i, to):
+            pl.semaphore_signal(credit.at[i], inc=1, device_id=(to, self.d), device_id_type=MESH)
+
+        tell(2, self.f + 1 - 2 * self.k)
+
+        @pl.when(self.c < self.C - 1)
+        def _():
+            tell(0, self.f + 2)
+
+        @pl.when(self.c > 0)
+        def _():
+            tell(1, self.f - 2)
+
+
+class Cube:
+    def __init__(self, nd, f, d, flip, lanes, size, own, land, total, out, sems):
+        m = nd.bit_length() - 1
+        self.bits = list(range(m))[::-1] if flip else list(range(m))
+        self.f, self.d, self.lanes = f, d, lanes
+        self.own, self.land, self.total, self.out = own, land, total, out
+        self.ss, self.rs = sems
+        self.m = m
+        self.low, self.length = [0], [size]
+        for b in self.bits:
+            half = self.length[-1] // 2
+            side = lax.rem(d // (1 << b), 2)
+            self.low.append(self.low[-1] + side * half)
+            self.length.append(half)
+
+    def cut(self, ref, at, n):
+        if self.lanes:
+            return ref.at[:, pl.ds(pl.multiple_of(at, 128), n)]
+        return ref.at[pl.ds(pl.multiple_of(at, 16), n)]
+
+    def remote(self, src, dst, i, to_bit):
+        return pltpu.make_async_remote_copy(src_ref=src, dst_ref=dst, send_sem=self.ss.at[i], recv_sem=self.rs.at[i],
+                                            device_id=(self.f, jnp.bitwise_xor(self.d, 1 << to_bit)),
+                                            device_id_type=MESH)
+
+    def level(self, i):
+        if i == 0:
+            return self.own, 0
+        if i == self.m:
+            return self.out, 0
+        return self.total(i - 1), self.low[i]
+
+    def down(self, i):
+        ref, base = self.level(i)
+        half = self.length[i + 1]
+        other = 2 * self.low[i] + half - self.low[i + 1]
+        return self.remote(self.cut(ref, other - base, half), self.land(i), i, self.bits[i])
+
+    def merge(self, i, add):
+        self.down(i).wait_recv()
+        self.fold(i, add)
+
+    def fold(self, i, add):
+        ref, base = self.level(i)
+        dst, dbase = self.level(i + 1)
+        half = self.length[i + 1]
+        low = self.low[i + 1]
+        add(self.cut(dst, low - dbase, half), self.cut(ref, low - base, half), self.land(i))
+
+    def up(self, i):
+        blk = self.cut(self.out, self.low[i + 1], self.length[i + 1])
+        return self.remote(blk, blk, self.m + i, self.bits[i])
+
+    def up_in(self, i):
+        half = self.length[i + 1]
+        other = 2 * self.low[i] + half - self.low[i + 1]
+        blk = self.cut(self.out, other, half)
+        return self.remote(blk, blk, self.m + i, self.bits[i])
+
+    def sent(self, first=0):
+        for i in range(self.m):
+            if i >= first:
+                self.down(i).wait_send()
+            self.up(i).wait_send()
+
+
+def pipe_add(dst, a, b):
+    n, w = dst.shape
+    tile = 128 if n % 128 == 0 else 64
+    spec = pl.BlockSpec((tile, w), lambda i: (i, 0))
+
+    def inner(a_ref, b_ref, o_ref):
+        o_ref[...] = (a_ref[...].astype(F32) + b_ref[...].astype(F32)).astype(o_ref.dtype)
+
+    pltpu.emit_pipeline(inner, grid=(n // tile,), in_specs=[spec, spec], out_specs=[spec])(a, b, dst)
 
 def visit(c, C, j):
     both = jnp.minimum(c, C - 1 - c)
@@ -371,10 +604,21 @@
     return chip, jnp.where(down, 1, 0), dist
 
 
-def experts_kernel(nf, el, cap, capp, ffn, cot_a, side, wg_h, wu_h, wd_h,
-                   out_o, gin_o, gp_o, t1_o, t2_o,
-                   wg, wu, wd, fa, sd, cotb, xs, gs, hs, hgs, orb, irb, st_o, st_i, st1, st2,
-                   s_sd, r_sd, s_z, r_z, s_sib, r_sib, s_w, s_loc, s_t):
+def term_cubes(nd, el, f, d, t1, t2, out1, out2, l1, l2, a1, a2, sems):
+    cubes = []
+    for e in range(el):
+        for j, (src, out, ls, ts) in enumerate(((t1, out1, l1, a1), (t2, out2, l2, a2))):
+            pick = functools.partial(lambda refs, e, i: refs[i].at[e], ls, e)
+            tot = functools.partial(lambda refs, e, i: refs[i].at[e], ts, e)
+            cubes.append(Cube(nd, f, d, (e + j) % 2 == 1, False, src.shape[1], src.at[e], pick, tot,
+                              None if out is None else out.at[e], (sems[0].at[2 * e + j], sems[1].at[2 * e + j])))
+    return cubes
+
+
+def experts_kernel(nf, nd, el, cap, capp, land_hbm, ffn, cot_a, side, wg_h, wu_h, wd_h,
+                   out_o, gin_o, gp_o, t1_o, t2_o, l1, l2, sib_l, rcv_l, acc,
+                   wg, wu, wd, fa, sd, cotb, xs, gs, hs, hgs, orb, irb, st_o, give, st1, st2, stage,
+                   s_sd, r_sd, s_z, r_z, s_sib, r_sib, s_w, s_loc, s_t, s_ls, r_ls, s_lz, r_lz, s_st, s_cube, r_cube):
     T, D = ffn.shape
     FFW = wg.shape[2]
     C = nf // 2
@@ -384,7 +628,7 @@
     c = f // 2
     k = lax.rem(f, 2)
     sib = f + 1 - 2 * k
-    greet(nf, 1, f, d)
+    greet(nf, nd, f, d)
 
     def remote(src, dst, ss, rs, to_f):
         return pltpu.make_async_remote_copy(src_ref=src, dst_ref=dst, send_sem=ss, recv_sem=rs,
@@ -421,6 +665,12 @@
     def sib_in(dr, s):
         ff = 2 * chip_at(dr, s) + 1 - k
         return remote(fa.at[ff], fa.at[ff], s_sib.at[dr, s], r_sib.at[dr, s], f)
+
+    line = Line(nf, f, d, lambda ch: acc.at[ch], lambda ch: give.at[0], lambda ch: sib_l.at[ch],
+                lambda dr, s: rcv_l.at[dr, s], stage if land_hbm else None, (s_ls, r_ls, s_lz, r_lz), s_st)
+
+    def handed(chip, slot):
+        return remote(give.at[slot], sib_l.at[chip], s_ls.at[chip], r_ls.at[chip], sib)
 
     for dr in range(2):
         @pl.when(nxt_ok(dr))
@@ -517,14 +767,32 @@
                     orb[kk, e * capp:(e + 1) * capp, n:n + 512] = orow[kk * capp:(kk + 1) * capp]
                     irb[kk, e * capp:(e + 1) * capp, n:n + 512] = irow[kk * capp:(kk + 1) * capp]
 
+        @pl.when(j >= 2)
+        def _():
+            before, _, _ = visit(c, C, j - 2)
+            handed(before, lax.rem(j, 2)).wait_send()
+        for kk in range(2):
+            s = 2 * b + kk
+
+            def combine(dst):
+                for n in range(0, D, 512):
+                    dst[:, n:n + 512] = dot_tn(picks[kk], irb[kk, :, n:n + 512]).astype(BF)
+
+            @pl.when(k == kk)
+            def _():
+                combine(acc.at[b])
+
+            @pl.when(k != kk)
+            def _():
+                combine(give.at[lax.rem(j, 2)])
+                handed(b, lax.rem(j, 2)).start()
+
         def back(bb):
-            return (pltpu.make_async_copy(st_o, out_o.at[pl.ds(2 * bb, 2)], s_loc.at[3]),
-                    pltpu.make_async_copy(st_i, gin_o.at[pl.ds(2 * bb, 2)], s_loc.at[4]))
+            return pltpu.make_async_copy(st_o, out_o.at[pl.ds(2 * bb, 2)], s_loc.at[3])
 
         @pl.when(j >= 1)
         def _():
-            for cp in back(0):
-                cp.wait()
+            back(0).wait()
         for kk in range(2):
             s = 2 * b + kk
             for e in range(el):
@@ -532,9 +800,9 @@
                 gp_o[s, e:e + 1, :] = jnp.sum(hit * gp_rows[e][kk * capp:(kk + 1) * capp], 0, keepdims=True)
             for n in range(0, D, 512):
                 st_o[kk, :, n:n + 512] = dot_tn(picks[kk], orb[kk, :, n:n + 512]).astype(BF)
-                st_i[kk, :, n:n + 512] = dot_tn(picks[kk], irb[kk, :, n:n + 512]).astype(BF)
-        for cp in back(b):
-            cp.start()
+        back(b).start()
+
+    line.step(1)
 
     n1 = D // 256
     n2 = FFW // 256
@@ -547,6 +815,7 @@
         return pltpu.make_async_copy(st2.at[lax.rem(i, 2)], t2_o.at[e, pl.ds(pl.multiple_of(i * 256, 256), 256)],
                                      s_t.at[1, lax.rem(i, 2)])
 
+    cubes = term_cubes(nd, el, f, d, t1_o, t2_o, None, None, [l1], [l2], [], [], (s_cube, r_cube))
     for e in range(el):
         @pl.loop(0, n1)
         def _(i):
@@ -556,6 +825,10 @@
             col = pl.ds(pl.multiple_of(i * 256, 256), 256)
             st1[lax.rem(i, 2)] = dot_tn(xs[e, :, col], hs[e]).astype(BF)
             t1_copy(e, i).start()
+
+        for i in range(2):
+            t1_copy(e, i).wait()
+        cubes[2 * e].down(0).start()
 
         @pl.loop(0, n2)
         def _(i):
@@ -566,11 +839,31 @@
             st2[lax.rem(i, 2)] = dot_tn(hgs[e, :, col], gs[e]).astype(BF)
             t2_copy(e, i).start()
         for i in range(2):
-            t1_copy(e, i).wait()
             t2_copy(e, i).wait()
+        cubes[2 * e + 1].down(0).start()
+        if e < C - 2:
+            line.step(e + 2)
+
+    for s in range(el + 2, C):
+        line.step(s)
+    for s in range(C - 2, el):
+        pass
+    line.last()
+    gin_o[...] = acc[c]
 
     pltpu.make_async_copy(st_o, out_o.at[pl.ds(0, 2)], s_loc.at[3]).wait()
-    pltpu.make_async_copy(st_i, gin_o.at[pl.ds(0, 2)], s_loc.at[4]).wait()
+    for j in range(max(C - 2, 0), C):
+        chip, _, _ = visit(c, C, j)
+        handed(chip, j % 2).wait_send()
+    for s in range(1, C):
+        for dr in range(2):
+            chip, ok, _ = line.dest(dr, s)
+
+            @pl.when(ok)
+            def _():
+                line.z_copy(dr, s, chip).wait_send()
+    for cube in cubes:
+        cube.down(0).wait()
     sib_own.wait_send()
     for dr in range(2):
         for s in range(1, C):
@@ -583,244 +876,50 @@
                 z_out(dr, s).wait_send()
 
 
-def experts_call(nf, cap, ffn_in, cot_all, side, w_gate, w_up, w_down):
+def experts_call(nf, nd, cap, ffn_in, cot_all, side, w_gate, w_up, w_down):
     T, D = ffn_in.shape
     el, _, FFW = w_gate.shape
     capp = cap + (-cap % 16)
     C = nf // 2
     rows = C * 2 * capp
+    land_hbm = C > 4
     dma = pltpu.SemaphoreType.DMA
-    out = [((nf, T, D), BF, 1), ((nf, T, D), BF, 1), ((nf, el, T), F32, 0),
-           ((el, D, 2 * FFW), BF, 1), ((el, FFW, D), BF, 1)]
+    out = [((nf, T, D), BF, 1), ((T, D), BF, 0), ((nf, el, T), F32, 0),
+           ((el, D, 2 * FFW), BF, 1), ((el, FFW, D), BF, 1),
+           ((el, D // 2, 2 * FFW), BF, 1), ((el, FFW // 2, D), BF, 1)]
+    lands = [(C, T, D), (2, C - 1, T, D)]
+    scratch = []
+    if land_hbm:
+        out += [(x, BF, 1) for x in lands]
+    else:
+        scratch += [VMEM(x, BF) for x in lands]
+    scratch += [
+        VMEM((C, T, D), BF),
+        VMEM((el, D, FFW), BF), VMEM((el, D, FFW), BF), VMEM((el, FFW, D), BF),
+        VMEM((nf, T, D), BF), VMEM(side.shape, F32), VMEM((2, T, D), BF),
+        VMEM((el, rows, D), BF), VMEM((el, rows, D), BF),
+        VMEM((el, rows, 2 * FFW), BF), VMEM((el, rows, FFW), BF),
+        VMEM((2, el * capp, D), BF), VMEM((2, el * capp, D), BF),
+        VMEM((2, T, D), BF), VMEM((2, T, D), BF),
+        VMEM((2, 256, 2 * FFW), BF), VMEM((2, 256, D), BF),
+        VMEM((T, D) if land_hbm else (16, 128), BF),
+        dma((nf,)), dma((nf,)),
+        dma((2, C)), dma((2, C)), dma((2, C)), dma((2, C)),
+        dma((3,)), dma((5,)), dma((2, 2)),
+        dma((C,)), dma((C,)), dma((2, C)), dma((2, C)), dma(()),
+        dma((2 * el, 2 * (nd.bit_length() - 1))), dma((2 * el, 2 * (nd.bit_length() - 1))),
+    ]
     return pl.pallas_call(
-        functools.partial(experts_kernel, nf, el, cap, capp),
+        functools.partial(experts_kernel, nf, nd, el, cap, capp, land_hbm),
         out_shape=[jax.ShapeDtypeStruct(o[0], o[1]) for o in out],
         in_specs=[vm(), hbm(), vm(), hbm(), hbm(), hbm()],
         out_specs=[hbm() if o[2] else vm() for o in out],
-        scratch_shapes=[
-            VMEM((el, D, FFW), BF), VMEM((el, D, FFW), BF), VMEM((el, FFW, D), BF),
-            VMEM((nf, T, D), BF), VMEM(side.shape, F32), VMEM((2, T, D), BF),
-            VMEM((el, rows, D), BF), VMEM((el, rows, D), BF),
-            VMEM((el, rows, 2 * FFW), BF), VMEM((el, rows, FFW), BF),
-            VMEM((2, el * capp, D), BF), VMEM((2, el * capp, D), BF),
-            VMEM((2, T, D), BF), VMEM((2, T, D), BF),
-            VMEM((2, 256, 2 * FFW), BF), VMEM((2, 256, D), BF),
-            dma((nf,)), dma((nf,)),
-            dma((2, C)), dma((2, C)), dma((2, C)), dma((2, C)),
-            dma((3,)), dma((5,)), dma((2, 2)),
-        ],
+        scratch_shapes=scratch,
         compiler_params=pltpu.CompilerParams(collective_id=2, has_side_effects=True,
-                                             vmem_limit_bytes=62 * 2 ** 20),
+                                             vmem_limit_bytes=63 * 2 ** 20),
         cost_estimate=pl.CostEstimate(flops=40_000_000_000, bytes_accessed=60_000_000, transcendentals=2_000_000),
         name="experts",
-    )(ffn_in, cot_all, side, w_gate, w_up, w_down)
-
-
-def add_blocks(dst, srcs, extra=None):
-    @pl.loop(0, dst.shape[0] // 16)
-    def _(i):
-        at = pl.ds(pl.multiple_of(i * 16, 16), 16)
-        total = srcs[0][at, :].astype(F32)
-        for s in srcs[1:]:
-            total = total + s[at, :].astype(F32)
-        dst[at, :] = total.astype(dst.dtype)
-
-
-class Line:
-    def __init__(self, nf, f, d, acc, give, sib, rcv, stage, sems, stage_sem, credit=None):
-        self.nf, self.f, self.d = nf, f, d
-        self.C = nf // 2
-        self.c, self.k = f // 2, lax.rem(f, 2)
-        self.acc, self.give, self.sib, self.rcv, self.stage = acc, give, sib, rcv, stage
-        self.s_sib, self.r_sib, self.s_z, self.r_z = sems
-        self.stage_sem, self.credit = stage_sem, credit
-
-    def remote(self, src, dst, ss, rs, to):
-        return pltpu.make_async_remote_copy(src_ref=src, dst_ref=dst, send_sem=ss, recv_sem=rs,
-                                            device_id=(to, self.d), device_id_type=MESH)
-
-    def dest(self, dr, s):
-        i = s - 1 - (self.C - 1 - self.c) if dr == 0 else s - 1 - self.c
-        room = self.c if dr == 0 else self.C - 1 - self.c
-        chip = i if dr == 0 else self.C - 1 - i
-        return jnp.clip(chip, 0, self.C - 1), (i >= 0) & (i < room), i == 0
-
-    def sib_copy(self, chip):
-        return self.remote(self.give(chip), self.sib(chip), self.s_sib.at[chip], self.r_sib.at[chip],
-                           self.f + 1 - 2 * self.k)
-
-    def z_copy(self, dr, s, chip):
-        return self.remote(self.acc(chip), self.rcv(dr, s - 1), self.s_z.at[dr, s - 1], self.r_z.at[dr, s - 1],
-                           self.f - 2 if dr == 0 else self.f + 2)
-
-    def z_in(self, dr, s):
-        return self.remote(self.rcv(dr, s - 1), self.rcv(dr, s - 1), self.s_z.at[dr, s - 1], self.r_z.at[dr, s - 1],
-                           self.f)
-
-    def start_sib(self):
-        if self.credit is not None:
-            pl.semaphore_wait(self.credit.at[2], 1)
-        for s in range(1, self.C):
-            for dr in range(2):
-                chip, ok, _ = self.dest(dr, s)
-
-                @pl.when(ok)
-                def _():
-                    self.sib_copy(chip).start()
-        self.sib_copy(self.c).start()
-
-    def gather(self, chip, srcs):
-        acc = self.acc(chip)
-        if self.stage is None:
-            add_blocks(acc, [acc] + srcs)
-            return
-        for s in srcs:
-            cp = pltpu.make_async_copy(s, self.stage, self.stage_sem)
-            cp.start()
-            cp.wait()
-            add_blocks(acc, [acc, self.stage])
-
-    def step(self, s):
-        for dr in range(2):
-            chip, ok, opening = self.dest(dr, s)
-            begins = (self.c == self.C - 1) if dr == 0 else (self.c == 0)
-
-            @pl.when(ok)
-            def _():
-                self.sib_copy(chip).wait_recv()
-
-                @pl.when(begins)
-                def _():
-                    self.gather(chip, [self.sib(chip)])
-                if s > 1:
-                    @pl.when(jnp.logical_not(begins))
-                    def _():
-                        self.z_in(dr, s - 1).wait_recv()
-                        self.gather(chip, [self.sib(chip), self.rcv(dr, s - 2)])
-                if self.credit is not None:
-                    @pl.when(opening)
-                    def _():
-                        pl.semaphore_wait(self.credit.at[dr], 1)
-                self.z_copy(dr, s, chip).start()
-
-    def last(self):
-        self.sib_copy(self.c).wait_recv()
-        mid = (self.c > 0) & (self.c < self.C - 1)
-        s = self.C - 1
-        for dr in range(2):
-            @pl.when((self.c < self.C - 1) if dr == 0 else (self.c > 0))
-            def _():
-                self.z_in(dr, s).wait_recv()
-
-        @pl.when(mid)
-        def _():
-            self.gather(self.c, [self.sib(self.c), self.rcv(0, s - 1), self.rcv(1, s - 1)])
-
-        @pl.when(self.c == 0)
-        def _():
-            self.gather(self.c, [self.sib(self.c), self.rcv(0, s - 1)])
-
-        @pl.when(self.c == self.C - 1)
-        def _():
-            self.gather(self.c, [self.sib(self.c), self.rcv(1, s - 1)])
-
-    def sent(self):
-        self.sib_copy(self.c).wait_send()
-        for s in range(1, self.C):
-            for dr in range(2):
-                chip, ok, _ = self.dest(dr, s)
-
-                @pl.when(ok)
-                def _():
-                    self.sib_copy(chip).wait_send()
-                    self.z_copy(dr, s, chip).wait_send()
-
-    def free(self, credit):
-        def tell(i, to):
-            pl.semaphore_signal(credit.at[i], inc=1, device_id=(to, self.d), device_id_type=MESH)
-
-        tell(2, self.f + 1 - 2 * self.k)
-
-        @pl.when(self.c < self.C - 1)
-        def _():
-            tell(0, self.f + 2)
-
-        @pl.when(self.c > 0)
-        def _():
-            tell(1, self.f - 2)
-
-
-class Cube:
-    def __init__(self, nd, f, d, flip, lanes, size, own, land, total, out, sems):
-        m = nd.bit_length() - 1
-        self.bits = list(range(m))[::-1] if flip else list(range(m))
-        self.f, self.d, self.lanes = f, d, lanes
-        self.own, self.land, self.total, self.out = own, land, total, out
-        self.ss, self.rs = sems
-        self.m = m
-        self.low, self.length = [0], [size]
-        for b in self.bits:
-            half = self.length[-1] // 2
-            side = lax.rem(d // (1 << b), 2)
-            self.low.append(self.low[-1] + side * half)
-            self.length.append(half)
-
-    def cut(self, ref, at, n):
-        if self.lanes:
-            return ref.at[:, pl.ds(pl.multiple_of(at, 128), n)]
-        return ref.at[pl.ds(pl.multiple_of(at, 16), n)]
-
-    def remote(self, src, dst, i, to_bit):
-        return pltpu.make_async_remote_copy(src_ref=src, dst_ref=dst, send_sem=self.ss.at[i], recv_sem=self.rs.at[i],
-                                            device_id=(self.f, jnp.bitwise_xor(self.d, 1 << to_bit)),
-                                            device_id_type=MESH)
-
-    def level(self, i):
-        if i == 0:
-            return self.own, 0
-        if i == self.m:
-            return self.out, 0
-        return self.total(i - 1), self.low[i]
-
-    def down(self, i):
-        ref, base = self.level(i)
-        half = self.length[i + 1]
-        other = 2 * self.low[i] + half - self.low[i + 1]
-        return self.remote(self.cut(ref, other - base, half), self.land(i), i, self.bits[i])
-
-    def merge(self, i, add):
-        self.down(i).wait_recv()
-        ref, base = self.level(i)
-        dst, dbase = self.level(i + 1)
-        half = self.length[i + 1]
-        low = self.low[i + 1]
-        add(self.cut(dst, low - dbase, half), self.cut(ref, low - base, half), self.land(i))
-
-    def up(self, i):
-        blk = self.cut(self.out, self.low[i + 1], self.length[i + 1])
-        return self.remote(blk, blk, self.m + i, self.bits[i])
-
-    def up_in(self, i):
-        half = self.length[i + 1]
-        other = 2 * self.low[i] + half - self.low[i + 1]
-        blk = self.cut(self.out, other, half)
-        return self.remote(blk, blk, self.m + i, self.bits[i])
-
-    def sent(self):
-        for i in range(self.m):
-            self.down(i).wait_send()
-            self.up(i).wait_send()
-
-
-def pipe_add(dst, a, b):
-    n, w = dst.shape
-    tile = 32
-    spec = pl.BlockSpec((tile, w), lambda i: (i, 0))
-
-    def inner(a_ref, b_ref, o_ref):
-        o_ref[...] = (a_ref[...].astype(F32) + b_ref[...].astype(F32)).astype(o_ref.dtype)
-
-    pltpu.emit_pipeline(inner, grid=(n // tile,), in_specs=[spec, spec], out_specs=[spec])(a, b, dst)
+    )(ffn_in, cot_all, side, w_gate, w_up, w_down)[:7]
 
 
 def back_kernel(nf, nd, el, land_hbm, *refs):
@@ -830,11 +929,11 @@
     def take(n):
         return [next(it) for _ in range(n)]
 
-    (gin_p, out_p, gp_p, t1, t2, tok_h, cot_h, hid_h, ffn_h, gates, mix_h, qk_h, v_h, prob_h, wf_h, rt,
-     cosr, sinr) = take(18)
+    (gin, out_p, gp_p, t1, t2, f1, f2, tok_h, cot_h, hid_h, ffn_h, gates, mix_h, qk_h, v_h, prob_h, wf_h, rt,
+     cosr, sinr) = take(20)
     out_o, gt_o, sh_o, sm_o, t1_o, t2_o = take(6)
-    l1 = take(m)
-    l2 = take(m)
+    l1 = [f1] + take(m - 1)
+    l2 = [f2] + take(m - 1)
     a1 = take(m - 1)
     a2 = take(m - 1)
     sib, rcv, sibq, rcvq = take(4)
@@ -870,17 +969,15 @@
     def sems(i):
         return (s_sib.at[i], r_sib.at[i], s_z.at[i], r_z.at[i])
 
-    gin_line = Line(nf, f, d, lambda ch: acc.at[ch], lambda ch: gin_p.at[2 * ch + 1 - k], lambda ch: sib.at[ch],
-                    lambda dr, s: rcv.at[dr, s], st, sems(0), s_stage)
     wo_cols = pl.ds(QV, D)
     o_line = Line(nf, f, d, lambda ch: wg.at[rows(2 * ch + k), wo_cols], lambda ch: wg.at[rows(2 * ch + 1 - k), wo_cols],
                   lambda ch: sib.at[ch, 0:R], lambda dr, s: rcv.at[dr, s, 0:R],
-                  stage.at[0:R] if land_hbm else None, sems(1), s_stage, cred.at[0])
+                  stage.at[0:R] if land_hbm else None, sems(1), s_stage)
     q_cols = pl.ds(0, QV)
     q_line = Line(nf, f, d, lambda ch: wg.at[rows(2 * ch + k), q_cols], lambda ch: wg.at[rows(2 * ch + 1 - k), q_cols],
                   lambda ch: sibq.at[ch], lambda dr, s: rcvq.at[dr, s], stq, sems(2), s_stage)
     out_line = Line(nf, f, d, lambda ch: acc.at[ch], lambda ch: out_p.at[2 * ch + 1 - k], lambda ch: sib.at[ch],
-                    lambda dr, s: rcv.at[dr, s], st, sems(3), s_stage, cred.at[1])
+                    lambda dr, s: rcv.at[dr, s], st, sems(3), s_stage, cred)
 
     def acc_loads(src):
         return [pltpu.make_async_copy(src.at[2 * ch + k], acc.at[ch], s_acc.at[ch]) for ch in range(C)]
@@ -891,20 +988,10 @@
         cp = remote(gp_p.at[to], gpb.at[f], s_gp.at[i - 1], r_gp.at[i - 1], to, d)
         cp.start()
         gp_copies.append(cp)
-    loads = acc_loads(gin_p)
-    for cp in loads:
+    out_loads = acc_loads(out_p)
+    for cp in out_loads:
         cp.start()
-    gin_line.start_sib()
-    cubes = []
-    for e in range(el):
-        for j, (src, out, ls, ts, size) in enumerate(((t1, t1_o, l1, a1, D), (t2, t2_o, l2, a2, t2.shape[1]))):
-            cube = Cube(nd, f, d, e >= el // 2, False, size, src.at[e],
-                        functools.partial(lambda ls, e, i: ls[i].at[e], ls, e),
-                        functools.partial(lambda ts, e, i: ts[i].at[e], ts, e), out.at[e],
-                        (s_cube.at[2 * e + j], r_cube.at[2 * e + j]))
-            cubes.append(cube)
-    for cube in cubes:
-        cube.down(0).start()
+    cubes = term_cubes(nd, el, f, d, t1, t2, t1_o, t2_o, l1, l2, a1, a2, (s_cube, r_cube))
     own_gp = pltpu.make_async_copy(gp_p.at[f], gpb.at[f], s_load.at[0])
     own_gp.start()
     wo = pltpu.make_async_copy(wf_h.at[:, QV:QV + D], wb.at[:, 0:D], s_load.at[1])
@@ -919,18 +1006,15 @@
         return pltpu.make_async_copy(prob_h.at[at], prob.at[lax.rem(i, 2)], s_prob.at[lax.rem(i, 2)])
 
     prob_load(0).start()
-    for cp in loads:
-        cp.wait()
-
-    for s in range(1, C):
-        gin_line.step(s)
+    for i in range(0, 1):
+        for cube in cubes:
+            cube.fold(i, pipe_add)
+            cube.down(i + 1).start() if m > 1 else cube.up(0).start()
     for cp in more:
         cp.wait()
     own_gp.wait()
     for cp in gp_copies:
         cp.wait()
-    gin_line.last()
-    gin_line.free(cred.at[0])
 
     gains = rt[E:E + 2].astype(F32)
     gain_one, gain_two = gains[0:1], gains[1:2]
@@ -950,7 +1034,7 @@
         h = hid[at, :]
         r2 = lax.rsqrt(jnp.mean(h * h, -1, keepdims=True) + EPSILON)
         n2 = h * r2
-        gf = acc[c, at, :].astype(F32) + ga[at, :]
+        gf = gin[at, :].astype(F32) + ga[at, :]
         sms[E + 1:E + 2, :] += jnp.sum(gf * n2, 0, keepdims=True)
         g2 = gf * gain_two
         x = cot[at, :].astype(F32) + r2 * (g2 - n2 * jnp.mean(g2 * n2, -1, keepdims=True))
@@ -963,7 +1047,6 @@
         wg[at, QV:QV + D] = dot_tn(mix[:, at], branch[...]).astype(BF)
     o_line.start_sib()
     o_line.step(1)
-    gin_line.sent()
     wo.wait()
 
     @pl.loop(0, QW // 256)
@@ -972,11 +1055,6 @@
         gm[:, at] = dot_nt(branch[...], wb[at, 0:D]).astype(BF)
     wq = pltpu.make_async_copy(wf_h.at[:, 0:QV], wb, s_load.at[1])
     wq.start()
-    for cube in cubes:
-        cube.merge(0, pipe_add)
-    for cube in cubes:
-        cube.down(1).start() if m > 1 else cube.up(0).start()
-
     factor = HEAD_SIZE ** (-0.5)
     lane = lax.broadcasted_iota(jnp.int32, (T, 128), 1)
     low = lane < HEAD_SIZE
@@ -1024,8 +1102,15 @@
         gproj[:, pl.ds(pl.multiple_of(QW + i * 128, 128), 128)] = unrotate(join(gk) * factor).astype(BF)
         gproj[:, pl.ds(pl.multiple_of(QW + KW + i * 128, 128), 128)] = join(gv).astype(BF)
 
-    if C > 2:
-        o_line.step(2)
+        if C > 2:
+            @pl.when(i == 1)
+            def _():
+                o_line.step(2)
+
+    if m > 1:
+        for cube in cubes:
+            cube.merge(1, pipe_add)
+            cube.down(2).start() if m > 2 else cube.up(1).start()
     @pl.loop(0, T // TR)
     def _(i):
         at = pl.ds(pl.multiple_of(i * TR, TR), TR)
@@ -1042,11 +1127,6 @@
     for s in range(3, C):
         o_line.step(s)
     q_line.step(1)
-    if m > 1:
-        for cube in cubes:
-            cube.merge(1, pipe_add)
-        for cube in cubes:
-            cube.down(2).start() if m > 2 else cube.up(1).start()
     wq.wait()
 
     @pl.loop(0, D // 256)
@@ -1078,13 +1158,21 @@
     smr_own.start()
 
     o_line.last()
-    o_line.free(cred.at[1])
+    o_line.free(cred)
+    if m > 2:
+        for i in range(2, m):
+            for cube in cubes:
+                cube.merge(i, pipe_add)
+                cube.down(i + 1).start() if i + 1 < m else cube.up(m - 1).start()
+    for i in range(m - 1, 0, -1):
+        for cube in cubes:
+            cube.up_in(i).wait_recv()
+            cube.up(i - 1).start()
     if C > 2:
         q_line.step(2)
     o_line.sent()
-    out_loads = acc_loads(out_p)
     for cp in out_loads:
-        cp.start()
+        cp.wait()
     smr_own.wait()
     for cp in sm_copies:
         cp.wait()
@@ -1100,19 +1188,6 @@
     for s in range(3, C):
         q_line.step(s)
     out_line.start_sib()
-    for cp in out_loads:
-        cp.wait()
-    if m > 2:
-        for i in range(2, m):
-            for cube in cubes:
-                cube.merge(i, pipe_add)
-            for cube in cubes:
-                cube.down(i + 1).start() if i + 1 < m else cube.up(m - 1).start()
-    for i in range(m - 1, 0, -1):
-        for cube in cubes:
-            cube.up_in(i).wait_recv()
-        for cube in cubes:
-            cube.up(i - 1).start()
     out_line.step(1)
     q_line.last()
 
@@ -1166,16 +1241,19 @@
 
     q_line.sent()
     out_line.sent()
-    for cube in cubes + shards:
+    for cube in cubes:
+        cube.up_in(0).wait_recv()
+        cube.sent(1)
+    for cube in shards:
         cube.up_in(0).wait_recv()
         cube.sent()
 
 
 def back(nf, nd, el, args):
     gin, t1, t2 = args[0], args[3], args[4]
-    _, T, D = gin.shape
-    E = args[9].shape[0]
-    W = args[14].shape[1]
+    T, D = gin.shape
+    E = args[11].shape[0]
+    W = args[16].shape[1]
     R = D // nf
     C = nf // 2
     m = nd.bit_length() - 1
@@ -1186,7 +1264,7 @@
     s = jax.ShapeDtypeStruct
     out_shape = [s((T, D), BF), s((T, D), BF), s((R, W), BF), s((SR, R), F32), s(t1.shape, BF), s(t2.shape, BF)]
     out_specs = [vm(), vm(), vm(), vm(), hbm(), hbm()]
-    extra = [(el, D >> (i + 1), t1.shape[2]) for i in range(m)] + [(el, FFW >> (i + 1), D) for i in range(m)]
+    extra = [(el, D >> (i + 1), t1.shape[2]) for i in range(1, m)] + [(el, FFW >> (i + 1), D) for i in range(1, m)]
     extra += [(el, D >> (i + 1), t1.shape[2]) for i in range(m - 1)] + [(el, FFW >> (i + 1), D) for i in range(m - 1)]
     lands = [(C, T, D), (2, C - 1, T, D), (C, R, QV), (2, C - 1, R, QV)]
     scratch = []
@@ -1212,9 +1290,9 @@
         dma((4, C)), dma((4, C)), dma((4, 2, C)), dma((4, 2, C)),
         dma((2 * el, 2 * m)), dma((2 * el, 2 * m)), dma((2, 2 * m)), dma((2, 2 * m)),
         dma((nf,)), dma((nf,)), dma((nd,)), dma((nd,)), dma(()), dma((2,)),
-        pltpu.SemaphoreType.REGULAR((2, 3)),
+        pltpu.SemaphoreType.REGULAR((3,)),
     ]
-    inner = [hbm(), hbm(), vm(), hbm(), hbm(), hbm(), hbm(), hbm(), hbm(), vm(), hbm(), hbm(), hbm(), hbm(), hbm(), vm(),
+    inner = [vm(), hbm(), vm(), hbm(), hbm(), hbm(), hbm(), hbm(), hbm(), hbm(), hbm(), vm(), hbm(), hbm(), hbm(), hbm(), hbm(), vm(),
              vm(), vm()]
     return pl.pallas_call(
         functools.partial(back_kernel, nf, nd, el, land_hbm),
@@ -1239,7 +1317,6 @@
     experts = el * nf
     cap = 9 * T * TOP // (8 * experts)
 
-    packed = jnp.concatenate([w_query, key_weight, value_weight, w_out], 1)
     pad = -(experts + 2) % 16
     small = jnp.concatenate([w_router, gain_attn[:, None], gain_ffn[:, None],
                              jnp.zeros((w_router.shape[0], pad), BF)], 1).T
@@ -1249,11 +1326,11 @@
     slots = jnp.where(onehot.T > 0, before, -1.0)
     cosr, sinr = rope_rows(T)
     ffn_in, hidden, gates, mixed, qk, v, probs, full, cot_all, rt = front(
-        nf, nd, experts, tokens, packed, small, cotangent, slots, cosr, sinr)
+        nf, nd, experts, tokens, (w_query, key_weight, value_weight, w_out), small, cotangent, slots, cosr, sinr)
     side = jnp.concatenate([slots.reshape(nf, el, T), gates.reshape(nf, el, T)], 1)
-    out_part, gin_part, gp_part, t1, t2 = experts_call(nf, cap, ffn_in, cot_all, side, w_gate, w_up, w_down)
+    out_part, gin, gp_part, t1, t2, f1, f2 = experts_call(nf, nd, cap, ffn_in, cot_all, side, w_gate, w_up, w_down)
     output, grad_tokens, shard, smalls, t1, t2 = back(nf, nd, el, (
-        gin_part, out_part, gp_part, t1, t2, tokens, cotangent, hidden, ffn_in, gates, mixed, qk, v, probs, full, rt,
+        gin, out_part, gp_part, t1, t2, f1, f2, tokens, cotangent, hidden, ffn_in, gates, mixed, qk, v, probs, full, rt,
         cosr, sinr))
     big = shard.astype(F32)
     return (

time: 526 us -> 467 us (0.89)
  Pallas kernels: 491 us -> 438 us
    pallas_call x1, Pallas kernels: 289 us -> 198 us  [back(): pl.pallas_call(functools.partial(back_kernel, nf, nd, el, land_hbm), out_...]
    pallas_call x1, Pallas kernels: 94 us -> 148 us  [experts_call(): pl.pallas_call(functools.partial(experts_kernel, nf, nd, el, cap, capp, l...]
    pallas_call x1, Pallas kernels: 109 us -> 92.5 us  [front(): pl.pallas_call(functools.partial(front_kernel, nf, nd, experts), out_shap...]
where the time goes in v4:
time: 467 us; the launch traced here: 462 us
  Pallas kernels  438 us (94%)
  other arithmetic  12.8 us (3%)
  local copies, waits for them, and re-layouts  10.5 us (2%)
    pallas_call x1, Pallas kernels, back(): pl.pallas_call(functools.partial(back_kernel, nf, nd, el, land_hbm), out_...  198 us
    pallas_call x1, Pallas kernels, experts_call(): pl.pallas_call(functools.partial(experts_kernel, nf, nd, el, cap, capp, l...  148 us
    pallas_call x1, Pallas kernels, front(): pl.pallas_call(functools.partial(front_kernel, nf, nd, experts), out_shap...  92.5 us

profile of v4, /device:TPU:10, one launch (start us, length us, event | category | flops | bytes accessed | tf_op | source)
XLA Modules:
  0.0 462.5 jit_solution(1528804088155780304)
XLA Ops:
  0.7 0.1 pad.5.clone
  0.7 0.7 broadcast_in_dim.17
  1.4 0.7 broadcast_in_dim.18
  2.0 0.7 fusion
  2.8 0.1 convolution_select_fusion.slots
  2.9 1.4 maximum_bitcast_fusion.small
  4.3 0.0 copy-done.4
  4.3 92.5 %front.1 = (bf16[256,1536]{1,0:T(8,128)(2,1)}, f32[256,1536]{1,0:T(8,128)}, f32[16,256]{1,0:T(8,128)}, bf16[256,1536]{1,0:T(8,128)(2,1)}, bf16[256,2048]{1,0:T(8...) custom-call(bf16[256,1536]{1,0:T(8,128)(2,1)} %refs_7_.1, ...), custom_call_target="tpu_custom_call" | custom-call | flops 4000000000 | bytes 60000000 | tf_op jit(solution)/shard_map/front/pallas_call | solution.py:363
  96.9 0.7 reshape.32
  97.6 0.6 pad_maximum_fusion.side
  98.2 148.2 %experts.1 = (bf16[8,256,1536]{2,1,0:T(8,128)(2,1)}, bf16[256,1536]{1,0:T(8,128)(2,1)}, f32[8,2,256]{2,1,0:T(2,128)}, bf16[2,1536,1024]{2,1,0:T(8,128)(2,1)}, bf...) custom-call(bf16[256,1536]{1,0:T(8,128)(2,1)} %get-tuple-element.35.ffn.refs_10_, ...), custom_call_target="tpu_custom_call" | custom-call | flops 40000000000 | bytes 60000000 | tf_op jit(solution)/shard_map/experts/pallas_call | solution.py:912
  246.5 197.5 %back.1 = (bf16[256,1536]{1,0:T(8,128)(2,1)}, bf16[256,1536]{1,0:T(8,128)(2,1)}, bf16[192,4096]{1,0:T(8,128)(2,1)}, f32[24,192]{1,0:T(8,128)}, bf16[2,1536,1024]...) custom-call(bf16[256,1536]{1,0:T(8,128)(2,1)} %get-tuple-element.38., ...), custom_call_target="tpu_custom_call" | custom-call | flops 8000000000 | bytes 90000000 | tf_op jit(solution)/shard_map/back/pallas_call | solution.py:1297
  444.0 0.0 copy-start
  444.0 1.4 fusion.3
  445.4 1.3 slice_bitcast_fusion
  446.7 2.1 fusion.2
  448.9 0.0 copy-done
  448.9 1.7 fusion.1
  450.6 0.0 copy-done.1
  450.6 3.6 convert_element_type.22
  454.2 6.5 %slice_convert_fusion = (f32[2,1536,512]{2,1,0:T(8,128)}, f32[2,1536,512]{2,1,0:T(8,128)}) fusion(bf16[2,1536,1024]{2,1,0:T(8,128)(2,1)S(1)} %bitcast.10), kind=kLoop, calls=%fused_computation | loop fusion | flops 3145728 | bytes 18874368 | tf_op jit(solution)/shard_map/convert_element_type | solution.py:1347
  460.7 0.9 copy.30
  461.6 0.0 copy-done.2
  461.6 0.9 copy.31
  (12 shorter events, 0.0 us)
Async XLA Ops:
  2.9 1.4 copy-start.4
  444.0 4.9 %copy-start = (bf16[192,4096]{1,0:T(8,128)(2,1)S(1)}, bf16[192,4096]{1,0:T(8,128)(2,1)}, u32[]{:S(2)}) copy-start(bf16[192,4096]{1,0:T(8,128)(2,1)} %get-tuple-element.54) | copy-start | bytes 4718596
  446.7 3.8 copy-start.1
  448.9 5.3 %slice-start = ((s8[6291456]{0:T(1024)(128)(4,1)}), s8[4194304]{0:T(1024)(128)(4,1)S(1)}, s32[]{:S(2)}) async-start(s8[6291456]{0:T(1024)(128)(4,1)} %bitcast.9), calls=%async_computation | async-start | bytes 8388608
  450.6 3.6 slice-start.1
  454.2 6.5 %copy-start.3 = (bf16[256,1536]{1,0:T(8,128)(2,1)S(1)}, bf16[256,1536]{1,0:T(8,128)(2,1)}, u32[]{:S(2)}) copy-start(bf16[256,1536]{1,0:T(8,128)(2,1)} %get-tuple-element.78) | copy-start | bytes 2359300
  454.2 7.4 %copy-start.2 = (bf16[256,1536]{1,0:T(8,128)(2,1)S(1)}, bf16[256,1536]{1,0:T(8,128)(2,1)}, u32[]{:S(2)}) copy-start(bf16[256,1536]{1,0:T(8,128)(2,1)} %get-tuple-element.79) | copy-start | bytes 2359300

commit v5 on v4

--- a/solution.py
+++ b/solution.py
@@ -130,6 +130,25 @@
         blk = wf.at[rows(2 * src_chip(dr, s) + k), cols(d, g)]
         return remote(blk, blk, s_z.at[g, dr, s - 1], r_z.at[g, dr, s - 1], f, d)
 
+    halves = (slice(0, D // 2), slice(D // 2, D))
+
+    def cz(dr, s, own, h):
+        ff = 2 * src_chip(dr, s - 1) + k
+        src = cot.at[:, halves[h]] if own else cot_o.at[ff, :, halves[h]]
+        return remote(src, cot_o.at[ff, :, halves[h]], s_cz.at[h, dr, s - 1], r_cz.at[h, dr, s - 1], nxt_f(dr), d)
+
+    def cz_in(dr, s, h):
+        blk = cot_o.at[2 * src_chip(dr, s) + k, :, halves[h]]
+        return remote(blk, blk, s_cz.at[h, dr, s - 1], r_cz.at[h, dr, s - 1], f, d)
+
+    def cs(dr, s):
+        ff = 2 * src_chip(dr, s) + k
+        return remote(cot_o.at[ff], cot_o.at[ff], s_cs.at[dr, s], r_cs.at[dr, s], sib, d)
+
+    def cs_in(dr, s):
+        ff = 2 * src_chip(dr, s) + 1 - k
+        return remote(cot_o.at[ff], cot_o.at[ff], s_cs.at[dr, s], r_cs.at[dr, s], sib, d)
+
     at = 0
     w_own = []
     for i, w in enumerate((wq, wk, wv, wo)):
@@ -144,7 +163,6 @@
             @pl.when(nxt_ok(dr))
             def _():
                 wz(dr, 1, g).start()
-
     own_small = pltpu.make_async_copy(small, sm.at[f], s_loc.at[0])
     own_small.start()
     sm_copies = []
@@ -152,6 +170,11 @@
         cp = remote(small, sm.at[f], s_sm.at[i - 1], r_sm.at[i - 1], lax.rem(f + i, nf), d)
         cp.start()
         sm_copies.append(cp)
+    for dr in range(2):
+        @pl.when((c if dr == 0 else C - 1 - c) == 0)
+        def _():
+            for h in range(2):
+                cz(dr, 1, True, h).start()
     sib_own = remote(wf.at[rows(f)], wf.at[rows(f)], s_sib.at[0, 0, 0], r_sib.at[0, 0, 0], sib, d)
     sib_own.start()
     own_c = pltpu.make_async_copy(cot, cot_o.at[f], s_loc.at[2])
@@ -175,23 +198,6 @@
         at, n = parts[g]
         blk = wf.at[rows(2 * src_chip(dr, s) + 1 - k), at:at + n]
         return remote(blk, blk, s_sib.at[g, dr, s], r_sib.at[g, dr, s], sib, d)
-
-    def cz(dr, s, own):
-        ff = 2 * src_chip(dr, s - 1) + k
-        src = cot if own else cot_o.at[ff]
-        return remote(src, cot_o.at[ff], s_cz.at[dr, s - 1], r_cz.at[dr, s - 1], nxt_f(dr), d)
-
-    def cz_in(dr, s):
-        ff = 2 * src_chip(dr, s) + k
-        return remote(cot_o.at[ff], cot_o.at[ff], s_cz.at[dr, s - 1], r_cz.at[dr, s - 1], f, d)
-
-    def cs(dr, s):
-        ff = 2 * src_chip(dr, s) + k
-        return remote(cot_o.at[ff], cot_o.at[ff], s_cs.at[dr, s], r_cs.at[dr, s], sib, d)
-
-    def cs_in(dr, s):
-        ff = 2 * src_chip(dr, s) + 1 - k
-        return remote(cot_o.at[ff], cot_o.at[ff], s_cs.at[dr, s], r_cs.at[dr, s], sib, d)
 
     for s in range(1, C):
         for g in range(2):
@@ -206,10 +212,11 @@
                     if g == 0:
                         for i in range(1, nd):
                             dp_copy(dr, s, g, i).start()
-    for dr in range(2):
-        @pl.when(nxt_ok(dr))
-        def _():
-            cz(dr, 1, True).start()
+        for dr in range(2):
+            @pl.when(nxt_ok(dr) & ((c if dr == 0 else C - 1 - c) == s))
+            def _():
+                for h in range(2):
+                    cz(dr, 1, True, h).start()
     sib_c.start()
     for s in range(1, C):
         for dr in range(2):
@@ -249,16 +256,19 @@
         for dr in range(2):
             @pl.when(has(dr, s))
             def _():
-                cz_in(dr, s).wait_recv()
-                if s < C - 1:
-                    @pl.when(nxt_ok(dr))
-                    def _():
-                        cz(dr, s + 1, False).start()
+                for h in range(2):
+                    cz_in(dr, s, h).wait_recv()
+                    if s < C - 1:
+                        @pl.when(nxt_ok(dr))
+                        def _():
+                            cz(dr, s + 1, False, h).start()
                 cs(dr, s).start()
 
+    cot_step(1)
     for s in range(1, C - 1):
         group_in(s, 0)
-    cot_step(1)
+    for s in range(2, min(C, 3)):
+        cot_step(s)
     group_in(C - 1, 0)
     sib_own.wait()
     cores_in(0)
@@ -278,9 +288,6 @@
     def _(i):
         col = pl.ds(pl.multiple_of(QW + KW + i * 256, 256), 256)
         v_o[:, pl.ds(pl.multiple_of(i * 256, 256), 256)] = dot(attn[...], wf[:, col]).astype(BF)
-
-    for s in range(2, min(C, 3)):
-        cot_step(s)
 
     factor = HEAD_SIZE ** (-0.5)
     lane = lax.broadcasted_iota(jnp.int32, (T, 128), 1)
@@ -311,6 +318,8 @@
     cores_in(1)
     out_w = pltpu.make_async_copy(wf, wf_o, s_loc.at[3])
     out_w.start()
+    for s in range(3, C):
+        cot_step(s)
 
     @pl.loop(0, D // 256)
     def _(i):
@@ -327,8 +336,6 @@
     ex = jnp.where(named, jnp.exp(logits - jnp.max(logits, 0, keepdims=True)), 0.0)
     gates_o[...] = ex / jnp.sum(ex, 0, keepdims=True)
 
-    for s in range(3, C):
-        cot_step(s)
     own_c.wait()
     sib_c.wait()
     out_w.wait()
@@ -347,7 +354,8 @@
             def _():
                 for g in range(2):
                     wz(dr, s, g).wait_send()
-                cz(dr, s, s == 1).wait_send()
+                for h in range(2):
+                    cz(dr, s, s == 1, h).wait_send()
 
 
 def front(nf, nd, experts, tok, ws, small, cot, slots, cosr, sinr):
@@ -374,7 +382,7 @@
             dma((2, 2, C)), dma((2, 2, C)),
             dma((2, 2, C, nd)), dma((2, 2, C, nd)),
             dma((2, 2, C)), dma((2, 2, C)),
-            dma((2, C)), dma((2, C)),
+            dma((2, 2, C)), dma((2, 2, C)),
             dma((2, C)), dma((2, C)),
             dma((4,)), dma((4,)),
         ],
@@ -396,13 +404,13 @@
 
 
 class Line:
-    def __init__(self, nf, f, d, acc, give, sib, rcv, stage, sems, stage_sem, credit=None):
+    def __init__(self, nf, f, d, acc, give, sib, rcv, stage, sems, stage_sem):
         self.nf, self.f, self.d = nf, f, d
         self.C = nf // 2
         self.c, self.k = f // 2, lax.rem(f, 2)
         self.acc, self.give, self.sib, self.rcv, self.stage = acc, give, sib, rcv, stage
         self.s_sib, self.r_sib, self.s_z, self.r_z = sems
-        self.stage_sem, self.credit = stage_sem, credit
+        self.stage_sem = stage_sem
 
     def remote(self, src, dst, ss, rs, to):
         return pltpu.make_async_remote_copy(src_ref=src, dst_ref=dst, send_sem=ss, recv_sem=rs,
@@ -412,7 +420,7 @@
         i = s - 1 - (self.C - 1 - self.c) if dr == 0 else s - 1 - self.c
         room = self.c if dr == 0 else self.C - 1 - self.c
         chip = i if dr == 0 else self.C - 1 - i
-        return jnp.clip(chip, 0, self.C - 1), (i >= 0) & (i < room), i == 0
+        return jnp.clip(chip, 0, self.C - 1), (i >= 0) & (i < room)
 
     def sib_copy(self, chip):
         return self.remote(self.give(chip), self.sib(chip), self.s_sib.at[chip], self.r_sib.at[chip],
@@ -427,11 +435,9 @@
                            self.f)
 
     def start_sib(self):
-        if self.credit is not None:
-            pl.semaphore_wait(self.credit.at[2], 1)
         for s in range(1, self.C):
             for dr in range(2):
-                chip, ok, _ = self.dest(dr, s)
+                chip, ok = self.dest(dr, s)
 
                 @pl.when(ok)
                 def _():
@@ -451,29 +457,31 @@
 
     def step(self, s):
         for dr in range(2):
-            chip, ok, opening = self.dest(dr, s)
+            chip, ok = self.dest(dr, s)
             begins = (self.c == self.C - 1) if dr == 0 else (self.c == 0)
 
             @pl.when(ok)
             def _():
-                self.sib_copy(chip).wait_recv()
-
-                @pl.when(begins)
-                def _():
-                    self.gather(chip, [self.sib(chip)])
+                other = []
+                if self.sib is not None:
+                    self.sib_copy(chip).wait_recv()
+                    other = [self.sib(chip)]
+
+                    @pl.when(begins)
+                    def _():
+                        self.gather(chip, other)
                 if s > 1:
                     @pl.when(jnp.logical_not(begins))
                     def _():
                         self.z_in(dr, s - 1).wait_recv()
-                        self.gather(chip, [self.sib(chip), self.rcv(dr, s - 2)])
-                if self.credit is not None:
-                    @pl.when(opening)
-                    def _():
-                        pl.semaphore_wait(self.credit.at[dr], 1)
+                        self.gather(chip, other + [self.rcv(dr, s - 2)])
                 self.z_copy(dr, s, chip).start()
 
     def last(self):
-        self.sib_copy(self.c).wait_recv()
+        other = []
+        if self.sib is not None:
+            self.sib_copy(self.c).wait_recv()
+            other = [self.sib(self.c)]
         mid = (self.c > 0) & (self.c < self.C - 1)
         s = self.C - 1
         for dr in range(2):
@@ -483,54 +491,51 @@
 
         @pl.when(mid)
         def _():
-            self.gather(self.c, [self.sib(self.c), self.rcv(0, s - 1), self.rcv(1, s - 1)])
+            self.gather(self.c, other + [self.rcv(0, s - 1), self.rcv(1, s - 1)])
 
         @pl.when(self.c == 0)
         def _():
-            self.gather(self.c, [self.sib(self.c), self.rcv(0, s - 1)])
+            self.gather(self.c, other + [self.rcv(0, s - 1)])
 
         @pl.when(self.c == self.C - 1)
         def _():
-            self.gather(self.c, [self.sib(self.c), self.rcv(1, s - 1)])
+            self.gather(self.c, other + [self.rcv(1, s - 1)])
 
     def sent(self):
-        self.sib_copy(self.c).wait_send()
+        if self.acc is None:
+            for chip in range(self.C):
+                self.sib_copy(chip).wait_send()
+            return
+        if self.sib is not None:
+            self.sib_copy(self.c).wait_send()
         for s in range(1, self.C):
             for dr in range(2):
-                chip, ok, _ = self.dest(dr, s)
+                chip, ok = self.dest(dr, s)
 
                 @pl.when(ok)
                 def _():
-                    self.sib_copy(chip).wait_send()
+                    if self.sib is not None:
+                        self.sib_copy(chip).wait_send()
                     self.z_copy(dr, s, chip).wait_send()
-
-    def free(self, credit):
-        def tell(i, to):
-            pl.semaphore_signal(credit.at[i], inc=1, device_id=(to, self.d), device_id_type=MESH)
-
-        tell(2, self.f + 1 - 2 * self.k)
-
-        @pl.when(self.c < self.C - 1)
-        def _():
-            tell(0, self.f + 2)
-
-        @pl.when(self.c > 0)
-        def _():
-            tell(1, self.f - 2)
 
 
 class Cube:
     def __init__(self, nd, f, d, flip, lanes, size, own, land, total, out, sems):
         m = nd.bit_length() - 1
-        self.bits = list(range(m))[::-1] if flip else list(range(m))
+        order = [1 << b for b in range(m)]
+        if isinstance(flip, bool):
+            self.masks = order[::-1] if flip else order
+        else:
+            self.masks = [jnp.where(flip, b, a) for a, b in zip(order, order[::-1])]
         self.f, self.d, self.lanes = f, d, lanes
         self.own, self.land, self.total, self.out = own, land, total, out
         self.ss, self.rs = sems
         self.m = m
+        self.in_place, self.whole = False, True
         self.low, self.length = [0], [size]
-        for b in self.bits:
+        for mask in self.masks:
             half = self.length[-1] // 2
-            side = lax.rem(d // (1 << b), 2)
+            side = lax.rem(d // mask, 2)
             self.low.append(self.low[-1] + side * half)
             self.length.append(half)
 
@@ -539,13 +544,13 @@
             return ref.at[:, pl.ds(pl.multiple_of(at, 128), n)]
         return ref.at[pl.ds(pl.multiple_of(at, 16), n)]
 
-    def remote(self, src, dst, i, to_bit):
+    def remote(self, src, dst, i, mask):
         return pltpu.make_async_remote_copy(src_ref=src, dst_ref=dst, send_sem=self.ss.at[i], recv_sem=self.rs.at[i],
-                                            device_id=(self.f, jnp.bitwise_xor(self.d, 1 << to_bit)),
+                                            device_id=(self.f, jnp.bitwise_xor(self.d, mask)),
                                             device_id_type=MESH)
 
     def level(self, i):
-        if i == 0:
+        if i == 0 or (self.in_place and (i < self.m or not self.whole)):
             return self.own, 0
         if i == self.m:
             return self.out, 0
@@ -555,7 +560,7 @@
         ref, base = self.level(i)
         half = self.length[i + 1]
         other = 2 * self.low[i] + half - self.low[i + 1]
-        return self.remote(self.cut(ref, other - base, half), self.land(i), i, self.bits[i])
+        return self.remote(self.cut(ref, other - base, half), self.land(i), i, self.masks[i])
 
     def merge(self, i, add):
         self.down(i).wait_recv()
@@ -570,13 +575,13 @@
 
     def up(self, i):
         blk = self.cut(self.out, self.low[i + 1], self.length[i + 1])
-        return self.remote(blk, blk, self.m + i, self.bits[i])
+        return self.remote(blk, blk, self.m + i, self.masks[i])
 
     def up_in(self, i):
         half = self.length[i + 1]
         other = 2 * self.low[i] + half - self.low[i + 1]
         blk = self.cut(self.out, other, half)
-        return self.remote(blk, blk, self.m + i, self.bits[i])
+        return self.remote(blk, blk, self.m + i, self.masks[i])
 
     def sent(self, first=0):
         for i in range(self.m):
@@ -616,8 +621,8 @@
 
 
 def experts_kernel(nf, nd, el, cap, capp, land_hbm, ffn, cot_a, side, wg_h, wu_h, wd_h,
-                   out_o, gin_o, gp_o, t1_o, t2_o, l1, l2, sib_l, rcv_l, acc,
-                   wg, wu, wd, fa, sd, cotb, xs, gs, hs, hgs, orb, irb, st_o, give, st1, st2, stage,
+                   out_o, gin_o, gp_o, t1_o, t2_o, l1, sib_l, rcv_l, acc,
+                   wg, wu, wd, fa, sd, cotb, xs, gs, hs, hgs, orb, irb, st_o, give, st1, st2, stage, us,
                    s_sd, r_sd, s_z, r_z, s_sib, r_sib, s_w, s_loc, s_t, s_ls, r_ls, s_lz, r_lz, s_st, s_cube, r_cube):
     T, D = ffn.shape
     FFW = wg.shape[2]
@@ -647,16 +652,18 @@
     def nxt_f(dr):
         return f + 2 if dr == 0 else f - 2
 
-    def z_out(dr, s):
-        ff = 2 * chip_at(dr, s - 1) + k
-        return remote(fa.at[ff], fa.at[ff], s_z.at[dr, s - 1], r_z.at[dr, s - 1], nxt_f(dr))
-
-    def z_own(dr):
-        return remote(ffn, fa.at[f], s_z.at[dr, 0], r_z.at[dr, 0], nxt_f(dr))
-
-    def z_in(dr, s):
-        ff = 2 * chip_at(dr, s) + k
-        return remote(fa.at[ff], fa.at[ff], s_z.at[dr, s - 1], r_z.at[dr, s - 1], f)
+    halves = (slice(0, D // 2), slice(D // 2, D))
+
+    def z_out(dr, s, h):
+        blk = fa.at[2 * chip_at(dr, s - 1) + k, :, halves[h]]
+        return remote(blk, blk, s_z.at[h, dr, s - 1], r_z.at[h, dr, s - 1], nxt_f(dr))
+
+    def z_own(dr, h):
+        return remote(ffn.at[:, halves[h]], fa.at[f, :, halves[h]], s_z.at[h, dr, 0], r_z.at[h, dr, 0], nxt_f(dr))
+
+    def z_in(dr, s, h):
+        blk = fa.at[2 * chip_at(dr, s) + k, :, halves[h]]
+        return remote(blk, blk, s_z.at[h, dr, s - 1], r_z.at[h, dr, s - 1], f)
 
     def sib_out(dr, s):
         ff = 2 * chip_at(dr, s) + k
@@ -666,16 +673,23 @@
         ff = 2 * chip_at(dr, s) + 1 - k
         return remote(fa.at[ff], fa.at[ff], s_sib.at[dr, s], r_sib.at[dr, s], f)
 
-    line = Line(nf, f, d, lambda ch: acc.at[ch], lambda ch: give.at[0], lambda ch: sib_l.at[ch],
-                lambda dr, s: rcv_l.at[dr, s], stage if land_hbm else None, (s_ls, r_ls, s_lz, r_lz), s_st)
-
-    def handed(chip, slot):
-        return remote(give.at[slot], sib_l.at[chip], s_ls.at[chip], r_ls.at[chip], sib)
-
-    for dr in range(2):
-        @pl.when(nxt_ok(dr))
-        def _():
-            z_own(dr).start()
+    lines = [Line(nf, f, d, lambda ch, cut=cut: acc.at[ch, :, cut], lambda ch, cut=cut: give.at[0, :, cut],
+                  lambda ch, cut=cut: sib_l.at[ch, :, cut], lambda dr, s, cut=cut: rcv_l.at[dr, s, :, cut],
+                  stage.at[:, cut] if land_hbm else None, (s_ls.at[h], r_ls.at[h], s_lz.at[h], r_lz.at[h]), s_st)
+             for h, cut in enumerate(halves)]
+
+    def handed(chip, slot, h):
+        return remote(give.at[slot, :, halves[h]], sib_l.at[chip, :, halves[h]], s_ls.at[h, chip], r_ls.at[h, chip], sib)
+
+    def reduce_step(s):
+        for line in lines:
+            line.step(s)
+
+    for h in range(2):
+        for dr in range(2):
+            @pl.when(nxt_ok(dr))
+            def _():
+                z_own(dr, h).start()
     sib_own = remote(ffn, fa.at[f], s_sib.at[1, 0], r_sib.at[1, 0], sib)
     sib_own.start()
     own = pltpu.make_async_copy(ffn, fa.at[f], s_loc.at[0])
@@ -708,20 +722,6 @@
         cot_cp = pltpu.make_async_copy(cot_a.at[pl.ds(2 * b, 2)], cotb, s_loc.at[2])
         cot_cp.start()
 
-        @pl.when(j >= 1)
-        def _():
-            for dr in range(2):
-                @pl.when(has(dr, j))
-                def _():
-                    z_in(dr, j).wait_recv()
-
-                    @pl.when(nxt_ok(dr) & (j < C - 1))
-                    def _():
-                        z_out(dr, j + 1).start()
-                    sib_out(dr, j).start()
-        sib_in(dr_b, dist_b).wait_recv()
-        cot_cp.wait()
-
         base = pl.multiple_of(b * B, 16)
         gate_rows = [[None, None] for _ in range(el)]
         picks = []
@@ -734,14 +734,36 @@
                 parts.append(jnp.where(hit, 1.0, 0.0).astype(BF))
             p2 = jnp.concatenate(parts, 0)
             picks.append(p2)
-            for n in range(0, D, 512):
-                xv = dot(p2, fa[s, :, n:n + 512]).astype(BF)
-                gv_ = dot(p2, cotb[kk, :, n:n + 512]).astype(BF)
-                for e in range(el):
-                    at = pl.ds(pl.multiple_of(base + kk * capp, 16), capp)
-                    xs[e, at, n:n + 512] = xv[e * capp:(e + 1) * capp]
-                    gs[e, at, n:n + 512] = gv_[e * capp:(e + 1) * capp]
+        cot_cp.wait()
+
+        def spread(rows_of, dst):
+            for kk in range(2):
+                for n in range(0, D, 512):
+                    val = dot(picks[kk], rows_of(kk, n)).astype(BF)
+                    for e in range(el):
+                        at = pl.ds(pl.multiple_of(base + kk * capp, 16), capp)
+                        dst[e, at, n:n + 512] = val[e * capp:(e + 1) * capp]
+
         here = pl.ds(base, B)
+        spread(lambda kk, n: cotb[kk, :, n:n + 512], gs)
+        for e in range(el):
+            for n in range(0, FFW, 256):
+                us[e, :, n:n + 256] = dot_nt(gs[e, here, :], wd[e, n:n + 256, :])
+
+        @pl.when(j >= 1)
+        def _():
+            for dr in range(2):
+                @pl.when(has(dr, j))
+                def _():
+                    for h in range(2):
+                        z_in(dr, j, h).wait_recv()
+
+                        @pl.when(nxt_ok(dr) & (j < C - 1))
+                        def _():
+                            z_out(dr, j + 1, h).start()
+                    sib_out(dr, j).start()
+        sib_in(dr_b, dist_b).wait_recv()
+        spread(lambda kk, n: fa[2 * b + kk, :, n:n + 512], xs)
         gp_rows = []
         for e in range(el):
             gate_row = jnp.concatenate(gate_rows[e], 0)
@@ -749,7 +771,7 @@
             for n in range(0, FFW, 256):
                 gv = dot(xs[e, here, :], wg[e, :, n:n + 256])
                 uv = dot(xs[e, here, :], wu[e, :, n:n + 256])
-                u = dot_nt(gs[e, here, :], wd[e, n:n + 256, :])
+                u = us[e, :, n:n + 256]
                 sg = 1.0 / (1.0 + jnp.exp(-gv))
                 act = gv * sg
                 hid = act * uv
@@ -760,32 +782,39 @@
                 hs[e, here, FFW + n:FFW + n + 256] = (gh * act).astype(BF)
             gp_rows.append(gpr)
             for n in range(0, D, 512):
-                orow = dot(hgs[e, here, :], wd[e, :, n:n + 512]).astype(BF)
                 irow = (dot_nt(hs[e, here, 0:FFW], wg[e, n:n + 512, :])
                         + dot_nt(hs[e, here, FFW:2 * FFW], wu[e, n:n + 512, :])).astype(BF)
                 for kk in range(2):
-                    orb[kk, e * capp:(e + 1) * capp, n:n + 512] = orow[kk * capp:(kk + 1) * capp]
                     irb[kk, e * capp:(e + 1) * capp, n:n + 512] = irow[kk * capp:(kk + 1) * capp]
 
         @pl.when(j >= 2)
         def _():
             before, _, _ = visit(c, C, j - 2)
-            handed(before, lax.rem(j, 2)).wait_send()
-        for kk in range(2):
-            s = 2 * b + kk
-
-            def combine(dst):
-                for n in range(0, D, 512):
-                    dst[:, n:n + 512] = dot_tn(picks[kk], irb[kk, :, n:n + 512]).astype(BF)
-
-            @pl.when(k == kk)
-            def _():
-                combine(acc.at[b])
-
-            @pl.when(k != kk)
-            def _():
-                combine(give.at[lax.rem(j, 2)])
-                handed(b, lax.rem(j, 2)).start()
+            for h in range(2):
+                handed(before, lax.rem(j, 2), h).wait_send()
+        for h in range(2):
+            for kk in range(2):
+                def combine(dst):
+                    cut = halves[h]
+                    dst[:, cut] = dot_tn(picks[kk], irb[kk, :, cut]).astype(BF)
+
+                @pl.when(k == kk)
+                def _():
+                    combine(acc.at[b])
+
+                @pl.when(k != kk)
+                def _():
+                    combine(give.at[lax.rem(j, 2)])
+                    handed(b, lax.rem(j, 2), h).start()
+
+        @pl.when(j == C - 1)
+        def _():
+            reduce_step(1)
+        for e in range(el):
+            for n in range(0, D, 512):
+                orow = dot(hgs[e, here, :], wd[e, :, n:n + 512]).astype(BF)
+                for kk in range(2):
+                    orb[kk, e * capp:(e + 1) * capp, n:n + 512] = orow[kk * capp:(kk + 1) * capp]
 
         def back(bb):
             return pltpu.make_async_copy(st_o, out_o.at[pl.ds(2 * bb, 2)], s_loc.at[3])
@@ -802,8 +831,6 @@
                 st_o[kk, :, n:n + 512] = dot_tn(picks[kk], orb[kk, :, n:n + 512]).astype(BF)
         back(b).start()
 
-    line.step(1)
-
     n1 = D // 256
     n2 = FFW // 256
 
@@ -815,7 +842,7 @@
         return pltpu.make_async_copy(st2.at[lax.rem(i, 2)], t2_o.at[e, pl.ds(pl.multiple_of(i * 256, 256), 256)],
                                      s_t.at[1, lax.rem(i, 2)])
 
-    cubes = term_cubes(nd, el, f, d, t1_o, t2_o, None, None, [l1], [l2], [], [], (s_cube, r_cube))
+    cubes = term_cubes(nd, el, f, d, t1_o, t2_o, None, None, [l1], None, [], [], (s_cube, r_cube))
     for e in range(el):
         @pl.loop(0, n1)
         def _(i):
@@ -829,6 +856,8 @@
         for i in range(2):
             t1_copy(e, i).wait()
         cubes[2 * e].down(0).start()
+        if e == el - 1 and C > 2:
+            reduce_step(2)
 
         @pl.loop(0, n2)
         def _(i):
@@ -840,29 +869,27 @@
             t2_copy(e, i).start()
         for i in range(2):
             t2_copy(e, i).wait()
-        cubes[2 * e + 1].down(0).start()
-        if e < C - 2:
-            line.step(e + 2)
-
-    for s in range(el + 2, C):
-        line.step(s)
-    for s in range(C - 2, el):
-        pass
-    line.last()
+
+    for s in range(3, C):
+        reduce_step(s)
+    for line in lines:
+        line.last()
     gin_o[...] = acc[c]
 
     pltpu.make_async_copy(st_o, out_o.at[pl.ds(0, 2)], s_loc.at[3]).wait()
     for j in range(max(C - 2, 0), C):
         chip, _, _ = visit(c, C, j)
-        handed(chip, j % 2).wait_send()
-    for s in range(1, C):
-        for dr in range(2):
-            chip, ok, _ = line.dest(dr, s)
-
-            @pl.when(ok)
-            def _():
-                line.z_copy(dr, s, chip).wait_send()
-    for cube in cubes:
+        for h in range(2):
+            handed(chip, j % 2, h).wait_send()
+    for line in lines:
+        for s in range(1, C):
+            for dr in range(2):
+                chip, ok = line.dest(dr, s)
+
+                @pl.when(ok)
+                def _():
+                    line.z_copy(dr, s, chip).wait_send()
+    for cube in cubes[::2]:
         cube.down(0).wait()
     sib_own.wait_send()
     for dr in range(2):
@@ -873,7 +900,8 @@
         for s in range(1, C):
             @pl.when(nxt_ok(dr) & has(dr, s - 1))
             def _():
-                z_out(dr, s).wait_send()
+                for h in range(2):
+                    z_out(dr, s, h).wait_send()
 
 
 def experts_call(nf, nd, cap, ffn_in, cot_all, side, w_gate, w_up, w_down):
@@ -886,7 +914,7 @@
     dma = pltpu.SemaphoreType.DMA
     out = [((nf, T, D), BF, 1), ((T, D), BF, 0), ((nf, el, T), F32, 0),
            ((el, D, 2 * FFW), BF, 1), ((el, FFW, D), BF, 1),
-           ((el, D // 2, 2 * FFW), BF, 1), ((el, FFW // 2, D), BF, 1)]
+           ((el, D // 2, 2 * FFW), BF, 1)]
     lands = [(C, T, D), (2, C - 1, T, D)]
     scratch = []
     if land_hbm:
@@ -903,10 +931,11 @@
         VMEM((2, T, D), BF), VMEM((2, T, D), BF),
         VMEM((2, 256, 2 * FFW), BF), VMEM((2, 256, D), BF),
         VMEM((T, D) if land_hbm else (16, 128), BF),
+        VMEM((el, 2 * capp, FFW), F32),
         dma((nf,)), dma((nf,)),
-        dma((2, C)), dma((2, C)), dma((2, C)), dma((2, C)),
+        dma((2, 2, C)), dma((2, 2, C)), dma((2, C)), dma((2, C)),
         dma((3,)), dma((5,)), dma((2, 2)),
-        dma((C,)), dma((C,)), dma((2, C)), dma((2, C)), dma(()),
+        dma((2, C)), dma((2, C)), dma((2, 2, C)), dma((2, 2, C)), dma(()),
         dma((2 * el, 2 * (nd.bit_length() - 1))), dma((2 * el, 2 * (nd.bit_length() - 1))),
     ]
     return pl.pallas_call(
@@ -919,30 +948,33 @@
                                              vmem_limit_bytes=63 * 2 ** 20),
         cost_estimate=pl.CostEstimate(flops=40_000_000_000, bytes_accessed=60_000_000, transcendentals=2_000_000),
         name="experts",
-    )(ffn_in, cot_all, side, w_gate, w_up, w_down)[:7]
-
-
-def back_kernel(nf, nd, el, land_hbm, *refs):
+    )(ffn_in, cot_all, side, w_gate, w_up, w_down)[:6]
+
+
+def back_kernel(nf, nd, el, land_hbm, split, *refs):
     m = nd.bit_length() - 1
     it = iter(refs)
 
     def take(n):
         return [next(it) for _ in range(n)]
 
-    (gin, out_p, gp_p, t1, t2, f1, f2, tok_h, cot_h, hid_h, ffn_h, gates, mix_h, qk_h, v_h, prob_h, wf_h, rt,
-     cosr, sinr) = take(20)
+    (gin, out_p, gp_p, t1, t2, f1, tok_h, cot_h, hid_h, ffn_h, gates, mix_h, qk_h, v_h, prob_h, wf_h, rt,
+     cosr, sinr) = take(19)
     out_o, gt_o, sh_o, sm_o, t1_o, t2_o = take(6)
     l1 = [f1] + take(m - 1)
-    l2 = [f2] + take(m - 1)
+    l2 = take(m)
     a1 = take(m - 1)
     a2 = take(m - 1)
-    sib, rcv, sibq, rcvq = take(4)
-    (acc, wb, wg, tok, cot, hid, ffn, mix, qk, v, prob, branch, gh, ga, gproj, gpb, smg, smr, smd, shb, sms) = take(21)
+    sibo, rcvo, sib, rcv, sibq, rcvq = take(6)
+    (acc, wb, wg, tok, cot, hid, ffn, mix, qk, v, prob, branch, gh, ga, gproj, gpb, smg, smr, smd, sms) = take(20)
     attn, gm = ffn, mix
     shl = take(m)
+    if split:
+        xo = next(it)
+        xol = take(m)
     stage, stageq = take(2)
     (s_load, s_acc, s_gp, r_gp, s_sib, r_sib, s_z, r_z, s_cube, r_cube, s_sc, r_sc, s_sm, r_sm, s_sd, r_sd,
-     s_stage, s_prob, cred) = take(19)
+     s_stage, s_prob) = take(18)
 
     T, D = tok.shape
     R = wg.shape[0] // nf
@@ -963,21 +995,45 @@
     def rows(ff):
         return pl.ds(pl.multiple_of(ff * R, 16), R)
 
-    st = stage if land_hbm else None
-    stq = stageq if land_hbm else None
 
     def sems(i):
         return (s_sib.at[i], r_sib.at[i], s_z.at[i], r_z.at[i])
 
-    wo_cols = pl.ds(QV, D)
-    o_line = Line(nf, f, d, lambda ch: wg.at[rows(2 * ch + k), wo_cols], lambda ch: wg.at[rows(2 * ch + 1 - k), wo_cols],
-                  lambda ch: sib.at[ch, 0:R], lambda dr, s: rcv.at[dr, s, 0:R],
-                  stage.at[0:R] if land_hbm else None, sems(1), s_stage)
-    q_cols = pl.ds(0, QV)
-    q_line = Line(nf, f, d, lambda ch: wg.at[rows(2 * ch + k), q_cols], lambda ch: wg.at[rows(2 * ch + 1 - k), q_cols],
-                  lambda ch: sibq.at[ch], lambda dr, s: rcvq.at[dr, s], stq, sems(2), s_stage)
-    out_line = Line(nf, f, d, lambda ch: acc.at[ch], lambda ch: out_p.at[2 * ch + 1 - k], lambda ch: sib.at[ch],
-                    lambda dr, s: rcv.at[dr, s], st, sems(3), s_stage, cred)
+    def halves_of(first, n, sb, rc, sg, ids):
+        res = []
+        for h in range(2):
+            at = first + h * (n // 2)
+            cut, loc = pl.ds(at, n // 2), pl.ds(h * (n // 2), n // 2)
+            res.append(Line(nf, f, d, lambda ch, cut=cut: wg.at[rows(2 * ch + k), cut],
+                            lambda ch, cut=cut: wg.at[rows(2 * ch + 1 - k), cut],
+                            lambda ch, loc=loc: sb.at[ch, :, loc], lambda dr, s, loc=loc: rc.at[dr, s, :, loc],
+                            sg.at[:, loc] if land_hbm else None, sems(ids[h]), s_stage))
+        return res
+
+    if split:
+        o_lines = []
+        pair = Line(nf, f, d, None, lambda ch: wg.at[rows(2 * ch + 1 - k), QV:QV + D], lambda ch: sib.at[ch], None, None,
+                    sems(0), s_stage)
+        o_cubes = []
+        for h in range(2):
+            top = h * (C * R // 2)
+            cube = Cube(nd, f, d, h == 1, True, D, xo.at[top:top + C * R // 2],
+                        functools.partial(lambda h, i: xol[i].at[h], h), None, None, (s_sc.at[h], r_sc.at[h]))
+            cube.in_place, cube.whole = True, False
+            o_cubes.append(cube)
+        o_low = [cube.low[m] for cube in o_cubes]
+
+        def o_block(ch):
+            low = pl.multiple_of(jnp.where(ch < C // 2, o_low[0], o_low[1]), 128)
+            return xo.at[pl.ds(pl.multiple_of(ch * R, 16), R), pl.ds(low, D >> m)]
+
+        o_line = Line(nf, f, d, o_block, None, None, lambda dr, s: rcv.at[dr, s], None, sems(1), s_stage)
+        o_up = Cube(nd, f, d, c >= C // 2, True, D, None, None, None, sh_o.at[:, QV:QV + D], (s_sc.at[2], r_sc.at[2]))
+    else:
+        o_lines = halves_of(QV, D, sib, rcv, stage.at[0:R], (0, 1))
+    q_lines = halves_of(0, QV, sibq, rcvq, stageq, (2, 4))
+    out_line = Line(nf, f, d, lambda ch: acc.at[ch], lambda ch: out_p.at[2 * ch + 1 - k], lambda ch: sibo.at[ch],
+                    lambda dr, s: rcvo.at[dr, s], stage, sems(3), s_stage)
 
     def acc_loads(src):
         return [pltpu.make_async_copy(src.at[2 * ch + k], acc.at[ch], s_acc.at[ch]) for ch in range(C)]
@@ -988,10 +1044,14 @@
         cp = remote(gp_p.at[to], gpb.at[f], s_gp.at[i - 1], r_gp.at[i - 1], to, d)
         cp.start()
         gp_copies.append(cp)
+    out_line.start_sib()
     out_loads = acc_loads(out_p)
     for cp in out_loads:
         cp.start()
     cubes = term_cubes(nd, el, f, d, t1, t2, t1_o, t2_o, l1, l2, a1, a2, (s_cube, r_cube))
+    first_terms, second_terms = cubes[::2], cubes[1::2]
+    for cube in second_terms:
+        cube.down(0).start()
     own_gp = pltpu.make_async_copy(gp_p.at[f], gpb.at[f], s_load.at[0])
     own_gp.start()
     wo = pltpu.make_async_copy(wf_h.at[:, QV:QV + D], wb.at[:, 0:D], s_load.at[1])
@@ -1006,10 +1066,38 @@
         return pltpu.make_async_copy(prob_h.at[at], prob.at[lax.rem(i, 2)], s_prob.at[lax.rem(i, 2)])
 
     prob_load(0).start()
-    for i in range(0, 1):
-        for cube in cubes:
-            cube.fold(i, pipe_add)
-            cube.down(i + 1).start() if m > 1 else cube.up(0).start()
+
+    def onward(cube, i):
+        cube.down(i + 1).start() if i + 1 < m else cube.up(i).start()
+
+    def chain(group, start, add):
+        def merged(i):
+            for cube in group:
+                cube.merge(i, add)
+                onward(cube, i)
+
+        def raised(i):
+            for cube in group:
+                cube.up_in(i).wait_recv()
+                cube.up(i - 1).start()
+
+        return ([functools.partial(merged, i) for i in range(start, m)]
+                + [functools.partial(raised, i) for i in range(m - 1, 0, -1)])
+
+    def vadd(dst, a, b):
+        add_blocks(dst, [a, b])
+
+    def run(steps, n=1):
+        for _ in range(min(n, len(steps))):
+            steps.pop(0)()
+
+    steps1, steps2 = chain(first_terms, 1, pipe_add), chain(second_terms, 1, pipe_add)
+    for cube in first_terms:
+        cube.fold(0, pipe_add)
+        onward(cube, 0)
+    for cp in out_loads:
+        cp.wait()
+    out_line.step(1)
     for cp in more:
         cp.wait()
     own_gp.wait()
@@ -1045,8 +1133,15 @@
     def _(i):
         at = pl.ds(pl.multiple_of(i * 256, 256), 256)
         wg[at, QV:QV + D] = dot_tn(mix[:, at], branch[...]).astype(BF)
-    o_line.start_sib()
-    o_line.step(1)
+    if split:
+        pair.start_sib()
+        if C > 2:
+            out_line.step(2)
+    else:
+        for line in o_lines:
+            line.start_sib()
+        for line in o_lines:
+            line.step(1)
     wo.wait()
 
     @pl.loop(0, QW // 256)
@@ -1055,6 +1150,15 @@
         gm[:, at] = dot_nt(branch[...], wb[at, 0:D]).astype(BF)
     wq = pltpu.make_async_copy(wf_h.at[:, 0:QV], wb, s_load.at[1])
     wq.start()
+    if split:
+        for ch in range(C):
+            pair.sib_copy(ch).wait_recv()
+            add_blocks(xo.at[ch * R:(ch + 1) * R], [wg.at[rows(2 * ch + k), QV:QV + D], sib.at[ch]])
+        for cube in o_cubes:
+            cube.down(0).start()
+    for cube in second_terms:
+        cube.merge(0, pipe_add)
+        onward(cube, 0)
     factor = HEAD_SIZE ** (-0.5)
     lane = lax.broadcasted_iota(jnp.int32, (T, 128), 1)
     low = lane < HEAD_SIZE
@@ -1105,12 +1209,16 @@
         if C > 2:
             @pl.when(i == 1)
             def _():
-                o_line.step(2)
-
-    if m > 1:
-        for cube in cubes:
-            cube.merge(1, pipe_add)
-            cube.down(2).start() if m > 2 else cube.up(1).start()
+                for line in o_lines:
+                    line.step(2)
+
+
+    def o_merge(i):
+        for cube in o_cubes:
+            cube.merge(i, vadd)
+            if i + 1 < m:
+                cube.down(i + 1).start()
+
     @pl.loop(0, T // TR)
     def _(i):
         at = pl.ds(pl.multiple_of(i * TR, TR), TR)
@@ -1123,10 +1231,17 @@
         at = pl.ds(pl.multiple_of(i * 256, 256), 256)
         for n in range(0, QV, 512):
             wg[at, n:n + 512] = dot_tn(attn[:, at], gproj[:, n:n + 512]).astype(BF)
-    q_line.start_sib()
+    for line in q_lines:
+        line.start_sib()
     for s in range(3, C):
-        o_line.step(s)
-    q_line.step(1)
+        for line in o_lines:
+            line.step(s)
+    for line in q_lines:
+        line.step(1)
+    run(steps1)
+    run(steps2)
+    if split:
+        o_merge(0)
     wq.wait()
 
     @pl.loop(0, D // 256)
@@ -1157,22 +1272,33 @@
     smr_own = pltpu.make_async_copy(smg.at[f], smr.at[f], s_load.at[0])
     smr_own.start()
 
-    o_line.last()
-    o_line.free(cred)
-    if m > 2:
-        for i in range(2, m):
-            for cube in cubes:
-                cube.merge(i, pipe_add)
-                cube.down(i + 1).start() if i + 1 < m else cube.up(m - 1).start()
-    for i in range(m - 1, 0, -1):
-        for cube in cubes:
-            cube.up_in(i).wait_recv()
-            cube.up(i - 1).start()
+    for line in o_lines:
+        line.last()
+    late = []
+    width = QV if split else W
+    for h in range(2):
+        top = h * (R // 2)
+        own = wg.at[pl.ds(pl.multiple_of(f * R + top, 16), R // 2), 0:width]
+        cube = Cube(nd, f, d, h == 1, True, width, own, functools.partial(lambda h, i: shl[i].at[h], h),
+                    None, sh_o.at[top:top + R // 2, 0:width], (s_sc.at[3 + h], r_sc.at[3 + h]))
+        cube.in_place = True
+        late.append(cube)
+    steps_l = chain(late, 0, vadd)
+    run(steps1)
+    run(steps2)
     if C > 2:
-        q_line.step(2)
-    o_line.sent()
-    for cp in out_loads:
-        cp.wait()
+        for line in q_lines:
+            line.step(2)
+    if split:
+        for i in range(1, m):
+            o_merge(i)
+        o_line.step(1)
+    if split:
+        if C > 2:
+            o_line.step(2)
+        pair.sent()
+    for line in o_lines:
+        line.sent()
     smr_own.wait()
     for cp in sm_copies:
         cp.wait()
@@ -1186,45 +1312,29 @@
         cp.start()
         sd_copies.append(cp)
     for s in range(3, C):
-        q_line.step(s)
-    out_line.start_sib()
-    out_line.step(1)
-    q_line.last()
-
-    own = wg.at[rows(f)]
-    add_blocks(shb, [own])
-    half = W // 2
-    shards = []
-    for h in range(2):
-        shards.append(Cube(nd, f, d, h == 1, True, half, shb.at[:, h * half:(h + 1) * half],
-                           functools.partial(lambda h, i: shl[i].at[h], h),
-                           functools.partial(lambda h, i: shb.at[:, h * half:(h + 1) * half], h),
-                           sh_o.at[:, h * half:(h + 1) * half], (s_sc.at[h], r_sc.at[h])))
-
-    def level(self, i):
-        return (self.own, 0) if i < self.m else (self.out, 0)
-
-    for cube in shards:
-        cube.level = functools.partial(level, cube)
+        for line in q_lines:
+            line.step(s)
+    if not split and C > 2:
+        out_line.step(2)
+    run(steps1, len(steps1))
+    run(steps2, len(steps2))
+    if split:
+        for s in range(3, C):
+            o_line.step(s)
+        o_line.last()
+        add_blocks(sh_o.at[:, pl.ds(pl.multiple_of(QV + o_up.low[m], 128), D >> m)], [o_block(c)])
+        o_up.up(m - 1).start()
+    for line in q_lines:
+        line.last()
+    for cube in late:
         cube.down(0).start()
-
-    def vadd(dst, a, b):
-        add_blocks(dst, [a, b])
-
-    if C > 2:
-        out_line.step(2)
-    for i in range(m):
-        for cube in shards:
-            cube.merge(i, vadd)
-        for cube in shards:
-            cube.down(i + 1).start() if i + 1 < m else cube.up(i).start()
     for s in range(3, C):
         out_line.step(s)
-    for i in range(m - 1, 0, -1):
-        for cube in shards:
-            cube.up_in(i).wait_recv()
-        for cube in shards:
-            cube.up(i - 1).start()
+    if split:
+        for i in range(m - 1, 0, -1):
+            o_up.up_in(i).wait_recv()
+            o_up.up(i - 1).start()
+    run(steps_l, len(steps_l))
     for cp in sd_copies:
         cp.wait()
     total = smd[0]
@@ -1239,12 +1349,20 @@
         out_o[at, :] = (hid[at, :] + acc[c, at, :].astype(F32)).astype(BF)
 
 
-    q_line.sent()
+    for line in q_lines:
+        line.sent()
     out_line.sent()
-    for cube in cubes:
+    for i, cube in enumerate(cubes):
         cube.up_in(0).wait_recv()
-        cube.sent(1)
-    for cube in shards:
+        cube.sent(1 - i % 2)
+    if split:
+        o_up.up_in(0).wait_recv()
+        o_line.sent()
+        for i in range(m):
+            o_up.up(i).wait_send()
+            for cube in o_cubes:
+                cube.down(i).wait_send()
+    for cube in late:
         cube.up_in(0).wait_recv()
         cube.sent()
 
@@ -1252,8 +1370,8 @@
 def back(nf, nd, el, args):
     gin, t1, t2 = args[0], args[3], args[4]
     T, D = gin.shape
-    E = args[11].shape[0]
-    W = args[16].shape[1]
+    E = args[10].shape[0]
+    W = args[15].shape[1]
     R = D // nf
     C = nf // 2
     m = nd.bit_length() - 1
@@ -1264,9 +1382,11 @@
     s = jax.ShapeDtypeStruct
     out_shape = [s((T, D), BF), s((T, D), BF), s((R, W), BF), s((SR, R), F32), s(t1.shape, BF), s(t2.shape, BF)]
     out_specs = [vm(), vm(), vm(), vm(), hbm(), hbm()]
-    extra = [(el, D >> (i + 1), t1.shape[2]) for i in range(1, m)] + [(el, FFW >> (i + 1), D) for i in range(1, m)]
+    extra = [(el, D >> (i + 1), t1.shape[2]) for i in range(1, m)] + [(el, FFW >> (i + 1), D) for i in range(m)]
     extra += [(el, D >> (i + 1), t1.shape[2]) for i in range(m - 1)] + [(el, FFW >> (i + 1), D) for i in range(m - 1)]
-    lands = [(C, T, D), (2, C - 1, T, D), (C, R, QV), (2, C - 1, R, QV)]
+    extra += [(C, T, D), (2, C - 1, T, D)]
+    split = not land_hbm and (D >> m) % 128 == 0 and (QV >> m) % 128 == 0
+    lands = [(C, R, D), (2, C - 1, R, D >> m if split else D), (C, R, QV), (2, C - 1, R, QV)]
     scratch = []
     if land_hbm:
         extra += lands
@@ -1280,22 +1400,23 @@
         VMEM((T, D), BF), VMEM((T, D), BF), VMEM((T, D), F32), VMEM((T, D), BF), VMEM((T, QW), BF),
         VMEM((T, QW + KW), BF), VMEM((T, KW), BF), VMEM((2, 2 * GROUP, T, T), BF),
         VMEM((T, D), BF), VMEM((T, D), F32), VMEM((T, D), F32), VMEM((T, QV), BF),
-        VMEM((nf, el, T), F32), VMEM((nf, SR, R), F32), VMEM((nf, SR, R), F32), VMEM((nd, SR, R), F32), VMEM((R, W), BF),
+        VMEM((nf, el, T), F32), VMEM((nf, SR, R), F32), VMEM((nf, SR, R), F32), VMEM((nd, SR, R), F32),
         VMEM((SR, D), F32),
     ]
-    scratch += [VMEM((2, R, W >> (i + 2)), BF) for i in range(m)]
-    scratch += [VMEM((T, D) if land_hbm else (16, 128), BF), VMEM((R, QV) if land_hbm else (16, 128), BF)]
+    scratch += [VMEM((2, R // 2, (QV if split else W) >> (i + 1)), BF) for i in range(m)]
+    if split:
+        scratch += [VMEM((C * R, D), BF)] + [VMEM((2, C * R // 2, D >> (i + 1)), BF) for i in range(m)]
+    scratch += [VMEM((T, D), BF), VMEM((R, QV) if land_hbm else (16, 128), BF)]
     scratch += [
         dma((10,)), dma((C,)), dma((nf,)), dma((nf,)),
-        dma((4, C)), dma((4, C)), dma((4, 2, C)), dma((4, 2, C)),
-        dma((2 * el, 2 * m)), dma((2 * el, 2 * m)), dma((2, 2 * m)), dma((2, 2 * m)),
+        dma((5, C)), dma((5, C)), dma((5, 2, C)), dma((5, 2, C)),
+        dma((2 * el, 2 * m)), dma((2 * el, 2 * m)), dma((5, 2 * m)), dma((5, 2 * m)),
         dma((nf,)), dma((nf,)), dma((nd,)), dma((nd,)), dma(()), dma((2,)),
-        pltpu.SemaphoreType.REGULAR((3,)),
     ]
-    inner = [vm(), hbm(), vm(), hbm(), hbm(), hbm(), hbm(), hbm(), hbm(), hbm(), hbm(), vm(), hbm(), hbm(), hbm(), hbm(), hbm(), vm(),
+    inner = [vm(), hbm(), vm(), hbm(), hbm(), hbm(), hbm(), hbm(), hbm(), hbm(), vm(), hbm(), hbm(), hbm(), hbm(), hbm(), vm(),
              vm(), vm()]
     return pl.pallas_call(
-        functools.partial(back_kernel, nf, nd, el, land_hbm),
+        functools.partial(back_kernel, nf, nd, el, land_hbm, split),
         out_shape=out_shape,
         in_specs=inner,
         out_specs=out_specs,
@@ -1311,7 +1432,6 @@
          w_gate, w_up, w_down, routes, cotangent):
     T = tokens.shape[0]
     el = w_gate.shape[0]
-    ff = w_gate.shape[2]
     nf = lax.axis_size("fsdp")
     nd = lax.axis_size("dp")
     experts = el * nf
@@ -1328,11 +1448,12 @@
     ffn_in, hidden, gates, mixed, qk, v, probs, full, cot_all, rt = front(
         nf, nd, experts, tokens, (w_query, key_weight, value_weight, w_out), small, cotangent, slots, cosr, sinr)
     side = jnp.concatenate([slots.reshape(nf, el, T), gates.reshape(nf, el, T)], 1)
-    out_part, gin, gp_part, t1, t2, f1, f2 = experts_call(nf, nd, cap, ffn_in, cot_all, side, w_gate, w_up, w_down)
+    out_part, gin, gp_part, t1, t2, f1 = experts_call(nf, nd, cap, ffn_in, cot_all, side, w_gate, w_up, w_down)
     output, grad_tokens, shard, smalls, t1, t2 = back(nf, nd, el, (
-        gin, out_part, gp_part, t1, t2, f1, f2, tokens, cotangent, hidden, ffn_in, gates, mixed, qk, v, probs, full, rt,
+        gin, out_part, gp_part, t1, t2, f1, tokens, cotangent, hidden, ffn_in, gates, mixed, qk, v, probs, full, rt,
         cosr, sinr))
     big = shard.astype(F32)
+    ff = w_gate.shape[2]
     return (
         output,
         grad_tokens,

time: 467 us -> 448 us (0.959)
  Pallas kernels: 438 us -> 422 us
    pallas_call x1, Pallas kernels: 198 us -> 184 us  [back(): pl.pallas_call(functools.partial(back_kernel, nf, nd, el, land_hbm, split...]
where the time goes in v5:
time: 448 us; the launch traced here: 446 us
  Pallas kernels  422 us (94%)
  other arithmetic  12.8 us (3%)
  local copies, waits for them, and re-layouts  10.5 us (2%)
    pallas_call x1, Pallas kernels, back(): pl.pallas_call(functools.partial(back_kernel, nf, nd, el, land_hbm, split...  184 us
    pallas_call x1, Pallas kernels, experts_call(): pl.pallas_call(functools.partial(experts_kernel, nf, nd, el, cap, capp, l...  149 us
    pallas_call x1, Pallas kernels, front(): pl.pallas_call(functools.partial(front_kernel, nf, nd, experts), out_shap...  89.7 us

profile of v5, /device:TPU:10, one launch (start us, length us, event | category | flops | bytes accessed | tf_op | source)
XLA Modules:
  0.0 446.3 jit_solution(17192368645804344843)
XLA Ops:
  0.7 0.1 pad.5.clone
  0.7 0.7 broadcast_in_dim.17
  1.4 0.7 broadcast_in_dim.18
  2.0 0.7 fusion
  2.8 0.1 convolution_select_fusion.slots
  2.9 1.4 maximum_bitcast_fusion.small
  4.3 0.0 copy-done.4
  4.3 89.7 %front.1 = (bf16[256,1536]{1,0:T(8,128)(2,1)}, f32[256,1536]{1,0:T(8,128)}, f32[16,256]{1,0:T(8,128)}, bf16[256,1536]{1,0:T(8,128)(2,1)}, bf16[256,2048]{1,0:T(8...) custom-call(bf16[256,1536]{1,0:T(8,128)(2,1)} %refs_6_.1, ...), custom_call_target="tpu_custom_call" | custom-call | flops 4000000000 | bytes 60000000 | tf_op jit(solution)/shard_map/front/pallas_call | solution.py:371
  94.0 0.7 reshape.32
  94.7 0.6 pad_maximum_fusion.side
  95.4 148.9 %experts.1 = (bf16[8,256,1536]{2,1,0:T(8,128)(2,1)}, bf16[256,1536]{1,0:T(8,128)(2,1)}, f32[8,2,256]{2,1,0:T(2,128)}, bf16[2,1536,1024]{2,1,0:T(8,128)(2,1)}, bf...) custom-call(bf16[256,1536]{1,0:T(8,128)(2,1)} %get-tuple-element.34.ffn.refs_9_, ...), custom_call_target="tpu_custom_call" | custom-call | flops 40000000000 | bytes 60000000 | tf_op jit(solution)/shard_map/experts/pallas_call | solution.py:941
  244.3 183.6 %back.1 = (bf16[256,1536]{1,0:T(8,128)(2,1)}, bf16[256,1536]{1,0:T(8,128)(2,1)}, bf16[192,4096]{1,0:T(8,128)(2,1)}, f32[24,192]{1,0:T(8,128)}, bf16[2,1536,1024]...) custom-call(bf16[256,1536]{1,0:T(8,128)(2,1)} %get-tuple-element.37., ...), custom_call_target="tpu_custom_call" | custom-call | flops 8000000000 | bytes 90000000 | tf_op jit(solution)/shard_map/back/pallas_call | solution.py:1418
  427.9 0.0 copy-start
  427.9 1.4 fusion.3
  429.3 1.3 slice_bitcast_fusion
  430.6 2.1 fusion.2
  432.8 0.0 copy-done
  432.8 1.7 fusion.1
  434.5 0.0 copy-done.1
  434.5 3.6 convert_element_type.22
  438.1 0.0 slice-done
  438.1 6.5 %slice_convert_fusion = (f32[2,1536,512]{2,1,0:T(8,128)}, f32[2,1536,512]{2,1,0:T(8,128)}) fusion(bf16[2,1536,1024]{2,1,0:T(8,128)(2,1)S(1)} %bitcast.10), kind=kLoop, calls=%fused_computation | loop fusion | flops 3145728 | bytes 18874368 | tf_op jit(solution)/shard_map/convert_element_type | solution.py:1468
  444.6 0.9 copy.30
  445.5 0.9 copy.31
  (12 shorter events, 0.0 us)
Async XLA Ops:
  2.9 1.4 copy-start.4
  427.9 4.9 %copy-start = (bf16[192,4096]{1,0:T(8,128)(2,1)S(1)}, bf16[192,4096]{1,0:T(8,128)(2,1)}, u32[]{:S(2)}) copy-start(bf16[192,4096]{1,0:T(8,128)(2,1)} %get-tuple-element.52) | copy-start | bytes 4718596
  430.6 3.8 copy-start.1
  432.8 5.3 %slice-start = ((s8[6291456]{0:T(1024)(128)(4,1)}), s8[4194304]{0:T(1024)(128)(4,1)S(1)}, s32[]{:S(2)}) async-start(s8[6291456]{0:T(1024)(128)(4,1)} %bitcast.9), calls=%async_computation | async-start | bytes 8388608
  434.5 3.6 slice-start.1
  438.1 6.5 %copy-start.3 = (bf16[256,1536]{1,0:T(8,128)(2,1)S(1)}, bf16[256,1536]{1,0:T(8,128)(2,1)}, u32[]{:S(2)}) copy-start(bf16[256,1536]{1,0:T(8,128)(2,1)} %get-tuple-element.76) | copy-start | bytes 2359300
  438.1 7.4 %copy-start.2 = (bf16[256,1536]{1,0:T(8,128)(2,1)S(1)}, bf16[256,1536]{1,0:T(8,128)(2,1)}, u32[]{:S(2)}) copy-start(bf16[256,1536]{1,0:T(8,128)(2,1)} %get-tuple-element.77) | copy-start | bytes 2359300

commit v6 on v5

--- a/solution.py
+++ b/solution.py
@@ -267,8 +267,6 @@
     cot_step(1)
     for s in range(1, C - 1):
         group_in(s, 0)
-    for s in range(2, min(C, 3)):
-        cot_step(s)
     group_in(C - 1, 0)
     sib_own.wait()
     cores_in(0)
@@ -295,6 +293,10 @@
 
     @pl.loop(0, KEY_VALUE_HEADS // 2)
     def _(i):
+        if C > 2:
+            @pl.when(i == 2)
+            def _():
+                cot_step(2)
         kc = pl.ds(pl.multiple_of(QW + i * 128, 128), 128)
         kh = head_masks(qk_o[:, kc], lane)
         vh = head_masks(v_o[:, pl.ds(pl.multiple_of(i * 128, 128), 128)], lane)
@@ -318,8 +320,6 @@
     cores_in(1)
     out_w = pltpu.make_async_copy(wf, wf_o, s_loc.at[3])
     out_w.start()
-    for s in range(3, C):
-        cot_step(s)
 
     @pl.loop(0, D // 256)
     def _(i):
@@ -336,6 +336,8 @@
     ex = jnp.where(named, jnp.exp(logits - jnp.max(logits, 0, keepdims=True)), 0.0)
     gates_o[...] = ex / jnp.sum(ex, 0, keepdims=True)
 
+    for s in range(3, C):
+        cot_step(s)
     own_c.wait()
     sib_c.wait()
     out_w.wait()
@@ -592,7 +594,7 @@
 
 def pipe_add(dst, a, b):
     n, w = dst.shape
-    tile = 128 if n % 128 == 0 else 64
+    tile = next(t for t in (256, 192, 128, 64) if n % t == 0 and t * w <= 256 * 1024)
     spec = pl.BlockSpec((tile, w), lambda i: (i, 0))
 
     def inner(a_ref, b_ref, o_ref):
@@ -968,7 +970,7 @@
     sibo, rcvo, sib, rcv, sibq, rcvq = take(6)
     (acc, wb, wg, tok, cot, hid, ffn, mix, qk, v, prob, branch, gh, ga, gproj, gpb, smg, smr, smd, sms) = take(20)
     attn, gm = ffn, mix
-    shl = take(m)
+    shl = take(m * (2 if split else 1))
     if split:
         xo = next(it)
         xol = take(m)
@@ -986,6 +988,7 @@
     c = f // 2
     k = lax.rem(f, 2)
     QV = QW + 2 * KW
+    QZ, OW = QV, D
     greet(nf, nd, f, d)
 
     def remote(src, dst, ss, rs, to_f, to_d):
@@ -999,11 +1002,10 @@
     def sems(i):
         return (s_sib.at[i], r_sib.at[i], s_z.at[i], r_z.at[i])
 
-    def halves_of(first, n, sb, rc, sg, ids):
+    def lines_of(first, cuts, sb, rc, sg, ids):
         res = []
-        for h in range(2):
-            at = first + h * (n // 2)
-            cut, loc = pl.ds(at, n // 2), pl.ds(h * (n // 2), n // 2)
+        for h, (top, n) in enumerate(cuts):
+            cut, loc = pl.ds(first + top, n), pl.ds(top, n)
             res.append(Line(nf, f, d, lambda ch, cut=cut: wg.at[rows(2 * ch + k), cut],
                             lambda ch, cut=cut: wg.at[rows(2 * ch + 1 - k), cut],
                             lambda ch, loc=loc: sb.at[ch, :, loc], lambda dr, s, loc=loc: rc.at[dr, s, :, loc],
@@ -1012,12 +1014,12 @@
 
     if split:
         o_lines = []
-        pair = Line(nf, f, d, None, lambda ch: wg.at[rows(2 * ch + 1 - k), QV:QV + D], lambda ch: sib.at[ch], None, None,
+        pair = Line(nf, f, d, None, lambda ch: wg.at[rows(2 * ch + 1 - k), QZ:W], lambda ch: sib.at[ch], None, None,
                     sems(0), s_stage)
         o_cubes = []
         for h in range(2):
             top = h * (C * R // 2)
-            cube = Cube(nd, f, d, h == 1, True, D, xo.at[top:top + C * R // 2],
+            cube = Cube(nd, f, d, h == 1, True, OW, xo.at[top:top + C * R // 2],
                         functools.partial(lambda h, i: xol[i].at[h], h), None, None, (s_sc.at[h], r_sc.at[h]))
             cube.in_place, cube.whole = True, False
             o_cubes.append(cube)
@@ -1025,13 +1027,14 @@
 
         def o_block(ch):
             low = pl.multiple_of(jnp.where(ch < C // 2, o_low[0], o_low[1]), 128)
-            return xo.at[pl.ds(pl.multiple_of(ch * R, 16), R), pl.ds(low, D >> m)]
+            return xo.at[pl.ds(pl.multiple_of(ch * R, 16), R), pl.ds(low, OW >> m)]
 
         o_line = Line(nf, f, d, o_block, None, None, lambda dr, s: rcv.at[dr, s], None, sems(1), s_stage)
-        o_up = Cube(nd, f, d, c >= C // 2, True, D, None, None, None, sh_o.at[:, QV:QV + D], (s_sc.at[2], r_sc.at[2]))
+        o_up = Cube(nd, f, d, c >= C // 2, True, OW, None, None, None, sh_o.at[:, QZ:W], (s_sc.at[2], r_sc.at[2]))
     else:
-        o_lines = halves_of(QV, D, sib, rcv, stage.at[0:R], (0, 1))
-    q_lines = halves_of(0, QV, sibq, rcvq, stageq, (2, 4))
+        o_lines = lines_of(QV, ((0, D // 2), (D // 2, D // 2)), sib, rcv, stage.at[0:R], (0, 1))
+    q_cuts = ((0, QW), (QW, 2 * KW))
+    q_lines = lines_of(0, q_cuts, sibq, rcvq, stageq, (2, 4))
     out_line = Line(nf, f, d, lambda ch: acc.at[ch], lambda ch: out_p.at[2 * ch + 1 - k], lambda ch: sibo.at[ch],
                     lambda dr, s: rcvo.at[dr, s], stage, sems(3), s_stage)
 
@@ -1091,7 +1094,7 @@
         for _ in range(min(n, len(steps))):
             steps.pop(0)()
 
-    steps1, steps2 = chain(first_terms, 1, pipe_add), chain(second_terms, 1, pipe_add)
+    steps1, steps2 = chain(first_terms, 1, pipe_add), chain(second_terms, 0, pipe_add)
     for cube in first_terms:
         cube.fold(0, pipe_add)
         onward(cube, 0)
@@ -1153,12 +1156,10 @@
     if split:
         for ch in range(C):
             pair.sib_copy(ch).wait_recv()
-            add_blocks(xo.at[ch * R:(ch + 1) * R], [wg.at[rows(2 * ch + k), QV:QV + D], sib.at[ch]])
+            add_blocks(xo.at[ch * R:(ch + 1) * R], [wg.at[rows(2 * ch + k), QZ:W], sib.at[ch]])
         for cube in o_cubes:
             cube.down(0).start()
-    for cube in second_terms:
-        cube.merge(0, pipe_add)
-        onward(cube, 0)
+    run(steps2)
     factor = HEAD_SIZE ** (-0.5)
     lane = lax.broadcasted_iota(jnp.int32, (T, 128), 1)
     low = lane < HEAD_SIZE
@@ -1226,17 +1227,17 @@
         r1 = lax.rsqrt(jnp.mean(x * x, -1, keepdims=True) + EPSILON)
         attn[at, :] = (x * r1 * gain_one).astype(BF)
 
-    @pl.loop(0, D // 256)
-    def _(i):
-        at = pl.ds(pl.multiple_of(i * 256, 256), 256)
-        for n in range(0, QV, 512):
-            wg[at, n:n + 512] = dot_tn(attn[:, at], gproj[:, n:n + 512]).astype(BF)
-    for line in q_lines:
+    for line, (top, width) in zip(q_lines, q_cuts):
+        @pl.loop(0, D // 256)
+        def _(i):
+            at = pl.ds(pl.multiple_of(i * 256, 256), 256)
+            for n in range(top, top + width, 512):
+                wg[at, n:n + 512] = dot_tn(attn[:, at], gproj[:, n:n + 512]).astype(BF)
         line.start_sib()
-    for s in range(3, C):
-        for line in o_lines:
-            line.step(s)
-    for line in q_lines:
+        if line is q_lines[0]:
+            for s in range(3, C):
+                for other in o_lines:
+                    other.step(s)
         line.step(1)
     run(steps1)
     run(steps2)
@@ -1274,16 +1275,18 @@
 
     for line in o_lines:
         line.last()
-    late = []
-    width = QV if split else W
-    for h in range(2):
-        top = h * (R // 2)
-        own = wg.at[pl.ds(pl.multiple_of(f * R + top, 16), R // 2), 0:width]
-        cube = Cube(nd, f, d, h == 1, True, width, own, functools.partial(lambda h, i: shl[i].at[h], h),
-                    None, sh_o.at[top:top + R // 2, 0:width], (s_sc.at[3 + h], r_sc.at[3 + h]))
-        cube.in_place = True
-        late.append(cube)
-    steps_l = chain(late, 0, vadd)
+    lates = []
+    for g, (left, width) in enumerate(q_cuts if split else ((0, W),)):
+        late = []
+        for h in range(2):
+            top = h * (R // 2)
+            own = wg.at[pl.ds(pl.multiple_of(f * R + top, 16), R // 2), left:left + width]
+            cube = Cube(nd, f, d, h == 1, True, width, own, functools.partial(lambda g, h, i: shl[g * m + i].at[h], g, h),
+                        None, sh_o.at[top:top + R // 2, left:left + width], (s_sc.at[3 + 2 * g + h], r_sc.at[3 + 2 * g + h]))
+            cube.in_place = True
+            late.append(cube)
+        lates.append(late)
+    steps_l = [chain(late, 0, vadd) for late in lates]
     run(steps1)
     run(steps2)
     if C > 2:
@@ -1322,19 +1325,22 @@
         for s in range(3, C):
             o_line.step(s)
         o_line.last()
-        add_blocks(sh_o.at[:, pl.ds(pl.multiple_of(QV + o_up.low[m], 128), D >> m)], [o_block(c)])
+        add_blocks(sh_o.at[:, pl.ds(pl.multiple_of(QZ + o_up.low[m], 128), OW >> m)], [o_block(c)])
         o_up.up(m - 1).start()
-    for line in q_lines:
+    for g, line in enumerate(q_lines):
         line.last()
-    for cube in late:
-        cube.down(0).start()
+        if split or line is q_lines[-1]:
+            for cube in lates[g if split else 0]:
+                cube.down(0).start()
     for s in range(3, C):
         out_line.step(s)
     if split:
         for i in range(m - 1, 0, -1):
             o_up.up_in(i).wait_recv()
             o_up.up(i - 1).start()
-    run(steps_l, len(steps_l))
+    while steps_l[-1]:
+        for steps in steps_l:
+            run(steps)
     for cp in sd_copies:
         cp.wait()
     total = smd[0]
@@ -1362,7 +1368,7 @@
             o_up.up(i).wait_send()
             for cube in o_cubes:
                 cube.down(i).wait_send()
-    for cube in late:
+    for cube in [cube for late in lates for cube in late]:
         cube.up_in(0).wait_recv()
         cube.sent()
 
@@ -1385,8 +1391,9 @@
     extra = [(el, D >> (i + 1), t1.shape[2]) for i in range(1, m)] + [(el, FFW >> (i + 1), D) for i in range(m)]
     extra += [(el, D >> (i + 1), t1.shape[2]) for i in range(m - 1)] + [(el, FFW >> (i + 1), D) for i in range(m - 1)]
     extra += [(C, T, D), (2, C - 1, T, D)]
-    split = not land_hbm and (D >> m) % 128 == 0 and (QV >> m) % 128 == 0
-    lands = [(C, R, D), (2, C - 1, R, D >> m if split else D), (C, R, QV), (2, C - 1, R, QV)]
+    QZ, OW = QV, D
+    split = not land_hbm and (OW >> m) % 128 == 0 and (QW >> m) % 128 == 0 and (2 * KW >> m) % 128 == 0
+    lands = [(C, R, OW), (2, C - 1, R, OW >> m if split else D), (C, R, QZ), (2, C - 1, R, QZ)]
     scratch = []
     if land_hbm:
         extra += lands
@@ -1403,14 +1410,15 @@
         VMEM((nf, el, T), F32), VMEM((nf, SR, R), F32), VMEM((nf, SR, R), F32), VMEM((nd, SR, R), F32),
         VMEM((SR, D), F32),
     ]
-    scratch += [VMEM((2, R // 2, (QV if split else W) >> (i + 1)), BF) for i in range(m)]
+    for n in ((QW, 2 * KW) if split else (W,)):
+        scratch += [VMEM((2, R // 2, n >> (i + 1)), BF) for i in range(m)]
     if split:
-        scratch += [VMEM((C * R, D), BF)] + [VMEM((2, C * R // 2, D >> (i + 1)), BF) for i in range(m)]
+        scratch += [VMEM((C * R, OW), BF)] + [VMEM((2, C * R // 2, OW >> (i + 1)), BF) for i in range(m)]
     scratch += [VMEM((T, D), BF), VMEM((R, QV) if land_hbm else (16, 128), BF)]
     scratch += [
         dma((10,)), dma((C,)), dma((nf,)), dma((nf,)),
         dma((5, C)), dma((5, C)), dma((5, 2, C)), dma((5, 2, C)),
-        dma((2 * el, 2 * m)), dma((2 * el, 2 * m)), dma((5, 2 * m)), dma((5, 2 * m)),
+        dma((2 * el, 2 * m)), dma((2 * el, 2 * m)), dma((7, 2 * m)), dma((7, 2 * m)),
         dma((nf,)), dma((nf,)), dma((nd,)), dma((nd,)), dma(()), dma((2,)),
     ]
     inner = [vm(), hbm(), vm(), hbm(), hbm(), hbm(), hbm(), hbm(), hbm(), hbm(), vm(), hbm(), hbm(), hbm(), hbm(), hbm(), vm(),

time: 448 us -> 439 us (0.980)
  Pallas kernels: 422 us -> 413 us
where the time goes in v6:
time: 439 us; the launch traced here: 437 us
  Pallas kernels  413 us (94%)
  other arithmetic  12.8 us (3%)
  local copies, waits for them, and re-layouts  10.5 us (2%)
    pallas_call x1, Pallas kernels, back(): pl.pallas_call(functools.partial(back_kernel, nf, nd, el, land_hbm, split...  180 us
    pallas_call x1, Pallas kernels, experts_call(): pl.pallas_call(functools.partial(experts_kernel, nf, nd, el, cap, capp, l...  145 us
    pallas_call x1, Pallas kernels, front(): pl.pallas_call(functools.partial(front_kernel, nf, nd, experts), out_shap...  88.4 us

profile of v6, /device:TPU:10, one launch (start us, length us, event | category | flops | bytes accessed | tf_op | source)
XLA Modules:
  0.0 437.2 jit_solution(12316000078994554456)
XLA Ops:
  0.7 0.1 pad.5.clone
  0.7 0.7 broadcast_in_dim.17
  1.4 0.7 broadcast_in_dim.18
  2.0 0.7 fusion
  2.8 0.1 convolution_select_fusion.slots
  2.9 1.4 maximum_bitcast_fusion.small
  4.3 0.0 copy-done.4
  4.3 88.4 %front.1 = (bf16[256,1536]{1,0:T(8,128)(2,1)}, f32[256,1536]{1,0:T(8,128)}, f32[16,256]{1,0:T(8,128)}, bf16[256,1536]{1,0:T(8,128)(2,1)}, bf16[256,2048]{1,0:T(8...) custom-call(bf16[256,1536]{1,0:T(8,128)(2,1)} %refs_6_.1, ...), custom_call_target="tpu_custom_call" | custom-call | flops 4000000000 | bytes 60000000 | tf_op jit(solution)/shard_map/front/pallas_call | solution.py:373
  92.7 0.7 reshape.32
  93.4 0.6 pad_maximum_fusion.side
  94.1 144.7 %experts.1 = (bf16[8,256,1536]{2,1,0:T(8,128)(2,1)}, bf16[256,1536]{1,0:T(8,128)(2,1)}, f32[8,2,256]{2,1,0:T(2,128)}, bf16[2,1536,1024]{2,1,0:T(8,128)(2,1)}, bf...) custom-call(bf16[256,1536]{1,0:T(8,128)(2,1)} %get-tuple-element.34.ffn.refs_9_, ...), custom_call_target="tpu_custom_call" | custom-call | flops 40000000000 | bytes 60000000 | tf_op jit(solution)/shard_map/experts/pallas_call | solution.py:943
  238.8 180.0 %back.1 = (bf16[256,1536]{1,0:T(8,128)(2,1)}, bf16[256,1536]{1,0:T(8,128)(2,1)}, bf16[192,4096]{1,0:T(8,128)(2,1)}, f32[24,192]{1,0:T(8,128)}, bf16[2,1536,1024]...) custom-call(bf16[256,1536]{1,0:T(8,128)(2,1)} %get-tuple-element.37., ...), custom_call_target="tpu_custom_call" | custom-call | flops 8000000000 | bytes 90000000 | tf_op jit(solution)/shard_map/back/pallas_call | solution.py:1426
  418.8 1.4 fusion.3
  420.2 1.3 slice_bitcast_fusion
  421.5 2.1 fusion.2
  423.7 0.0 copy-done
  423.7 1.7 fusion.1
  425.4 3.6 convert_element_type.22
  429.0 0.0 slice-done.1
  429.0 0.0 copy-start.2
  429.0 6.5 %slice_convert_fusion = (f32[2,1536,512]{2,1,0:T(8,128)}, f32[2,1536,512]{2,1,0:T(8,128)}) fusion(bf16[2,1536,1024]{2,1,0:T(8,128)(2,1)S(1)} %bitcast.10), kind=kLoop, calls=%fused_computation | loop fusion | flops 3145728 | bytes 18874368 | tf_op jit(solution)/shard_map/convert_element_type | solution.py:1476
  435.5 0.0 copy-done.3
  435.5 0.9 copy.30
  436.4 0.9 copy.31
  (12 shorter events, 0.0 us)
Async XLA Ops:
  2.9 1.4 copy-start.4
  418.8 4.9 %copy-start = (bf16[192,4096]{1,0:T(8,128)(2,1)S(1)}, bf16[192,4096]{1,0:T(8,128)(2,1)}, u32[]{:S(2)}) copy-start(bf16[192,4096]{1,0:T(8,128)(2,1)} %get-tuple-element.52) | copy-start | bytes 4718596
  421.5 3.8 copy-start.1
  423.7 5.3 %slice-start = ((s8[6291456]{0:T(1024)(128)(4,1)}), s8[4194304]{0:T(1024)(128)(4,1)S(1)}, s32[]{:S(2)}) async-start(s8[6291456]{0:T(1024)(128)(4,1)} %bitcast.9), calls=%async_computation | async-start | bytes 8388608
  425.4 3.6 slice-start.1
  429.0 6.5 %copy-start.3 = (bf16[256,1536]{1,0:T(8,128)(2,1)S(1)}, bf16[256,1536]{1,0:T(8,128)(2,1)}, u32[]{:S(2)}) copy-start(bf16[256,1536]{1,0:T(8,128)(2,1)} %get-tuple-element.76) | copy-start | bytes 2359300
  429.0 7.4 %copy-start.2 = (bf16[256,1536]{1,0:T(8,128)(2,1)S(1)}, bf16[256,1536]{1,0:T(8,128)(2,1)}, u32[]{:S(2)}) copy-start(bf16[256,1536]{1,0:T(8,128)(2,1)} %get-tuple-element.77) | copy-start | bytes 2359300

commit v7 on v6

--- a/solution.py
+++ b/solution.py
@@ -83,7 +83,7 @@
 
 
 def front_kernel(nf, nd, experts, tok, wq, wk, wv, wo, small, cot, slots, cosr, sinr,
-                 ffn_o, hid_o, gates_o, mix_o, qk_o, v_o, prob_o, wf_o, cot_o, rt_o,
+                 ffn_o, hid_o, gates_o, side_o, mix_o, qk_o, v_o, prob_o, wf_o, cot_o, rt_o,
                  wf, sm, attn, rot,
                  s_sm, r_sm, s_z, r_z, s_dp, r_dp, s_sib, r_sib, s_cz, r_cz, s_cs, r_cs, s_loc, s_w):
     T, D = tok.shape
@@ -334,7 +334,12 @@
     named = slots[...] >= 0.0
     logits = jnp.where(named, logits, MASKED)
     ex = jnp.where(named, jnp.exp(logits - jnp.max(logits, 0, keepdims=True)), 0.0)
-    gates_o[...] = ex / jnp.sum(ex, 0, keepdims=True)
+    gates = ex / jnp.sum(ex, 0, keepdims=True)
+    gates_o[...] = gates
+    el = experts // nf
+    for i in range(nf):
+        side_o[i, 0:el] = slots[i * el:(i + 1) * el, :]
+        side_o[i, el:2 * el] = gates[i * el:(i + 1) * el]
 
     for s in range(3, C):
         cot_step(s)
@@ -365,7 +370,7 @@
     C = nf // 2
     W = sum(w.shape[1] for w in ws)
     out = [
-        (T, D, BF, 0), (T, D, F32, 0), (experts, T, F32, 0), (T, QW, BF, 0), (T, QW + KW, BF, 0),
+        (T, D, BF, 0), (T, D, F32, 0), (experts, T, F32, 0), (nf, 2 * experts // nf, T, F32, 0), (T, QW, BF, 0), (T, QW + KW, BF, 0),
         (T, KW, BF, 0), (QUERY_HEADS, T, T, BF, 0), (D, W, BF, 1), (nf, T, D, BF, 1),
         (small.shape[0], D, BF, 0),
     ]
@@ -716,6 +721,45 @@
     for cp in w_copies:
         cp.wait()
 
+    n1 = D // 256
+    n2 = FFW // 256
+    cubes = term_cubes(nd, el, f, d, t1_o, t2_o, None, None, [l1], None, [], [], (s_cube, r_cube))
+
+    def t1_copy(e, i):
+        return pltpu.make_async_copy(st1.at[lax.rem(i, 2)], t1_o.at[e, pl.ds(pl.multiple_of(i * 256, 256), 256)],
+                                     s_t.at[0, lax.rem(i, 2)])
+
+    def t2_copy(e, i):
+        return pltpu.make_async_copy(st2.at[lax.rem(i, 2)], t2_o.at[e, pl.ds(pl.multiple_of(i * 256, 256), 256)],
+                                     s_t.at[1, lax.rem(i, 2)])
+
+    def t1_terms(e):
+        @pl.loop(0, n1)
+        def _(i):
+            @pl.when(i >= 2)
+            def _():
+                t1_copy(e, i).wait()
+            col = pl.ds(pl.multiple_of(i * 256, 256), 256)
+            st1[lax.rem(i, 2)] = dot_tn(xs[e, :, col], hs[e]).astype(BF)
+            t1_copy(e, i).start()
+
+        for i in range(2):
+            t1_copy(e, i).wait()
+        cubes[2 * e].down(0).start()
+
+    def t2_terms(e):
+        @pl.loop(0, n2)
+        def _(i):
+            @pl.when(i >= 2)
+            def _():
+                t2_copy(e, i).wait()
+            col = pl.ds(pl.multiple_of(i * 256, 256), 256)
+            st2[lax.rem(i, 2)] = dot_tn(hgs[e, :, col], gs[e]).astype(BF)
+            t2_copy(e, i).start()
+
+        for i in range(2):
+            t2_copy(e, i).wait()
+
     row_ids = lax.broadcasted_iota(jnp.int32, (capp, T), 0).astype(F32)
 
     @pl.loop(0, C)
@@ -812,6 +856,8 @@
         @pl.when(j == C - 1)
         def _():
             reduce_step(1)
+            for e in range(el):
+                t1_terms(e)
         for e in range(el):
             for n in range(0, D, 512):
                 orow = dot(hgs[e, here, :], wd[e, :, n:n + 512]).astype(BF)
@@ -833,45 +879,10 @@
                 st_o[kk, :, n:n + 512] = dot_tn(picks[kk], orb[kk, :, n:n + 512]).astype(BF)
         back(b).start()
 
-    n1 = D // 256
-    n2 = FFW // 256
-
-    def t1_copy(e, i):
-        return pltpu.make_async_copy(st1.at[lax.rem(i, 2)], t1_o.at[e, pl.ds(pl.multiple_of(i * 256, 256), 256)],
-                                     s_t.at[0, lax.rem(i, 2)])
-
-    def t2_copy(e, i):
-        return pltpu.make_async_copy(st2.at[lax.rem(i, 2)], t2_o.at[e, pl.ds(pl.multiple_of(i * 256, 256), 256)],
-                                     s_t.at[1, lax.rem(i, 2)])
-
-    cubes = term_cubes(nd, el, f, d, t1_o, t2_o, None, None, [l1], None, [], [], (s_cube, r_cube))
+    if C > 2:
+        reduce_step(2)
     for e in range(el):
-        @pl.loop(0, n1)
-        def _(i):
-            @pl.when(i >= 2)
-            def _():
-                t1_copy(e, i).wait()
-            col = pl.ds(pl.multiple_of(i * 256, 256), 256)
-            st1[lax.rem(i, 2)] = dot_tn(xs[e, :, col], hs[e]).astype(BF)
-            t1_copy(e, i).start()
-
-        for i in range(2):
-            t1_copy(e, i).wait()
-        cubes[2 * e].down(0).start()
-        if e == el - 1 and C > 2:
-            reduce_step(2)
-
-        @pl.loop(0, n2)
-        def _(i):
-            @pl.when(i >= 2)
-            def _():
-                t2_copy(e, i).wait()
-            col = pl.ds(pl.multiple_of(i * 256, 256), 256)
-            st2[lax.rem(i, 2)] = dot_tn(hgs[e, :, col], gs[e]).astype(BF)
-            t2_copy(e, i).start()
-        for i in range(2):
-            t2_copy(e, i).wait()
-
+        t2_terms(e)
     for s in range(3, C):
         reduce_step(s)
     for line in lines:
@@ -1453,9 +1464,8 @@
     before = lax.dot_general(onehot, earlier, (((0,), (0,)), ((), ())), preferred_element_type=F32)
     slots = jnp.where(onehot.T > 0, before, -1.0)
     cosr, sinr = rope_rows(T)
-    ffn_in, hidden, gates, mixed, qk, v, probs, full, cot_all, rt = front(
+    ffn_in, hidden, gates, side, mixed, qk, v, probs, full, cot_all, rt = front(
         nf, nd, experts, tokens, (w_query, key_weight, value_weight, w_out), small, cotangent, slots, cosr, sinr)
-    side = jnp.concatenate([slots.reshape(nf, el, T), gates.reshape(nf, el, T)], 1)
     out_part, gin, gp_part, t1, t2, f1 = experts_call(nf, nd, cap, ffn_in, cot_all, side, w_gate, w_up, w_down)
     output, grad_tokens, shard, smalls, t1, t2 = back(nf, nd, el, (
         gin, out_part, gp_part, t1, t2, f1, tokens, cotangent, hidden, ffn_in, gates, mixed, qk, v, probs, full, rt,

time: 439 us -> 436 us (level)
  no operation moved by 1% of the time
where the time goes in v7:
time: 436 us; the launch traced here: 434 us
  Pallas kernels  411 us (94%)
  other arithmetic  12.2 us (3%)
  local copies, waits for them, and re-layouts  9.73 us (2%)
    pallas_call x1, Pallas kernels, back(): pl.pallas_call(functools.partial(back_kernel, nf, nd, el, land_hbm, split...  180 us
    pallas_call x1, Pallas kernels, experts_call(): pl.pallas_call(functools.partial(experts_kernel, nf, nd, el, cap, capp, l...  143 us
    pallas_call x1, Pallas kernels, front(): pl.pallas_call(functools.partial(front_kernel, nf, nd, experts), out_shap...  88.3 us

profile of v7, /device:TPU:10, one launch (start us, length us, event | category | flops | bytes accessed | tf_op | source)
XLA Modules:
  0.0 434.4 jit_solution(13468718586420532222)
XLA Ops:
  0.7 0.1 pad.3.clone
  0.7 0.7 broadcast_in_dim.17
  1.4 0.7 broadcast_in_dim.18
  2.0 0.7 fusion
  2.8 0.8 convolution_select_fusion.slots
  3.5 1.4 maximum_bitcast_fusion.small
  4.9 88.3 %front.1 = (bf16[256,1536]{1,0:T(8,128)(2,1)}, f32[256,1536]{1,0:T(8,128)}, f32[16,256]{1,0:T(8,128)}, f32[8,4,256]{2,1,0:T(4,128)}, bf16[256,1536]{1,0:T(8,128)...) custom-call(bf16[256,1536]{1,0:T(8,128)(2,1)} %refs_6_.1, ...), custom_call_target="tpu_custom_call" | custom-call | flops 4000000000 | bytes 60000000 | tf_op jit(solution)/shard_map/front/pallas_call | solution.py:378
  93.2 142.9 %experts.1 = (bf16[8,256,1536]{2,1,0:T(8,128)(2,1)}, bf16[256,1536]{1,0:T(8,128)(2,1)}, f32[8,2,256]{2,1,0:T(2,128)}, bf16[2,1536,1024]{2,1,0:T(8,128)(2,1)}, bf...) custom-call(bf16[256,1536]{1,0:T(8,128)(2,1)} %get-tuple-element.35.ffn.refs_9_, ...), custom_call_target="tpu_custom_call" | custom-call | flops 40000000000 | bytes 60000000 | tf_op jit(solution)/shard_map/experts/pallas_call | solution.py:954
  236.1 179.9 %back.1 = (bf16[256,1536]{1,0:T(8,128)(2,1)}, bf16[256,1536]{1,0:T(8,128)(2,1)}, bf16[192,4096]{1,0:T(8,128)(2,1)}, f32[24,192]{1,0:T(8,128)}, bf16[2,1536,1024]...) custom-call(bf16[256,1536]{1,0:T(8,128)(2,1)} %get-tuple-element.38., ...), custom_call_target="tpu_custom_call" | custom-call | flops 8000000000 | bytes 90000000 | tf_op jit(solution)/shard_map/back/pallas_call | solution.py:1437
  416.0 0.0 copy-start
  416.0 1.4 fusion.3
  417.4 1.3 slice_bitcast_fusion
  418.7 2.1 fusion.2
  420.9 0.0 copy-done
  420.9 1.7 fusion.1
  422.6 0.0 copy-done.1
  422.6 3.6 convert_element_type.22
  426.2 0.0 slice-done
  426.2 0.0 slice-done.1
  426.2 0.0 copy-start.2
  426.2 6.5 %slice_convert_fusion = (f32[2,1536,512]{2,1,0:T(8,128)}, f32[2,1536,512]{2,1,0:T(8,128)}) fusion(bf16[2,1536,1024]{2,1,0:T(8,128)(2,1)S(1)} %bitcast.10), kind=kLoop, calls=%fused_computation | loop fusion | flops 3145728 | bytes 18874368 | tf_op jit(solution)/shard_map/convert_element_type | solution.py:1486
  432.7 0.0 copy-done.3
  432.7 0.9 copy.30
  433.6 0.9 copy.31
  (7 shorter events, 0.0 us)
Async XLA Ops:
  416.0 4.9 %copy-start = (bf16[192,4096]{1,0:T(8,128)(2,1)S(1)}, bf16[192,4096]{1,0:T(8,128)(2,1)}, u32[]{:S(2)}) copy-start(bf16[192,4096]{1,0:T(8,128)(2,1)} %get-tuple-element.54) | copy-start | bytes 4718596
  418.7 3.8 copy-start.1
  420.9 5.3 %slice-start = ((s8[6291456]{0:T(1024)(128)(4,1)}), s8[4194304]{0:T(1024)(128)(4,1)S(1)}, s32[]{:S(2)}) async-start(s8[6291456]{0:T(1024)(128)(4,1)} %bitcast.9), calls=%async_computation | async-start | bytes 8388608
  422.6 3.6 slice-start.1
  426.2 6.5 %copy-start.3 = (bf16[256,1536]{1,0:T(8,128)(2,1)S(1)}, bf16[256,1536]{1,0:T(8,128)(2,1)}, u32[]{:S(2)}) copy-start(bf16[256,1536]{1,0:T(8,128)(2,1)} %get-tuple-element.78) | copy-start | bytes 2359300
  426.2 7.4 %copy-start.2 = (bf16[256,1536]{1,0:T(8,128)(2,1)S(1)}, bf16[256,1536]{1,0:T(8,128)(2,1)}, u32[]{:S(2)}) copy-start(bf16[256,1536]{1,0:T(8,128)(2,1)} %get-tuple-element.79) | copy-start | bytes 2359300

commit v8 on v7

--- a/solution.py
+++ b/solution.py
@@ -1109,6 +1109,7 @@
     for cube in first_terms:
         cube.fold(0, pipe_add)
         onward(cube, 0)
+    middle = steps1.pop(0) if steps1 else None
     for cp in out_loads:
         cp.wait()
     out_line.step(1)
@@ -1219,6 +1220,11 @@
         gproj[:, pl.ds(pl.multiple_of(QW + KW + i * 128, 128), 128)] = join(gv).astype(BF)
 
         if C > 2:
+            @pl.when(i == 2)
+            def _():
+                if middle is not None:
+                    middle()
+
             @pl.when(i == 1)
             def _():
                 for line in o_lines:
@@ -1250,7 +1256,6 @@
                 for other in o_lines:
                     other.step(s)
         line.step(1)
-    run(steps1)
     run(steps2)
     if split:
         o_merge(0)

time: 436 us -> 432 us (level)
  no operation moved by 1% of the time
where the time goes in v8:
time: 432 us; the launch traced here: 430 us
  Pallas kernels  407 us (94%)
  other arithmetic  12.2 us (3%)
  local copies, waits for them, and re-layouts  9.73 us (2%)
    pallas_call x1, Pallas kernels, back(): pl.pallas_call(functools.partial(back_kernel, nf, nd, el, land_hbm, split...  176 us
    pallas_call x1, Pallas kernels, experts_call(): pl.pallas_call(functools.partial(experts_kernel, nf, nd, el, cap, capp, l...  143 us
    pallas_call x1, Pallas kernels, front(): pl.pallas_call(functools.partial(front_kernel, nf, nd, experts), out_shap...  88.3 us

profile of v8, /device:TPU:10, one launch (start us, length us, event | category | flops | bytes accessed | tf_op | source)
XLA Modules:
  0.0 430.4 jit_solution(17756015212514042752)
XLA Ops:
  0.7 0.1 pad.3.clone
  0.7 0.7 broadcast_in_dim.17
  1.4 0.7 broadcast_in_dim.18
  2.0 0.7 fusion
  2.8 0.8 convolution_select_fusion.slots
  3.5 1.4 maximum_bitcast_fusion.small
  4.9 88.3 %front.1 = (bf16[256,1536]{1,0:T(8,128)(2,1)}, f32[256,1536]{1,0:T(8,128)}, f32[16,256]{1,0:T(8,128)}, f32[8,4,256]{2,1,0:T(4,128)}, bf16[256,1536]{1,0:T(8,128)...) custom-call(bf16[256,1536]{1,0:T(8,128)(2,1)} %refs_6_.1, ...), custom_call_target="tpu_custom_call" | custom-call | flops 4000000000 | bytes 60000000 | tf_op jit(solution)/shard_map/front/pallas_call | solution.py:378
  93.2 142.9 %experts.1 = (bf16[8,256,1536]{2,1,0:T(8,128)(2,1)}, bf16[256,1536]{1,0:T(8,128)(2,1)}, f32[8,2,256]{2,1,0:T(2,128)}, bf16[2,1536,1024]{2,1,0:T(8,128)(2,1)}, bf...) custom-call(bf16[256,1536]{1,0:T(8,128)(2,1)} %get-tuple-element.35.ffn.refs_9_, ...), custom_call_target="tpu_custom_call" | custom-call | flops 40000000000 | bytes 60000000 | tf_op jit(solution)/shard_map/experts/pallas_call | solution.py:954
  236.1 175.8 %back.1 = (bf16[256,1536]{1,0:T(8,128)(2,1)}, bf16[256,1536]{1,0:T(8,128)(2,1)}, bf16[192,4096]{1,0:T(8,128)(2,1)}, f32[24,192]{1,0:T(8,128)}, bf16[2,1536,1024]...) custom-call(bf16[256,1536]{1,0:T(8,128)(2,1)} %get-tuple-element.38., ...), custom_call_target="tpu_custom_call" | custom-call | flops 8000000000 | bytes 90000000 | tf_op jit(solution)/shard_map/back/pallas_call | solution.py:1442
  411.9 0.0 copy-start
  411.9 1.4 fusion.3
  413.3 1.3 slice_bitcast_fusion
  414.7 2.1 fusion.2
  416.8 0.0 copy-done
  416.8 1.7 fusion.1
  418.5 0.0 copy-done.1
  418.5 3.6 convert_element_type.22
  422.1 0.0 slice-done
  422.1 0.0 slice-done.1
  422.1 0.0 copy-start.2
  422.1 6.5 %slice_convert_fusion = (f32[2,1536,512]{2,1,0:T(8,128)}, f32[2,1536,512]{2,1,0:T(8,128)}) fusion(bf16[2,1536,1024]{2,1,0:T(8,128)(2,1)S(1)} %bitcast.10), kind=kLoop, calls=%fused_computation | loop fusion | flops 3145728 | bytes 18874368 | tf_op jit(solution)/shard_map/convert_element_type | solution.py:1491
  428.6 0.9 copy.30
  429.5 0.0 copy-done.2
  429.5 0.9 copy.31
  (7 shorter events, 0.0 us)
Async XLA Ops:
  411.9 4.9 %copy-start = (bf16[192,4096]{1,0:T(8,128)(2,1)S(1)}, bf16[192,4096]{1,0:T(8,128)(2,1)}, u32[]{:S(2)}) copy-start(bf16[192,4096]{1,0:T(8,128)(2,1)} %get-tuple-element.54) | copy-start | bytes 4718596
  414.7 3.8 copy-start.1
  416.8 5.3 %slice-start = ((s8[6291456]{0:T(1024)(128)(4,1)}), s8[4194304]{0:T(1024)(128)(4,1)S(1)}, s32[]{:S(2)}) async-start(s8[6291456]{0:T(1024)(128)(4,1)} %bitcast.9), calls=%async_computation | async-start | bytes 8388608
  418.5 3.6 slice-start.1
  422.1 6.5 %copy-start.3 = (bf16[256,1536]{1,0:T(8,128)(2,1)S(1)}, bf16[256,1536]{1,0:T(8,128)(2,1)}, u32[]{:S(2)}) copy-start(bf16[256,1536]{1,0:T(8,128)(2,1)} %get-tuple-element.78) | copy-start | bytes 2359300
  422.1 7.4 %copy-start.2 = (bf16[256,1536]{1,0:T(8,128)(2,1)S(1)}, bf16[256,1536]{1,0:T(8,128)(2,1)}, u32[]{:S(2)}) copy-start(bf16[256,1536]{1,0:T(8,128)(2,1)} %get-tuple-element.79) | copy-start | bytes 2359300
